TPU v7x, 32 devices: a whole 2x2x4 slice. The times are simulated.
32 devices in a mesh: row: 8 (over y, x, core), col: 4 (over z).
Axes of the slice: x: 2, y: 2, z: 4, core: 2. Of those that a mesh axis runs over, the one named last changes fastest.
Arguments:
- flow: float32 [2, 8, 64, 1024], P(None, None, 'row', 'col'), may hold values from -4 to 4
- temp: float32 [8, 64, 1024], P(None, 'row', 'col'), may hold values from -4 to 4
- tracers: float32 [8, 16, 8, 16, 512], P('row', None, None, None, 'col'), may hold values from -4 to 4
- bottom: int32 [64, 1024], P('row', 'col'), may hold values from 0 to 8
- sunlight: float32 [64, 1024], P('row', 'col'), may hold values from 0.5 to 2
- rates: float32 [16, 16], replicated, may hold values from -2 to 2
Outputs:
- flow_out: float32 [2, 8, 64, 1024], P(None, None, 'row', 'col')
- temp_out: float32 [8, 64, 1024], P(None, 'row', 'col')
- tracers_out: float32 [8, 16, 8, 16, 512], P('row', None, None, None, 'col')
Inputs may be any that keep to these rules, and one draw needn't show every extreme that they name: Columns are water at levels 0 to bottom - 1; 0 marks land.
All inputs are finite; a program needn't handle non-finite values.
Results may differ from a plain program's by a relative error of at most 0.0001.
Values sent between devices are 32-bit elements; how exact they have to be, the bound alone decides.
No kernel may reach another device: no remote copies, remote signals or barrier semaphores. Data moves between devices by JAX's collectives and lax.ppermute only.
A program may use at most 64 MiB of HBM per device.

v0:
```python
import jax
import jax.numpy as jnp
from jax import lax
from jax.sharding import PartitionSpec as P

NZ = 8
KL = 4
STEPS = 2


time_step = 0.2
viscosity = 0.2
expansion = 0.05
coriolis_base = 0.5
kappa_base = 0.05
kappa_shear = 0.2
react_step = 0.25
water_absorb = 0.1
pigment_absorb = 0.6
heat_gain = 1.0


def extended(block, sides, width):
    for axis, dim in sides:
        count = lax.axis_size(axis)
        forward = [(i, i + 1) for i in range(count - 1)]
        backward = [(target, source) for source, target in forward]
        low = lax.ppermute(
            lax.slice_in_dim(block, block.shape[dim] - width, None, axis=dim), axis, forward
        )
        high = lax.ppermute(lax.slice_in_dim(block, 0, width, axis=dim), axis, backward)
        block = jnp.concatenate([low, block, high], axis=dim)
    return block


def from_partner(array, axis, bit):
    return lax.ppermute(array, axis, [(i, i ^ 1 << bit) for i in range(lax.axis_size(axis))])


def passed_along(array, axis, by):
    size = lax.axis_size(axis)
    pairs = [(i, i + by) for i in range(size) if 0 <= i + by < size]
    return lax.ppermute(array, axis, pairs)


def neighbour_sides(padded):
    middle = padded[..., 1:-1, 1:-1]
    return (
        middle,
        padded[..., 1:-1, 2:],
        padded[..., 1:-1, :-2],
        padded[..., 2:, 1:-1],
        padded[..., :-2, 1:-1],
    )


def shear_kappa(flow_u, flow_v):
    below_u = jnp.concatenate([flow_u[1:], flow_u[-1:]], axis=0)
    below_v = jnp.concatenate([flow_v[1:], flow_v[-1:]], axis=0)
    shear_sq = (flow_u - below_u) ** 2 + (flow_v - below_v) ** 2
    return kappa_base + kappa_shear * shear_sq / (1.0 + shear_sq)


def make_faces(padded):
    kappa_pad = shear_kappa(padded[0], padded[1])
    u_mid, u_east, u_west, u_north, u_south = neighbour_sides(padded[0])
    v_mid, v_east, v_west, v_north, v_south = neighbour_sides(padded[1])
    m_mid, m_east, m_west, m_north, m_south = neighbour_sides(padded[3])
    k_mid, k_east, k_west, k_north, k_south = neighbour_sides(kappa_pad)
    open_e = m_mid * m_east
    open_w = m_mid * m_west
    open_n = m_mid * m_north
    open_s = m_mid * m_south
    return jnp.stack(
        [
            0.5 * (u_mid + u_east) * open_e,
            0.5 * (u_mid + u_west) * open_w,
            0.5 * (v_mid + v_north) * open_n,
            0.5 * (v_mid + v_south) * open_s,
            0.5 * (k_mid + k_east) * open_e,
            0.5 * (k_mid + k_west) * open_w,
            0.5 * (k_mid + k_north) * open_n,
            0.5 * (k_mid + k_south) * open_s,
            m_mid,
        ]
    )


def transport(face_terms, padded):
    east_flux, west_flux, north_flux, south_flux = (
        face_terms[0],
        face_terms[1],
        face_terms[2],
        face_terms[3],
    )
    east_cond, west_cond, north_cond, south_cond = (
        face_terms[4],
        face_terms[5],
        face_terms[6],
        face_terms[7],
    )
    wet_mask = face_terms[8]
    middle, eastward, westward, northward, southward = neighbour_sides(padded)
    divergence = east_flux - west_flux + north_flux - south_flux
    upward = -lax.cumsum(divergence, axis=0, reverse=True)
    zero_top = jnp.zeros_like(upward[:1])
    w_bottom = jnp.concatenate([upward[1:], zero_top], axis=0)
    w_top = jnp.concatenate([zero_top, upward[1:]], axis=0)
    above_val = jnp.concatenate([middle[..., :1, :, :], middle[..., :-1, :, :]], axis=-3)
    below_val = jnp.concatenate([middle[..., 1:, :, :], middle[..., -1:, :, :]], axis=-3)
    advection = (
        east_flux * 0.5 * (middle + eastward)
        - west_flux * 0.5 * (middle + westward)
        + north_flux * 0.5 * (middle + northward)
        - south_flux * 0.5 * (middle + southward)
        + w_top * 0.5 * (middle + above_val)
        - w_bottom * 0.5 * (middle + below_val)
    )
    diffusion = (
        east_cond * (eastward - middle)
        + west_cond * (westward - middle)
        + north_cond * (northward - middle)
        + south_cond * (southward - middle)
    )
    return wet_mask * (middle + time_step * (diffusion - advection))


def momentum(padded, coriolis):
    pressure = -expansion * jnp.cumsum(padded[2], axis=0)
    p_mid, p_east, p_west, p_north, p_south = neighbour_sides(pressure)
    u_mid, u_east, u_west, u_north, u_south = neighbour_sides(padded[0])
    v_mid, v_east, v_west, v_north, v_south = neighbour_sides(padded[1])
    m_mid, m_east, m_west, m_north, m_south = neighbour_sides(padded[3])
    lap_u = m_mid * (
        m_east * (u_east - u_mid)
        + m_west * (u_west - u_mid)
        + m_north * (u_north - u_mid)
        + m_south * (u_south - u_mid)
    )
    lap_v = m_mid * (
        m_east * (v_east - v_mid)
        + m_west * (v_west - v_mid)
        + m_north * (v_north - v_mid)
        + m_south * (v_south - v_mid)
    )
    new_u = m_mid * (
        u_mid + time_step * (coriolis * v_mid - 0.5 * (p_east - p_west) + viscosity * lap_u)
    )
    new_v = m_mid * (
        v_mid + time_step * (-coriolis * u_mid - 0.5 * (p_north - p_south) + viscosity * lap_v)
    )
    return (new_u, new_v)


def absorption(pigment_top):
    squared = pigment_top * pigment_top
    transmit = jnp.exp(-(water_absorb + pigment_absorb * squared / (1.0 + squared)))
    above_light = jnp.cumprod(
        jnp.concatenate([jnp.ones_like(transmit[:1]), transmit[:-1]], axis=0), axis=0
    )
    return above_light * (1.0 - transmit)


def reaction(moved_field, rates, wet_mask):
    saturated = moved_field / jnp.sqrt(1.0 + moved_field * moved_field)
    coupling = jnp.einsum("nm,mkji->nkji", rates, saturated, precision=lax.Precision.HIGHEST)
    return moved_field + react_step * wet_mask * coupling


def split_lon(field, lower):
    half = field.shape[-1] // 2
    first, second = (field[..., :half], field[..., half:])
    return (jnp.where(lower, first, second), jnp.where(lower, second, first))


def split_lat(field, lower):
    half = field.shape[-2] // 2
    first, second = (field[..., :half, :], field[..., half:, :])
    return (jnp.where(lower, first, second), jnp.where(lower, second, first))


def join_lat(own_part, other_part, lower):
    return jnp.where(
        lower,
        jnp.concatenate([own_part, other_part], axis=-2),
        jnp.concatenate([other_part, own_part], axis=-2),
    )


def join_lon(own_part, other_part, lower):
    return jnp.where(
        lower,
        jnp.concatenate([own_part, other_part], axis=-1),
        jnp.concatenate([other_part, own_part], axis=-1),
    )


def ocean_step(flow_u, flow_v, heat_field, wet_mask, coriolis):
    padded = extended(
        jnp.stack([flow_u, flow_v, heat_field, wet_mask]), (("row", 2), ("col", 3)), 1
    )
    face_terms = make_faces(padded)
    new_u, new_v = momentum(padded, coriolis)
    return (face_terms, new_u, new_v, transport(face_terms, padded[2]))


def on_device(flow, temp, tracers, bottom, sunlight, rates):
    lat_dev = bottom.shape[0]
    lon_dev = bottom.shape[1]
    levels = lax.broadcasted_iota(jnp.int32, (NZ, lat_dev, lon_dev), 0)
    wet_mask = (levels < bottom[None]).astype(jnp.float32)
    row_index = lax.axis_index("row")
    lower = row_index % 2 == 0
    first_row = row_index * lat_dev
    latitude = (first_row + lax.broadcasted_iota(jnp.int32, (lat_dev, 1), 0)).astype(jnp.float32)
    total_lat = lat_dev * lax.axis_size("row")
    coriolis = coriolis_base * (2.0 * (latitude + 0.5) / total_lat - 1.0)
    flow_u = flow[0] * wet_mask
    flow_v = flow[1] * wet_mask
    heat_field = temp * wet_mask
    tracer_field = tracers[0]
    for step_index in range(STEPS):
        face_terms, flow_u, flow_v, heat_field = ocean_step(
            flow_u, flow_v, heat_field, wet_mask, coriolis
        )
        keep_faces, send_faces = split_lon(face_terms, lower)
        got_faces, got_east, got_west = from_partner(
            (send_faces, tracer_field[..., -1], tracer_field[..., 0]), "row", 0
        )
        block_faces = join_lat(keep_faces, got_faces, lower)
        if step_index == 0:
            tracer_field = tracer_field * block_faces[8]
        moved_cols = []
        for offset, column in ((1, got_east), (-1, got_west)):
            moved_cols.append(passed_along(column, "col", offset))
        west_rim = jnp.where(lower, moved_cols[0], got_east)
        east_rim = jnp.where(lower, got_west, moved_cols[1])
        moved_rows = []
        for offset, slab in ((2, tracer_field[..., -1:, :]), (-2, tracer_field[..., :1, :])):
            moved_rows.append(passed_along(slab, "row", offset))
        inner = jnp.concatenate([west_rim[..., None], tracer_field, east_rim[..., None]], axis=-1)
        widths = ((0, 0), (0, 0), (0, 0), (1, 1))
        padded = jnp.concatenate(
            [jnp.pad(moved_rows[0], widths), inner, jnp.pad(moved_rows[1], widths)], axis=-2
        )
        tracer_field = reaction(transport(block_faces, padded), rates, block_faces[8])
        profile = absorption(tracer_field[0, :KL])
        keep_light, send_light = split_lat(profile, lower)
        got_light = from_partner(send_light, "row", 0)
        returned = join_lon(keep_light, got_light, lower)
        heat_field = heat_field.at[:KL].add(heat_gain * sunlight * wet_mask[:KL] * returned)
    return (jnp.stack([flow_u, flow_v]), heat_field, tracer_field[None])


def solution(mesh):
    in_specs = (
        P(None, None, "row", "col"),
        P(None, "row", "col"),
        P("row", None, None, None, "col"),
        P("row", "col"),
        P("row", "col"),
        P(),
    )
    out_specs = (
        P(None, None, "row", "col"),
        P(None, "row", "col"),
        P("row", None, None, None, "col"),
    )
    return jax.shard_map(
        on_device, mesh=mesh, in_specs=in_specs, out_specs=out_specs, check_vma=False
    )
```

profile of v0, /device:TPU:3, one launch (start us, length us, event | category | flops | bytes accessed | tf_op | source)
XLA Modules:
  0.0 105.9 jit_solution(10219344398863705676)
XLA Ops:
  0.7 2.5 %slice_reduce_fusion.3 = (f32[16,8,16]{2,1,0:T(8,128)S(1)}, f32[16,8,16]{2,1,0:T(8,128)S(1)}) fusion(f32[16,8,16,128]{3,2,1,0:T(8,128)} %bitcast.171), kind=kLoop, calls=%fused_computation.71 | loop fusion | bytes 32768 | tf_op jit(solution)/shard_map/slice | solution.py:228
  3.2 0.7 collective-permute-start.5
  4.2 3.7 %collective-permute-start = (f32[4,8,1,256]{3,2,1,0:T(1,128)S(1)}, f32[4,8,1,256]{3,2,1,0:T(1,128)S(1)}, u32[]{:S(2)}, u32[]{:S(2)}) collective-permute-start(f32[4,8,1,256]{3,2,1,0:T(1,128)S(1)} %get-tuple-element.152), channel_id=1, source_target_pairs={{0,4},{4,8},{8,12},{12,16},{16,20},{20,24},{24,28},{1,5},{5,9},{9,... | collective-permute-start | bytes 98312 | tf_op jit(solution)/shard_map/ppermute | solution.py:28
  7.8 1.9 %collective-permute-start.1 = (f32[4,8,1,256]{3,2,1,0:T(1,128)S(1)}, f32[4,8,1,256]{3,2,1,0:T(1,128)S(1)}, u32[]{:S(2)}, u32[]{:S(2)}) collective-permute-start(f32[4,8,1,256]{3,2,1,0:T(1,128)S(1)} %get-tuple-element.153), channel_id=1, source_target_pairs={{4,0},{8,4},{12,8},{16,12},{20,16},{24,20},{28,24},{5,1},{9,5},{13... | collective-permute-start | bytes 98312 | tf_op jit(solution)/shard_map/ppermute | solution.py:31
  9.8 0.6 iota_compare_fusion
  10.4 1.3 %collective-permute-start.6 = (f32[16,8,16]{2,1,0:T(8,128)S(1)}, f32[16,8,16]{2,1,0:T(8,128)S(1)}, u32[]{:S(2)}, u32[]{:S(2)}) collective-permute-start(f32[16,8,16]{2,1,0:T(8,128)S(1)} %collective-permute-done.5), channel_id=1, source_target_pairs={{1,0},{2,1},{3,2},{5,4},{6,5},{7,6},{9,8},{10,9},{11,10},{13,12},{... | collective-permute-start | bytes 24584 | tf_op jit(solution)/shard_map/ppermute | solution.py:43
  11.7 4.0 %collective-permute-start.8 = (f32[16,8,16]{2,1,0:T(8,128)S(1)}, f32[16,8,16]{2,1,0:T(8,128)S(1)}, u32[]{:S(2)}, u32[]{:S(2)}) collective-permute-start(f32[16,8,16]{2,1,0:T(8,128)S(1)} %collective-permute-done.7), channel_id=1, source_target_pairs={{0,1},{1,2},{2,3},{4,5},{5,6},{6,7},{8,9},{9,10},{10,11},{12,13},{... | collective-permute-start | bytes 24584 | tf_op jit(solution)/shard_map/ppermute | solution.py:43
  15.9 0.8 fusion.208
  16.7 3.2 %collective-permute-start.2 = (f32[4,8,10,1]{3,2,1,0:T(8,128)}, f32[4,8,10,1]{3,2,1,0:T(8,128)S(1)}, u32[]{:S(2)}, u32[]{:S(2)}) collective-permute-start(f32[4,8,10,1]{3,2,1,0:T(8,128)} %get-tuple-element.148), channel_id=1, source_target_pairs={{0,1},{1,2},{2,3},{4,5},{5,6},{6,7},{8,9},{9,10},{10,11},{12,13},{... | collective-permute-start | bytes 3848 | tf_op jit(solution)/shard_map/ppermute | solution.py:28
  19.9 1.3 %collective-permute-start.3 = (f32[4,8,10,1]{3,2,1,0:T(8,128)S(1)}, f32[4,8,10,1]{3,2,1,0:T(8,128)S(1)}, u32[]{:S(2)}, u32[]{:S(2)}) collective-permute-start(f32[4,8,10,1]{3,2,1,0:T(8,128)S(1)} %get-tuple-element.149), channel_id=1, source_target_pairs={{1,0},{2,1},{3,2},{5,4},{6,5},{7,6},{9,8},{10,9},{11,10},{13,12},{... | collective-permute-start | bytes 3848 | tf_op jit(solution)/shard_map/ppermute | solution.py:31
  21.3 0.8 copy.220
  22.1 0.8 copy.219
  22.9 1.5 %collective-permute-done.2 = f32[4,8,10,1]{3,2,1,0:T(8,128)S(1)} collective-permute-done((f32[4,8,10,1]{3,2,1,0:T(8,128)}, f32[4,8,10,1]{3,2,1,0:T(8,128)S(1)}, u32[]{:S(2)}, u32[]{:S(2)}) %collective-permute-start.2) | collective-permute-done | bytes 1312 | tf_op jit(solution)/shard_map/ppermute | solution.py:28
  24.4 3.5 %collective-permute-done.3 = f32[4,8,10,1]{3,2,1,0:T(8,128)S(1)} collective-permute-done((f32[4,8,10,1]{3,2,1,0:T(8,128)S(1)}, f32[4,8,10,1]{3,2,1,0:T(8,128)S(1)}, u32[]{:S(2)}, u32[]{:S(2)}) %collective-permute-start.3) | collective-permute-done | bytes 1312 | tf_op jit(solution)/shard_map/ppermute | solution.py:31
  27.9 0.6 fusion.55
  30.3 2.7 %collective-permute-start.4 = (f32[9,8,8,128]{3,2,1,0:T(8,128)S(1)}, f32[9,8,8,128]{3,2,1,0:T(8,128)S(1)}, u32[]{:S(2)}, u32[]{:S(2)}) collective-permute-start(f32[9,8,8,128]{3,2,1,0:T(8,128)S(1)} %get-tuple-element.145), channel_id=1, source_target_pairs={{0,4},{4,0},{8,12},{12,8},{16,20},{20,16},{24,28},{28,24},{1,5},{5... | collective-permute-start | bytes 884744 | tf_op jit(solution)/shard_map/ppermute | solution.py:37
  33.0 0.2 fusion.146
  33.2 0.3 fusion.123
  33.5 0.3 fusion.135
  33.8 0.5 collective-permute-done.4
  34.4 1.1 %copy-done.1 = f32[1,16,8,16,128]{4,3,2,1,0:T(8,128)S(1)} copy-done((f32[1,16,8,16,128]{4,3,2,1,0:T(8,128)S(1)}, f32[1,16,8,16,128]{4,3,2,1,0:T(8,128)}, u32[]{:S(2)}) %copy-start.1) | copy-done | bytes 1048600
  35.9 1.9 %collective-permute-start.9 = (f32[16,8,1,128]{3,2,1,0:T(1,128)S(1)}, f32[16,8,1,128]{3,2,1,0:T(1,128)S(1)}, u32[]{:S(2)}, u32[]{:S(2)}) collective-permute-start(f32[16,8,1,128]{3,2,1,0:T(1,128)S(1)} %get-tuple-element.100), channel_id=1, source_target_pairs={{8,0},{12,4},{16,8},{20,12},{24,16},{28,20},{9,1},{13,5},{17,9},{2... | collective-permute-start | bytes 196616 | tf_op jit(solution)/shard_map/ppermute | solution.py:43
  37.8 4.3 %collective-permute-start.10 = (f32[16,8,1,128]{3,2,1,0:T(1,128)S(1)}, f32[16,8,1,128]{3,2,1,0:T(1,128)S(1)}, u32[]{:S(2)}, u32[]{:S(2)}) collective-permute-start(f32[16,8,1,128]{3,2,1,0:T(1,128)S(1)} %get-tuple-element.101), channel_id=1, source_target_pairs={{0,8},{4,12},{8,16},{12,20},{16,24},{20,28},{1,9},{5,13},{9,17},{1... | collective-permute-start | bytes 196616 | tf_op jit(solution)/shard_map/ppermute | solution.py:43
  42.1 1.3 %collective-permute-done.10 = f32[16,8,1,128]{3,2,1,0:T(1,128)S(1)} collective-permute-done((f32[16,8,1,128]{3,2,1,0:T(1,128)S(1)}, f32[16,8,1,128]{3,2,1,0:T(1,128)S(1)}, u32[]{:S(2)}, u32[]{:S(2)}) %collective-permute-start.10) | collective-permute-done | bytes 65568 | tf_op jit(solution)/shard_map/ppermute | solution.py:43
  43.4 2.5 %rsqrt_multiply_fusion.1 = (f32[16,8,16,128]{3,2,1,0:T(8,128)S(1)}, f32[16,8,16,128]{3,2,1,0:T(8,128)S(1)}) fusion(f32[16,8,16,128]{3,2,1,0:T(8,128)S(1)} %broadcast_multiply_fusion, f32[16,1,16,128]{3,2,1,0:T(8,128)S(1)} %get-tuple-element.103, f32[16,7,16,128]{3,2,1,0:T(8,128)S(1)} %get-tuple-element.105, f32[8,16,128]{2,1,0:T(8,128)S(1)} %get-tuple-element.167, ...), kind=kLoop, calls=%fused_computation.89 | loop fusion | flops 13369344 | bytes 6111232 | tf_op jit(solution)/shard_map/div | solution.py:165
  45.9 1.6 %fusion.50 = f32[8,16,128,16]{2,3,1,0:T(8,128)S(1)} fusion(f32[16,8,16,128]{3,2,1,0:T(8,128)S(1)} %get-tuple-element.76, f32[16,16]{1,0:T(8,128)S(1)} %copy-done), kind=kOutput, calls=%fused_computation.86 | convolution fusion | flops 50331648 | bytes 2098176 | tf_op jit(solution)/shard_map/nm,mkji->nkji/dot_general | solution.py:166
  47.5 0.4 bitcast_add_fusion.1
  47.9 0.7 fusion.201
  48.7 0.9 slice_reduce_fusion.1
  49.6 1.4 %fusion.203 = (f32[16,7,16,128]{3,2,1,0:T(8,128)}, f32[16,7,16,128]{3,2,1,0:T(8,128)}) fusion(f32[16,8,16,128]{3,2,1,0:T(8,128)S(1)} %bitcast_add_fusion.1), kind=kLoop, calls=%fused_computation.375 | loop fusion | bytes 3670016 | tf_op jit(solution)/shard_map/slice | solution.py:109
  51.0 1.6 %collective-permute-start.11 = (f32[4,8,128]{2,1,0:T(8,128)S(1)}, f32[4,8,128]{2,1,0:T(8,128)S(1)}, u32[]{:S(2)}, u32[]{:S(2)}) collective-permute-start(f32[4,8,128]{2,1,0:T(8,128)S(1)} %get-tuple-element.171), channel_id=1, source_target_pairs={{0,4},{4,0},{8,12},{12,8},{16,20},{20,16},{24,28},{28,24},{1,5},{5... | collective-permute-start | bytes 49160 | tf_op jit(solution)/shard_map/ppermute | solution.py:37
  52.7 0.4 collective-permute-start.19
  53.1 0.7 fusion.202
  53.8 1.9 %collective-permute-start.21 = (f32[16,8,1,128]{3,2,1,0:T(1,128)}, f32[16,8,1,128]{3,2,1,0:T(1,128)}, u32[]{:S(2)}, u32[]{:S(2)}) collective-permute-start(f32[16,8,1,128]{3,2,1,0:T(1,128)} %get-tuple-element.94), channel_id=1, source_target_pairs={{8,0},{12,4},{16,8},{20,12},{24,16},{28,20},{9,1},{13,5},{17,9},{2... | collective-permute-start | bytes 196616 | tf_op jit(solution)/shard_map/ppermute | solution.py:43
  55.7 4.9 %collective-permute-start.22 = (f32[16,8,1,128]{3,2,1,0:T(1,128)}, f32[16,8,1,128]{3,2,1,0:T(1,128)}, u32[]{:S(2)}, u32[]{:S(2)}) collective-permute-start(f32[16,8,1,128]{3,2,1,0:T(1,128)} %get-tuple-element.95), channel_id=1, source_target_pairs={{0,8},{4,12},{8,16},{12,20},{16,24},{20,28},{1,9},{5,13},{9,17},{1... | collective-permute-start | bytes 196616 | tf_op jit(solution)/shard_map/ppermute | solution.py:43
  60.6 1.3 %collective-permute-start.18 = (f32[16,8,16]{2,1,0:T(8,128)S(1)}, f32[16,8,16]{2,1,0:T(8,128)S(1)}, u32[]{:S(2)}, u32[]{:S(2)}) collective-permute-start(f32[16,8,16]{2,1,0:T(8,128)S(1)} %collective-permute-done.17), channel_id=1, source_target_pairs={{1,0},{2,1},{3,2},{5,4},{6,5},{7,6},{9,8},{10,9},{11,10},{13,12},{... | collective-permute-start | bytes 24584 | tf_op jit(solution)/shard_map/ppermute | solution.py:43
  61.9 4.0 %collective-permute-start.20 = (f32[16,8,16]{2,1,0:T(8,128)S(1)}, f32[16,8,16]{2,1,0:T(8,128)S(1)}, u32[]{:S(2)}, u32[]{:S(2)}) collective-permute-start(f32[16,8,16]{2,1,0:T(8,128)S(1)} %collective-permute-done.19), channel_id=1, source_target_pairs={{0,1},{1,2},{2,3},{4,5},{5,6},{6,7},{8,9},{9,10},{10,11},{12,13},{... | collective-permute-start | bytes 24584 | tf_op jit(solution)/shard_map/ppermute | solution.py:43
  66.0 5.0 %collective-permute-start.12 = (f32[4,8,1,256]{3,2,1,0:T(1,128)S(1)}, f32[4,8,1,256]{3,2,1,0:T(1,128)S(1)}, u32[]{:S(2)}, u32[]{:S(2)}) collective-permute-start(f32[4,8,1,256]{3,2,1,0:T(1,128)S(1)} %get-tuple-element.150), channel_id=1, source_target_pairs={{0,4},{4,8},{8,12},{12,16},{16,20},{20,24},{24,28},{1,5},{5,9},{9,... | collective-permute-start | bytes 98312 | tf_op jit(solution)/shard_map/ppermute | solution.py:28
  71.1 1.9 %collective-permute-start.13 = (f32[4,8,1,256]{3,2,1,0:T(1,128)S(1)}, f32[4,8,1,256]{3,2,1,0:T(1,128)S(1)}, u32[]{:S(2)}, u32[]{:S(2)}) collective-permute-start(f32[4,8,1,256]{3,2,1,0:T(1,128)S(1)} %get-tuple-element.151), channel_id=1, source_target_pairs={{4,0},{8,4},{12,8},{16,12},{20,16},{24,20},{28,24},{5,1},{9,5},{13... | collective-permute-start | bytes 98312 | tf_op jit(solution)/shard_map/ppermute | solution.py:31
  73.0 0.6 select_bitcast_fusion.1
  73.7 3.6 %collective-permute-done.13 = f32[4,8,1,256]{3,2,1,0:T(1,128)S(1)} collective-permute-done((f32[4,8,1,256]{3,2,1,0:T(1,128)S(1)}, f32[4,8,1,256]{3,2,1,0:T(1,128)S(1)}, u32[]{:S(2)}, u32[]{:S(2)}) %collective-permute-start.13) | collective-permute-done | bytes 32800 | tf_op jit(solution)/shard_map/ppermute | solution.py:31
  77.3 0.5 copy-done.10
  77.8 0.9 fusion.207
  78.7 3.9 %collective-permute-start.14 = (f32[4,8,10,1]{3,2,1,0:T(8,128)}, f32[4,8,10,1]{3,2,1,0:T(8,128)}, u32[]{:S(2)}, u32[]{:S(2)}) collective-permute-start(f32[4,8,10,1]{3,2,1,0:T(8,128)} %get-tuple-element.146), channel_id=1, source_target_pairs={{0,1},{1,2},{2,3},{4,5},{5,6},{6,7},{8,9},{9,10},{10,11},{12,13},{... | collective-permute-start | bytes 3848 | tf_op jit(solution)/shard_map/ppermute | solution.py:28
  82.6 1.5 %collective-permute-start.15 = (f32[4,8,10,1]{3,2,1,0:T(8,128)}, f32[4,8,10,1]{3,2,1,0:T(8,128)}, u32[]{:S(2)}, u32[]{:S(2)}) collective-permute-start(f32[4,8,10,1]{3,2,1,0:T(8,128)} %get-tuple-element.147), channel_id=1, source_target_pairs={{1,0},{2,1},{3,2},{5,4},{6,5},{7,6},{9,8},{10,9},{11,10},{13,12},{... | collective-permute-start | bytes 3848 | tf_op jit(solution)/shard_map/ppermute | solution.py:31
  84.1 0.8 copy.226
  84.9 1.7 %copy.225 = f32[16,8,16,1]{3,2,1,0:T(8,128)S(1)} copy(f32[16,8,16,1]{2,1,0,3:T(8,128)} %select_bitcast_fusion.1) | data formatting | bytes 16384 | tf_op jit(solution)/shard_map/broadcast_in_dim | solution.py:241
  86.6 4.0 %collective-permute-done.15 = f32[4,8,10,1]{3,2,1,0:T(8,128)} collective-permute-done((f32[4,8,10,1]{3,2,1,0:T(8,128)}, f32[4,8,10,1]{3,2,1,0:T(8,128)}, u32[]{:S(2)}, u32[]{:S(2)}) %collective-permute-start.15) | collective-permute-done | bytes 1312 | tf_op jit(solution)/shard_map/ppermute | solution.py:31
  90.6 1.7 %fusion.59 = f32[4,8,10,258]{3,2,1,0:T(8,128)S(1)} fusion(f32[1,8,8,256]{3,2,1,0:T(8,128)S(1)} %fusion.174, f32[4,8,10,1]{3,2,1,0:T(8,128)} %collective-permute-done.15, f32[4,8,1,256]{3,2,1,0:T(1,128)} %copy-done.10, f32[1,8,8,256]{3,2,1,0:T(8,128)S(1)} %fusion.185, f32[1,8,8,256]{3,2,1,0:T(8,128)S(1)} %fusion.123, f32[1,8,8,256]{3,2,1,0:T(8,128)S(1)} %fusion.135, ...), kind=kLoop, calls=%fused_computation.97 | loop fusion | flops 577920 | bytes 660480 | tf_op jit(solution)/shard_map/concatenate | solution.py:32
  92.5 0.6 copy-done.18
  93.1 0.3 fusion.88
  93.3 0.3 copy-done.16
  93.7 0.2 fusion.100
  95.8 1.3 %collective-permute-done.16 = f32[9,8,8,128]{3,2,1,0:T(8,128)S(1)} collective-permute-done((f32[9,8,8,128]{3,2,1,0:T(8,128)S(1)}, f32[9,8,8,128]{3,2,1,0:T(8,128)S(1)}, u32[]{:S(2)}, u32[]{:S(2)}) %collective-permute-start.16) | collective-permute-done | bytes 294944 | tf_op jit(solution)/shard_map/ppermute | solution.py:37
  97.3 0.7 copy-done.5
  98.0 0.4 copy-done.2
  98.4 0.3 copy-done.3
  98.6 3.3 %rsqrt_multiply_fusion = (f32[16,8,16,128]{3,2,1,0:T(8,128)S(1)}, f32[16,8,16,128]{3,2,1,0:T(8,128)S(1)}) fusion(f32[16,8,16,128]{3,2,1,0:T(8,128)S(1)} %bitcast_add_fusion.1, f32[16,1,16,128]{3,2,1,0:T(8,128)S(1)} %copy-done.5, f32[16,7,16,128]{3,2,1,0:T(8,128)S(1)} %copy-done.3, f32[8,16,128]{2,1,0:T(8,128)S(1)} %get-tuple-element.165, ...), kind=kLoop, calls=%fused_computation.88 | loop fusion | flops 13369344 | bytes 6111232 | tf_op jit(solution)/shard_map/div | solution.py:165
  101.9 1.6 %fusion.48 = f32[8,16,128,16]{2,3,1,0:T(8,128)S(1)} fusion(f32[16,8,16,128]{3,2,1,0:T(8,128)S(1)} %get-tuple-element.58, f32[16,16]{1,0:T(8,128)S(1)} %copy-done), kind=kOutput, calls=%fused_computation.83 | convolution fusion | flops 50331648 | bytes 2098176 | tf_op jit(solution)/shard_map/nm,mkji->nkji/dot_general | solution.py:166
  103.5 0.4 bitcast_add_fusion
  104.0 0.2 collective-permute-start.23
  104.2 0.7 pad_maximum_fusion.18
  104.9 0.3 collective-permute-done.23
  105.3 0.6 copy-done.6
  (124 shorter events, 5.1 us)
Async XLA Ops:
  0.6 45.3 %copy-start = (f32[16,16]{1,0:T(8,128)S(1)}, f32[16,16]{1,0:T(8,128)}, u32[]{:S(2)}) copy-start(f32[16,16]{1,0:T(8,128)} %param.15) | copy-start | bytes 3076
  0.6 3.3 %copy-start.7 = (s32[8,256]{1,0:T(8,128)S(1)}, s32[8,256]{1,0:T(8,128)}, u32[]{:S(2)}) copy-start(s32[8,256]{1,0:T(8,128)} %param.13) | copy-start | bytes 24580
  0.7 3.3 %copy-start.13 = (f32[8,8,256]{2,1,0:T(8,128)S(1)}, f32[8,8,256]{2,1,0:T(8,128)}, u32[]{:S(2)}) copy-start(f32[8,8,256]{2,1,0:T(8,128)} %param.11) | copy-start | bytes 196612
  3.2 0.9 copy-start.8
  3.2 7.2 %collective-permute-start.5 = (f32[16,8,16]{2,1,0:T(8,128)S(1)}, f32[16,8,16]{2,1,0:T(8,128)S(1)}, u32[]{:S(2)}, u32[]{:S(2)}) collective-permute-start(f32[16,8,16]{2,1,0:T(8,128)S(1)} %get-tuple-element.56), channel_id=1, source_target_pairs={{0,4},{4,0},{8,12},{12,8},{16,20},{20,16},{24,28},{28,24},{1,5},{5... | collective-permute-start | bytes 24584 | tf_op jit(solution)/shard_map/ppermute | solution.py:37
  3.9 7.8 %collective-permute-start.7 = (f32[16,8,16]{2,1,0:T(8,128)S(1)}, f32[16,8,16]{2,1,0:T(8,128)S(1)}, u32[]{:S(2)}, u32[]{:S(2)}) collective-permute-start(f32[16,8,16]{2,1,0:T(8,128)S(1)} %get-tuple-element.57), channel_id=1, source_target_pairs={{0,4},{4,0},{8,12},{12,8},{16,20},{20,16},{24,28},{28,24},{1,5},{5... | collective-permute-start | bytes 24584 | tf_op jit(solution)/shard_map/ppermute | solution.py:37
  4.2 11.6 %collective-permute-start = (f32[4,8,1,256]{3,2,1,0:T(1,128)S(1)}, f32[4,8,1,256]{3,2,1,0:T(1,128)S(1)}, u32[]{:S(2)}, u32[]{:S(2)}) collective-permute-start(f32[4,8,1,256]{3,2,1,0:T(1,128)S(1)} %get-tuple-element.152), channel_id=1, source_target_pairs={{0,4},{4,8},{8,12},{12,16},{16,20},{20,24},{24,28},{1,5},{5,9},{9,... | collective-permute-start | bytes 98312 | tf_op jit(solution)/shard_map/ppermute | solution.py:28
  7.8 7.9 %collective-permute-start.1 = (f32[4,8,1,256]{3,2,1,0:T(1,128)S(1)}, f32[4,8,1,256]{3,2,1,0:T(1,128)S(1)}, u32[]{:S(2)}, u32[]{:S(2)}) collective-permute-start(f32[4,8,1,256]{3,2,1,0:T(1,128)S(1)} %get-tuple-element.153), channel_id=1, source_target_pairs={{4,0},{8,4},{12,8},{16,12},{20,16},{24,20},{28,24},{5,1},{9,5},{13... | collective-permute-start | bytes 98312 | tf_op jit(solution)/shard_map/ppermute | solution.py:31
  10.4 5.3 %collective-permute-start.6 = (f32[16,8,16]{2,1,0:T(8,128)S(1)}, f32[16,8,16]{2,1,0:T(8,128)S(1)}, u32[]{:S(2)}, u32[]{:S(2)}) collective-permute-start(f32[16,8,16]{2,1,0:T(8,128)S(1)} %collective-permute-done.5), channel_id=1, source_target_pairs={{1,0},{2,1},{3,2},{5,4},{6,5},{7,6},{9,8},{10,9},{11,10},{13,12},{... | collective-permute-start | bytes 24584 | tf_op jit(solution)/shard_map/ppermute | solution.py:43
  11.7 21.5 %copy-start.17 = (f32[8]{0:T(128)}, f32[8]{0:T(128)S(1)}, u32[]{:S(2)}) copy-start(f32[8]{0:T(128)S(1)} %get-tuple-element.173) | copy-start | bytes 100
  11.7 21.8 %copy-start.15 = (f32[8]{0:T(128)}, f32[8]{0:T(128)S(1)}, u32[]{:S(2)}) copy-start(f32[8]{0:T(128)S(1)} %get-tuple-element.172) | copy-start | bytes 100
  11.7 9.5 %collective-permute-start.8 = (f32[16,8,16]{2,1,0:T(8,128)S(1)}, f32[16,8,16]{2,1,0:T(8,128)S(1)}, u32[]{:S(2)}, u32[]{:S(2)}) collective-permute-start(f32[16,8,16]{2,1,0:T(8,128)S(1)} %collective-permute-done.7), channel_id=1, source_target_pairs={{0,1},{1,2},{2,3},{4,5},{5,6},{6,7},{8,9},{9,10},{10,11},{12,13},{... | collective-permute-start | bytes 24584 | tf_op jit(solution)/shard_map/ppermute | solution.py:43
  16.7 7.7 %collective-permute-start.2 = (f32[4,8,10,1]{3,2,1,0:T(8,128)}, f32[4,8,10,1]{3,2,1,0:T(8,128)S(1)}, u32[]{:S(2)}, u32[]{:S(2)}) collective-permute-start(f32[4,8,10,1]{3,2,1,0:T(8,128)} %get-tuple-element.148), channel_id=1, source_target_pairs={{0,1},{1,2},{2,3},{4,5},{5,6},{6,7},{8,9},{9,10},{10,11},{12,13},{... | collective-permute-start | bytes 3848 | tf_op jit(solution)/shard_map/ppermute | solution.py:28
  19.9 8.0 %collective-permute-start.3 = (f32[4,8,10,1]{3,2,1,0:T(8,128)S(1)}, f32[4,8,10,1]{3,2,1,0:T(8,128)S(1)}, u32[]{:S(2)}, u32[]{:S(2)}) collective-permute-start(f32[4,8,10,1]{3,2,1,0:T(8,128)S(1)} %get-tuple-element.149), channel_id=1, source_target_pairs={{1,0},{2,1},{3,2},{5,4},{6,5},{7,6},{9,8},{10,9},{11,10},{13,12},{... | collective-permute-start | bytes 3848 | tf_op jit(solution)/shard_map/ppermute | solution.py:31
  30.3 3.9 %collective-permute-start.4 = (f32[9,8,8,128]{3,2,1,0:T(8,128)S(1)}, f32[9,8,8,128]{3,2,1,0:T(8,128)S(1)}, u32[]{:S(2)}, u32[]{:S(2)}) collective-permute-start(f32[9,8,8,128]{3,2,1,0:T(8,128)S(1)} %get-tuple-element.145), channel_id=1, source_target_pairs={{0,4},{4,0},{8,12},{12,8},{16,20},{20,16},{24,28},{28,24},{1,5},{5... | collective-permute-start | bytes 884744 | tf_op jit(solution)/shard_map/ppermute | solution.py:37
  34.3 1.2 %copy-start.1 = (f32[1,16,8,16,128]{4,3,2,1,0:T(8,128)S(1)}, f32[1,16,8,16,128]{4,3,2,1,0:T(8,128)}, u32[]{:S(2)}) copy-start(f32[1,16,8,16,128]{4,3,2,1,0:T(8,128)} %param.12) | copy-start | bytes 3145732
  35.9 6.2 %collective-permute-start.9 = (f32[16,8,1,128]{3,2,1,0:T(1,128)S(1)}, f32[16,8,1,128]{3,2,1,0:T(1,128)S(1)}, u32[]{:S(2)}, u32[]{:S(2)}) collective-permute-start(f32[16,8,1,128]{3,2,1,0:T(1,128)S(1)} %get-tuple-element.100), channel_id=1, source_target_pairs={{8,0},{12,4},{16,8},{20,12},{24,16},{28,20},{9,1},{13,5},{17,9},{2... | collective-permute-start | bytes 196616 | tf_op jit(solution)/shard_map/ppermute | solution.py:43
  37.8 5.6 %collective-permute-start.10 = (f32[16,8,1,128]{3,2,1,0:T(1,128)S(1)}, f32[16,8,1,128]{3,2,1,0:T(1,128)S(1)}, u32[]{:S(2)}, u32[]{:S(2)}) collective-permute-start(f32[16,8,1,128]{3,2,1,0:T(1,128)S(1)} %get-tuple-element.101), channel_id=1, source_target_pairs={{0,8},{4,12},{8,16},{12,20},{16,24},{20,28},{1,9},{5,13},{9,17},{1... | collective-permute-start | bytes 196616 | tf_op jit(solution)/shard_map/ppermute | solution.py:43
  51.0 14.9 %collective-permute-start.11 = (f32[4,8,128]{2,1,0:T(8,128)S(1)}, f32[4,8,128]{2,1,0:T(8,128)S(1)}, u32[]{:S(2)}, u32[]{:S(2)}) collective-permute-start(f32[4,8,128]{2,1,0:T(8,128)S(1)} %get-tuple-element.171), channel_id=1, source_target_pairs={{0,4},{4,0},{8,12},{12,8},{16,20},{20,16},{24,28},{28,24},{1,5},{5... | collective-permute-start | bytes 49160 | tf_op jit(solution)/shard_map/ppermute | solution.py:37
  52.6 8.0 %collective-permute-start.17 = (f32[16,8,16]{2,1,0:T(8,128)S(1)}, f32[16,8,16]{2,1,0:T(8,128)S(1)}, u32[]{:S(2)}, u32[]{:S(2)}) collective-permute-start(f32[16,8,16]{2,1,0:T(8,128)S(1)} %get-tuple-element.54), channel_id=1, source_target_pairs={{0,4},{4,0},{8,12},{12,8},{16,20},{20,16},{24,28},{28,24},{1,5},{5... | collective-permute-start | bytes 24584 | tf_op jit(solution)/shard_map/ppermute | solution.py:37
  52.6 13.3 %copy-start.11 = (pred[8,8,256]{2,1,0:T(8,128)(4,1)S(1)}, pred[8,8,256]{2,1,0:T(8,128)(4,1)}, u32[]{:S(2)}) copy-start(pred[8,8,256]{2,1,0:T(8,128)(4,1)} %iota_compare_fusion) | copy-start | bytes 49156
  52.7 9.3 %collective-permute-start.19 = (f32[16,8,16]{2,1,0:T(8,128)S(1)}, f32[16,8,16]{2,1,0:T(8,128)S(1)}, u32[]{:S(2)}, u32[]{:S(2)}) collective-permute-start(f32[16,8,16]{2,1,0:T(8,128)S(1)} %get-tuple-element.55), channel_id=1, source_target_pairs={{0,4},{4,0},{8,12},{12,8},{16,20},{20,16},{24,28},{28,24},{1,5},{5... | collective-permute-start | bytes 24584 | tf_op jit(solution)/shard_map/ppermute | solution.py:37
  53.1 12.8 %copy-start.14 = (f32[8,256]{1,0:T(8,128)S(1)}, f32[8,256]{1,0:T(8,128)}, u32[]{:S(2)}) copy-start(f32[8,256]{1,0:T(8,128)} %param.14) | copy-start | bytes 24580
  53.8 43.5 %collective-permute-start.21 = (f32[16,8,1,128]{3,2,1,0:T(1,128)}, f32[16,8,1,128]{3,2,1,0:T(1,128)}, u32[]{:S(2)}, u32[]{:S(2)}) collective-permute-start(f32[16,8,1,128]{3,2,1,0:T(1,128)} %get-tuple-element.94), channel_id=1, source_target_pairs={{8,0},{12,4},{16,8},{20,12},{24,16},{28,20},{9,1},{13,5},{17,9},{2... | collective-permute-start | bytes 196616 | tf_op jit(solution)/shard_map/ppermute | solution.py:43
  55.7 41.6 %collective-permute-start.22 = (f32[16,8,1,128]{3,2,1,0:T(1,128)}, f32[16,8,1,128]{3,2,1,0:T(1,128)}, u32[]{:S(2)}, u32[]{:S(2)}) collective-permute-start(f32[16,8,1,128]{3,2,1,0:T(1,128)} %get-tuple-element.95), channel_id=1, source_target_pairs={{0,8},{4,12},{8,16},{12,20},{16,24},{20,28},{1,9},{5,13},{9,17},{1... | collective-permute-start | bytes 196616 | tf_op jit(solution)/shard_map/ppermute | solution.py:43
  60.6 10.5 %collective-permute-start.18 = (f32[16,8,16]{2,1,0:T(8,128)S(1)}, f32[16,8,16]{2,1,0:T(8,128)S(1)}, u32[]{:S(2)}, u32[]{:S(2)}) collective-permute-start(f32[16,8,16]{2,1,0:T(8,128)S(1)} %collective-permute-done.17), channel_id=1, source_target_pairs={{1,0},{2,1},{3,2},{5,4},{6,5},{7,6},{9,8},{10,9},{11,10},{13,12},{... | collective-permute-start | bytes 24584 | tf_op jit(solution)/shard_map/ppermute | solution.py:43
  61.9 22.2 %collective-permute-start.20 = (f32[16,8,16]{2,1,0:T(8,128)S(1)}, f32[16,8,16]{2,1,0:T(8,128)S(1)}, u32[]{:S(2)}, u32[]{:S(2)}) collective-permute-start(f32[16,8,16]{2,1,0:T(8,128)S(1)} %collective-permute-done.19), channel_id=1, source_target_pairs={{0,1},{1,2},{2,3},{4,5},{5,6},{6,7},{8,9},{9,10},{10,11},{12,13},{... | collective-permute-start | bytes 24584 | tf_op jit(solution)/shard_map/ppermute | solution.py:43
  66.0 7.6 %collective-permute-start.12 = (f32[4,8,1,256]{3,2,1,0:T(1,128)S(1)}, f32[4,8,1,256]{3,2,1,0:T(1,128)S(1)}, u32[]{:S(2)}, u32[]{:S(2)}) collective-permute-start(f32[4,8,1,256]{3,2,1,0:T(1,128)S(1)} %get-tuple-element.150), channel_id=1, source_target_pairs={{0,4},{4,8},{8,12},{12,16},{16,20},{20,24},{24,28},{1,5},{5,9},{9,... | collective-permute-start | bytes 98312 | tf_op jit(solution)/shard_map/ppermute | solution.py:28
  71.1 6.1 %collective-permute-start.13 = (f32[4,8,1,256]{3,2,1,0:T(1,128)S(1)}, f32[4,8,1,256]{3,2,1,0:T(1,128)S(1)}, u32[]{:S(2)}, u32[]{:S(2)}) collective-permute-start(f32[4,8,1,256]{3,2,1,0:T(1,128)S(1)} %get-tuple-element.151), channel_id=1, source_target_pairs={{4,0},{8,4},{12,8},{16,12},{20,16},{24,20},{28,24},{5,1},{9,5},{13... | collective-permute-start | bytes 98312 | tf_op jit(solution)/shard_map/ppermute | solution.py:31
  73.7 3.7 %copy-start.9 = (f32[4,8,1,256]{3,2,1,0:T(1,128)}, f32[4,8,1,256]{3,2,1,0:T(1,128)S(1)}, u32[]{:S(2)}) copy-start(f32[4,8,1,256]{3,2,1,0:T(1,128)S(1)} %collective-permute-done.12) | copy-start | bytes 98308
  77.2 0.6 copy-start.10
  78.7 7.9 %collective-permute-start.14 = (f32[4,8,10,1]{3,2,1,0:T(8,128)}, f32[4,8,10,1]{3,2,1,0:T(8,128)}, u32[]{:S(2)}, u32[]{:S(2)}) collective-permute-start(f32[4,8,10,1]{3,2,1,0:T(8,128)} %get-tuple-element.146), channel_id=1, source_target_pairs={{0,1},{1,2},{2,3},{4,5},{5,6},{6,7},{8,9},{9,10},{10,11},{12,13},{... | collective-permute-start | bytes 3848 | tf_op jit(solution)/shard_map/ppermute | solution.py:28
  82.6 8.0 %collective-permute-start.15 = (f32[4,8,10,1]{3,2,1,0:T(8,128)}, f32[4,8,10,1]{3,2,1,0:T(8,128)}, u32[]{:S(2)}, u32[]{:S(2)}) collective-permute-start(f32[4,8,10,1]{3,2,1,0:T(8,128)} %get-tuple-element.147), channel_id=1, source_target_pairs={{1,0},{2,1},{3,2},{5,4},{6,5},{7,6},{9,8},{10,9},{11,10},{13,12},{... | collective-permute-start | bytes 3848 | tf_op jit(solution)/shard_map/ppermute | solution.py:31
  92.5 0.6 copy-start.18
  93.1 0.6 copy-start.16
  95.5 1.6 %collective-permute-start.16 = (f32[9,8,8,128]{3,2,1,0:T(8,128)S(1)}, f32[9,8,8,128]{3,2,1,0:T(8,128)S(1)}, u32[]{:S(2)}, u32[]{:S(2)}) collective-permute-start(f32[9,8,8,128]{3,2,1,0:T(8,128)S(1)} %get-tuple-element.133), channel_id=1, source_target_pairs={{0,4},{4,0},{8,12},{12,8},{16,20},{20,16},{24,28},{28,24},{1,5},{5... | collective-permute-start | bytes 884744 | tf_op jit(solution)/shard_map/ppermute | solution.py:37
  97.1 0.9 copy-start.5
  97.2 1.2 %copy-start.2 = (f32[16,7,16,128]{3,2,1,0:T(8,128)S(1)}, f32[16,7,16,128]{3,2,1,0:T(8,128)}, u32[]{:S(2)}) copy-start(f32[16,7,16,128]{3,2,1,0:T(8,128)} %get-tuple-element.98) | copy-start | bytes 2752516
  97.2 1.5 %copy-start.3 = (f32[16,7,16,128]{3,2,1,0:T(8,128)S(1)}, f32[16,7,16,128]{3,2,1,0:T(8,128)}, u32[]{:S(2)}) copy-start(f32[16,7,16,128]{3,2,1,0:T(8,128)} %get-tuple-element.99) | copy-start | bytes 2752516
  103.9 1.4 %copy-start.4 = (f32[16,8,16,128]{3,2,1,0:T(8,128)}, f32[16,8,16,128]{3,2,1,0:T(8,128)S(1)}, u32[]{:S(2)}) copy-start(f32[16,8,16,128]{3,2,1,0:T(8,128)S(1)} %bitcast_add_fusion) | copy-start | bytes 3145732
  104.0 1.3 %copy-start.12 = (pred[8,8,256]{2,1,0:T(8,128)(4,1)S(1)}, pred[8,8,256]{2,1,0:T(8,128)(4,1)}, u32[]{:S(2)}) copy-start(pred[8,8,256]{2,1,0:T(8,128)(4,1)} %iota_compare_fusion) | copy-start | bytes 49156
  104.0 1.2 %collective-permute-start.23 = (f32[4,8,128]{2,1,0:T(8,128)S(1)}, f32[4,8,128]{2,1,0:T(8,128)S(1)}, u32[]{:S(2)}, u32[]{:S(2)}) collective-permute-start(f32[4,8,128]{2,1,0:T(8,128)S(1)} %get-tuple-element.169), channel_id=1, source_target_pairs={{0,4},{4,0},{8,12},{12,8},{16,20},{20,16},{24,28},{28,24},{1,5},{5... | collective-permute-start | bytes 49160 | tf_op jit(solution)/shard_map/ppermute | solution.py:37
  105.3 0.6 copy-start.6
where the time goes:
time: 107 us; the launch traced here: 106 us
  starting transfers between devices  51.8 us (48%)
  local copies, waits for them, and re-layouts  17.7 us (17%)
  waiting for transfers between devices  16 us (15%)
  other arithmetic  15.5 us (14%)
  matrix products  3.22 us (3%)
  between operations  1.65 us (2%)
    ppermute x8, starting transfers between devices, passed_along(): return lax.ppermute(array, axis, pairs)  23.5 us
    ppermute x4, starting transfers between devices, extended(): lax.ppermute(lax.slice_in_dim(block, block.shape[dim] - width, None, axis...  15.8 us
    ppermute x4, waiting for transfers between devices, extended(): lax.ppermute(lax.slice_in_dim(block, 0, width, axis=dim), axis, backward)  11.1 us
    ppermute x4, starting transfers between devices, extended(): lax.ppermute(lax.slice_in_dim(block, 0, width, axis=dim), axis, backward)  6.59 us
    ppermute x8, starting transfers between devices, from_partner(): lax.ppermute(array, axis, [(i, i ^ 1 << bit) for i in range(lax.axis_size...  5.87 us
    div x2, other arithmetic, reaction(): saturated = moved_field / jnp.sqrt(1.0 + moved_field * moved_field)  5.77 us
    unnamed x39, local copies, waits for them, and re-layouts  4.58 us
    slice x2, local copies, waits for them, and re-layouts, on_device(): tracer_field[..., 0]  3.38 us
  transfers between devices with their start and end apart: 24, of which 8 were waited for; matrix products, arithmetic and copies ran while one was open for 13% of the time, Pallas kernels for 0%

commit v1 on v0

v1 whole, which is shorter than its diff:
```python
import functools
import jax
import jax.numpy as jnp
from jax import lax
from jax.experimental import pallas as pl
from jax.experimental.pallas import tpu as pltpu
from jax.sharding import PartitionSpec as P

KL = 4
STEPS = 2

time_step = 0.2
viscosity = 0.2
expansion = 0.05
coriolis_base = 0.5
kappa_base = 0.05
kappa_shear = 0.2
react_step = 0.25
water_absorb = 0.1
pigment_absorb = 0.6
heat_gain = 1.0

EXTRA = 4
WIN = 4


def up(x):
    return pltpu.roll(x, 1, 0)


def down(x):
    return pltpu.roll(x, x.shape[0] - 1, 0)


def lanes_of(shape):
    return lax.broadcasted_iota(jnp.int32, shape, 1)


def levels_of(shape):
    return lax.broadcasted_iota(jnp.int32, shape, 0)


def window(x, lat, into):
    lon = x.shape[1]
    lane = lanes_of(x.shape)
    base = WIN * (lat + 1)
    moved = pltpu.roll(x, (base + 2) % lon, 1)
    return jnp.where((lane >= base) & (lane < base + WIN), moved, into)


def pack_kernel(sc, flow, temp, tracers, bottom, sunlight, mine, other, g_send, g_other):
    nz, lat_dev, lon_dev = temp.shape
    ntr, _, lat_blk, lon = tracers.shape
    first = sc[0] == 0
    zero = jnp.zeros((nz, lon), jnp.float32)
    level = levels_of((nz, lon_dev))
    own = [zero] * EXTRA
    far = [zero] * EXTRA
    for t in range(lat_dev):
        depth = jnp.broadcast_to(bottom[t : t + 1, :], (nz, lon_dev))
        light = jnp.broadcast_to(sunlight[t : t + 1, :], (nz, lon_dev))
        wet = (level < depth).astype(jnp.float32)
        aux = jnp.where(level == 0, depth.astype(jnp.float32), jnp.where(level == 1, light, 0.0))
        for f, tile in enumerate((flow[0, :, t, :] * wet, flow[1, :, t, :] * wet, temp[:, t, :] * wet, aux)):
            low, high = (tile[:, :lon], tile[:, lon:])
            a, b = (jnp.where(first, low, high), jnp.where(first, high, low))
            mine[f, t] = a
            other[f, t] = b
            own[f] = window(a, t, own[f])
            far[f] = window(b, t, far[f])
    shift = sc[0] * (WIN * lat_dev)
    for f in range(EXTRA):
        g_send[ntr + f] = pltpu.roll(own[f], shift, 1)
        g_other[f] = pltpu.roll(far[f], shift, 1)

    def one(n, _):
        g = zero
        for t in range(lat_blk):
            g = window(tracers[n, :, t, :], t, g)
        g_send[n] = g
        return 0

    lax.fori_loop(0, ntr, one, 0)


def in_half(shape, half, lat_dev):
    lane = lanes_of(shape)
    base = WIN * (lat_dev * half + 1)
    return (lane >= base) & (lane < base + WIN * lat_dev)


def join_kernel(sc, mine, got, g_send, ocean, g_own):
    _, lat_dev, nz, lon = mine.shape
    ntr = g_send.shape[0] - EXTRA
    half = sc[0]
    own_lanes = in_half((nz, lon), half, lat_dev)
    zero = jnp.zeros((nz, lon), jnp.float32)
    g_own[:ntr] = g_send[:ntr]
    shift = (1 - half) * (WIN * lat_dev)
    for f in range(EXTRA):
        g = zero
        for t in range(lat_dev):
            ocean[f, half * lat_dev + t] = mine[f, t]
            ocean[f, (1 - half) * lat_dev + t] = got[f, t]
            g = window(got[f, t], t, g)
        g_own[ntr + f] = jnp.where(own_lanes, g_send[ntr + f], pltpu.roll(g, shift, 1))


def edge_kernel(sc, tracers, ocean, g_partner, g_other, g_outer, z, to_a, to_b):
    ntr, nz, lat_blk, lon = tracers.shape
    nf = ntr + EXTRA
    half = sc[0]
    tile = (nz, lon)
    own_lanes = in_half(tile, half, lat_blk // 2)
    west = lanes_of(tile) % WIN < 2
    outer_ok = sc[2] > 0
    even = sc[1] == 0
    lane = lanes_of(tile)
    low_corner = jnp.zeros(tile, jnp.float32)
    high_corner = low_corner
    for f in range(nf):
        partner = g_partner[f]
        if f >= ntr:
            partner = jnp.where(own_lanes, g_other[f - ntr], partner)
        outer = jnp.where(outer_ok, g_outer[f], 0.0)
        from_partner = (west.astype(jnp.int32) == half)
        cols = jnp.where(from_partner, partner, outer)
        z[f] = cols
        at = (lane >= WIN * f) & (lane < WIN * f + WIN)
        low_corner = jnp.where(at, pltpu.roll(cols, (WIN * f - WIN) % lon, 1), low_corner)
        high_corner = jnp.where(at, pltpu.roll(cols, (WIN * f - WIN * lat_blk) % lon, 1), high_corner)

    def fill(out, high):
        start = lat_blk - 2 if high else 0
        for i in range(2):
            for n in range(ntr):
                out[2 * n + i] = tracers[n, :, start + i, :]
            for f in range(EXTRA):
                out[2 * (ntr + f) + i] = ocean[f, start + i]
        out[2 * nf] = high_corner if high else low_corner

    @pl.when(even)
    def _():
        fill(to_a, True)
        fill(to_b, False)

    @pl.when(jnp.logical_not(even))
    def _():
        fill(to_a, False)
        fill(to_b, True)


def kappa_of(u, v):
    level = levels_of(u.shape)
    du, dv = (u - down(u), v - down(v))
    sq = jnp.where(level < u.shape[0] - 1, du * du + dv * dv, 0.0)
    return kappa_base + kappa_shear * sq / (1.0 + sq)


def pressure_of(heat):
    level = levels_of(heat.shape)
    total = heat
    k = 1
    while k < heat.shape[0]:
        total = total + jnp.where(level >= k, pltpu.roll(total, k, 0), 0.0)
        k *= 2
    return -expansion * total


def wet_of(aux):
    depth = jnp.broadcast_to(aux[0:1, :], aux.shape)
    return (levels_of(aux.shape).astype(jnp.float32) < depth).astype(jnp.float32)


def light_of(aux):
    return jnp.broadcast_to(aux[1:2, :], aux.shape)


def dynamics(u, v, wet, kap, prs, coriolis):
    um, ue, uw, un, us = u
    vm, ve, vw, vn, vs = v
    wm, we, ww, wn, ws = wet
    km, ke, kw, kn, ks = kap
    _, pe, pw, pn, ps = prs
    level = levels_of(um.shape)
    nz = um.shape[0]
    oe, ow, on, os_ = (wm * we, wm * ww, wm * wn, wm * ws)
    fe, fw, fn, fs = (0.5 * (um + ue) * oe, 0.5 * (um + uw) * ow, 0.5 * (vm + vn) * on, 0.5 * (vm + vs) * os_)
    ce, cw, cn, cs = (0.5 * (km + ke) * oe, 0.5 * (km + kw) * ow, 0.5 * (km + kn) * on, 0.5 * (km + ks) * os_)
    div = fe - fw + fn - fs
    total = div
    k = 1
    while k < nz:
        total = total + jnp.where(level < nz - k, pltpu.roll(total, nz - k, 0), 0.0)
        k *= 2
    w_top = jnp.where(level >= 1, -total, 0.0)
    w_bot = jnp.where(level < nz - 1, -down(total), 0.0)
    weights = (
        wm * (1.0 - time_step * (ce + cw + cn + cs + 0.5 * (div + w_top - w_bot))),
        time_step * (ce - 0.5 * fe),
        time_step * (cw + 0.5 * fw),
        time_step * (cn - 0.5 * fn),
        time_step * (cs + 0.5 * fs),
        (-0.5 * time_step) * wm * w_top,
        (0.5 * time_step) * wm * w_bot,
    )
    lap_u = oe * (ue - um) + ow * (uw - um) + on * (un - um) + os_ * (us - um)
    lap_v = oe * (ve - vm) + ow * (vw - vm) + on * (vn - vm) + os_ * (vs - vm)
    new_u = wm * (um + time_step * (coriolis * vm - 0.5 * (pe - pw) + viscosity * lap_u))
    new_v = wm * (vm + time_step * (-coriolis * um - 0.5 * (pn - ps) + viscosity * lap_v))
    return (new_u, new_v, weights)


def transport(weights, x, east, west, north, south):
    a0, ae, aw, an, as_, at, ab = weights
    return (a0 * x + ae * east) + (aw * west + an * north) + (as_ * south + at * up(x)) + ab * down(x)


def saturated(x):
    return x * lax.rsqrt(1.0 + x * x)


def absorbed(pigment):
    level = levels_of(pigment.shape)
    sq = pigment * pigment
    depth = water_absorb + pigment_absorb * (sq / (1.0 + sq))
    above = jnp.where(level >= 1, up(depth), 0.0)
    k = 1
    while k < KL:
        above = above + jnp.where(level >= k, pltpu.roll(above, k, 0), 0.0)
        k *= 2
    return jnp.where(level < KL, jnp.exp(-above) * (1.0 - jnp.exp(-depth)), 0.0)


def steps_kernel(total_lat, sc, tracers, ocean, z_in, g_in, got_a, got_b, mix, out, keep, send, m0, m1, dv, z0, z1, g0, zd, sat, uvh):
    ntr, nz, lat_blk, lon = tracers.shape
    nf = ntr + EXTRA
    U, V, H, X = (ntr, ntr + 1, ntr + 2, ntr + 3)
    KAP, PRS, WET = (0, 1, 2)
    tile = (nz, lon)
    lane = lanes_of(tile)
    col = lane % WIN
    at_first, at_last = (lane == 0, lane == lon - 1)
    even = sc[1] == 0
    south_ok, north_ok = (sc[3] > 0, sc[4] > 0)
    first_lat = sc[5] * lat_blk
    rows = lat_blk + 4

    def got(high, index):
        a, b = (got_a[index], got_b[index])
        picked = jnp.where(even, a, b) if high else jnp.where(even, b, a)
        return jnp.where(north_ok if high else south_ok, picked, 0.0)

    for f in range(EXTRA):
        for i in range(2):
            m0[ntr + f, i] = got(False, 2 * (ntr + f) + i)
            m0[ntr + f, lat_blk + 2 + i] = got(True, 2 * (ntr + f) + i)
        for t in range(lat_blk):
            m0[ntr + f, t + 2] = ocean[f, t]

    def derive0(r, _):
        dv[WET, r] = wet_of(m0[X, r])
        dv[KAP, r] = kappa_of(m0[U, r], m0[V, r])
        dv[PRS, r] = pressure_of(m0[H, r])
        return 0

    lax.fori_loop(0, rows, derive0, 0)

    for i in range(2):
        for n in range(ntr):
            m0[n, i] = got(False, 2 * n + i) * dv[WET, i]
            m0[n, lat_blk + 2 + i] = got(True, 2 * n + i) * dv[WET, lat_blk + 2 + i]

    def load(t, _):
        wet = dv[WET, t + 2]
        for n in range(ntr):
            m0[n, t + 2] = tracers[n, :, t, :] * wet
        return 0

    for t in range(lat_blk):
        load(t, 0)

    low_corner, high_corner = (got(False, 2 * nf), got(True, 2 * nf))
    at_low, at_high = (lane < WIN, (lane >= WIN * (lat_blk + 1)) & (lane < WIN * (lat_blk + 2)))
    for f in reversed(range(nf)):
        cols = jnp.where(at_low, pltpu.roll(low_corner, (-WIN * f) % lon, 1), z_in[f])
        cols = jnp.where(at_high, pltpu.roll(high_corner, (WIN * (lat_blk + 1) - WIN * f) % lon, 1), cols)
        own = g_in[f]
        if f == X:
            wet_z, wet_g = (wet_of(cols), wet_of(own))
            light_z = light_of(cols)
        if f < ntr:
            cols, own = (cols * wet_z, own * wet_g)
        z0[f] = cols
        g0[f] = own
    zd[KAP] = kappa_of(z0[U], z0[V])
    zd[PRS] = pressure_of(z0[H])
    zd[WET] = wet_z

    def coriolis_at(lat):
        return coriolis_base * (2.0 * (lat.astype(jnp.float32) + 0.5) / total_lat - 1.0)

    def react(moved, wet):
        for n in range(ntr):
            sat[n * nz : (n + 1) * nz, :] = saturated(moved[n])
        mixed = jnp.dot(mix[...], sat[...], precision=lax.Precision.HIGHEST, preferred_element_type=jnp.float32)
        gain = react_step * wet
        return [moved[n] + gain * mixed[n * nz : (n + 1) * nz, :] for n in range(ntr)]

    def around_z(x, own):
        west = pltpu.roll(jnp.where(col == 0, x, own), 1, 1)
        east = pltpu.roll(jnp.where(col == WIN - 1, x, own), lon - 1, 1)
        return (x, east, west, pltpu.roll(x, lon - WIN, 1), pltpu.roll(x, WIN, 1))

    own_u, own_v = (g0[U], g0[V])
    new_u, new_v, weights = dynamics(
        around_z(z0[U], own_u),
        around_z(z0[V], own_v),
        around_z(wet_z, wet_g),
        around_z(zd[KAP], kappa_of(own_u, own_v)),
        around_z(zd[PRS], pressure_of(g0[H])),
        coriolis_at(first_lat + lane // WIN - 1),
    )
    moved = [transport(weights, *around_z(z0[n], g0[n])) for n in range(ntr)]
    done = react(moved, wet_z)
    for n in range(ntr):
        z1[n] = done[n]
    z1[U] = new_u
    z1[V] = new_v
    z1[H] = transport(weights, *around_z(z0[H], g0[H])) + heat_gain * light_z * wet_z * absorbed(done[0])

    def row_step(r, m, z):
        shift = lon - 2 - WIN * (r - 1)

        def sides(x, cols):
            beside = pltpu.roll(cols, shift, 1)
            west = pltpu.roll(jnp.where(at_last, beside, x), 1, 1)
            east = pltpu.roll(jnp.where(at_first, beside, x), lon - 1, 1)
            return (east, west)

        def around(f):
            x = m[f, r]
            return (x, *sides(x, z[f]), m[f, r + 1], m[f, r - 1])

        def around_dv(f):
            x = dv[f, r]
            return (x, *sides(x, zd[f]), dv[f, r + 1], dv[f, r - 1])

        wet = around_dv(WET)
        new_u, new_v, weights = dynamics(
            around(U), around(V), wet, around_dv(KAP), around_dv(PRS), coriolis_at(first_lat + r - 2)
        )
        moved = [transport(weights, *around(n)) for n in range(ntr)]
        done = react(moved, wet[0])
        heat = transport(weights, *around(H)) + heat_gain * light_of(m0[X, r]) * wet[0] * absorbed(done[0])
        return (done, new_u, new_v, heat)

    def first(r, _):
        done, new_u, new_v, heat = row_step(r, m0, z0)
        for n in range(ntr):
            m1[n, r] = done[n]
        m1[U, r] = new_u
        m1[V, r] = new_v
        m1[H, r] = heat
        return 0

    lax.fori_loop(1, rows - 1, first, 0)

    def derive1(r, _):
        dv[KAP, r] = kappa_of(m1[U, r], m1[V, r])
        dv[PRS, r] = pressure_of(m1[H, r])
        return 0

    lax.fori_loop(1, rows - 1, derive1, 0)
    zd[KAP] = kappa_of(z1[U], z1[V])
    zd[PRS] = pressure_of(z1[H])

    def second(r, _):
        done, new_u, new_v, heat = row_step(r, m1, z1)
        for n in range(ntr):
            m0[n, r] = done[n]
        uvh[0, r - 2] = new_u
        uvh[1, r - 2] = new_v
        uvh[2, r - 2] = heat
        return 0

    lax.fori_loop(2, rows - 2, second, 0)
    for t in range(lat_blk):
        for n in range(ntr):
            out[n, :, t, :] = m0[n, t + 2]
    half = lat_blk // 2
    for f in range(3):
        for t in range(half):
            keep[f, t] = uvh[f, sc[0] * half + t]
            send[f, t] = uvh[f, (1 - sc[0]) * half + t]


def unpack_kernel(sc, keep, got, flow, temp):
    _, lat_dev, nz, lon = keep.shape
    first = sc[0] == 0
    for t in range(lat_dev):
        for f in range(3):
            a, b = (keep[f, t], got[f, t])
            low, high = (jnp.where(first, a, b), jnp.where(first, b, a))
            if f < 2:
                flow[f, :, t, :lon] = low
                flow[f, :, t, lon:] = high
            else:
                temp[:, t, :lon] = low
                temp[:, t, lon:] = high


def call(kernel, outs, *args, scratch=()):
    vmem = pl.BlockSpec(memory_space=pltpu.VMEM)
    return pl.pallas_call(
        kernel,
        out_shape=[jax.ShapeDtypeStruct(s, jnp.float32) for s in outs],
        in_specs=[pl.BlockSpec(memory_space=pltpu.SMEM)] + [vmem] * (len(args) - 1),
        out_specs=[vmem] * len(outs),
        scratch_shapes=[pltpu.VMEM(s, jnp.float32) for s in scratch],
        compiler_params=pltpu.CompilerParams(vmem_limit_bytes=40 * 2**20),
    )(*args)


def both_ways(pairs):
    return sorted(pairs + [(b, a) for a, b in pairs])


def exchanges(n_row, n_col):
    chips = n_row // 2

    def dev(p, h, c):
        return (2 * p + h) * n_col + c

    partner = [(dev(p, 0, c), dev(p, 1, c)) for p in range(chips) for c in range(n_col)]
    outer = [(dev(p, 1, c), dev(p, 0, c + 1)) for p in range(chips) for c in range(n_col - 1)]
    for p in range(0, chips - 1, 2):
        outer += [(dev(p, 0, 0), dev(p + 1, 0, 0)), (dev(p, 1, n_col - 1), dev(p + 1, 1, n_col - 1))]
    lat_a = [(dev(p, h, c), dev(p + 1, h, c)) for p in range(0, chips - 1, 2) for h in (0, 1) for c in range(n_col)]
    lat_b = [(dev(p, h, c), dev(p + 1, h, c)) for p in range(1, chips - 1, 2) for h in (0, 1) for c in range(n_col)]
    if chips % 2 == 0 and chips > 2:
        lat_b += [(dev(0, h, c), dev(chips - 1, h, c)) for h in (0, 1) for c in range(n_col)]
    return [both_ways(x) for x in (partner, outer, lat_a, lat_b)]


def on_device(n_row, n_col, flow, temp, tracers, bottom, sunlight, rates):
    nz, lat_dev, lon_dev = temp.shape
    _, ntr, _, lat_blk, lon = tracers.shape
    nf = ntr + EXTRA
    chips = n_row // 2
    row, column = (lax.axis_index("row"), lax.axis_index("col"))
    half, place = (row % 2, row // 2)
    outer_ok = jnp.where(half == 0, column > 0, column < n_col - 1)
    sc = jnp.stack([half, place % 2, outer_ok, place > 0, place < chips - 1, place]).astype(jnp.int32)
    partner, outer, lat_a, lat_b = exchanges(n_row, n_col)

    def swap(x, pairs):
        return lax.ppermute(x, ("row", "col"), pairs)

    block = tracers[0]
    mix = jnp.kron(rates, jnp.eye(nz, dtype=jnp.float32))
    half_shape = (EXTRA, lat_dev, nz, lon)
    mine, other, g_send, g_other = call(
        pack_kernel, [half_shape, half_shape, (nf, nz, lon), (EXTRA, nz, lon)], sc, flow, temp, block, bottom, sunlight
    )
    got, g_partner = swap((other, g_send), partner)
    ocean, g_own = call(join_kernel, [(EXTRA, lat_blk, nz, lon), (nf, nz, lon)], sc, mine, got, g_send)
    g_outer = swap(g_own, outer)
    edge_shape = (2 * nf + 1, nz, lon)
    z, to_a, to_b = call(
        edge_kernel, [(nf, nz, lon), edge_shape, edge_shape], sc, block, ocean, g_partner, g_other, g_outer
    )
    got_a, got_b = (swap(to_a, lat_a), swap(to_b, lat_b))
    rows = lat_blk + 4
    cols = (nf, nz, lon)
    third = (3, lat_dev, nz, lon)
    out, keep, send = call(
        functools.partial(steps_kernel, n_row * lat_dev),
        [(ntr, nz, lat_blk, lon), third, third],
        sc,
        block,
        ocean,
        z,
        g_own,
        got_a,
        got_b,
        mix,
        scratch=[
            (nf, rows, nz, lon),
            (nf, rows, nz, lon),
            (3, rows, nz, lon),
            cols,
            cols,
            cols,
            (3, nz, lon),
            (ntr * nz, lon),
            (3, lat_blk, nz, lon),
        ],
    )
    flow_out, temp_out = call(
        unpack_kernel, [(2, nz, lat_dev, lon_dev), (nz, lat_dev, lon_dev)], sc, keep, swap(send, partner)
    )
    return (flow_out, temp_out, out[None])


def solution(mesh):
    in_specs = (
        P(None, None, "row", "col"),
        P(None, "row", "col"),
        P("row", None, None, None, "col"),
        P("row", "col"),
        P("row", "col"),
        P(),
    )
    out_specs = (
        P(None, None, "row", "col"),
        P(None, "row", "col"),
        P("row", None, None, None, "col"),
    )
    return jax.shard_map(
        functools.partial(on_device, mesh.shape["row"], mesh.shape["col"]),
        mesh=mesh,
        in_specs=in_specs,
        out_specs=out_specs,
        check_vma=False,
    )
```

time: 107 us -> 46.9 us (0.44)
  the two profiles are of different devices: /device:TPU:3 before, /device:TPU:0 now
where the time goes in v1:
time: 46.9 us; the launch traced here: 46.7 us
  Pallas kernels  23.8 us (51%)
  waiting for transfers between devices  11.6 us (25%)
  starting transfers between devices  7.03 us (15%)
  local copies, waits for them, and re-layouts  3.41 us (7%)
  between operations  0.74 us (2%)
    pallas_call x5, Pallas kernels, call(): pl.pallas_call(kernel, out_shape=[jax.ShapeDtypeStruct(s, jnp.float32) fo...  23.8 us
    ppermute x6, waiting for transfers between devices, swap(): return lax.ppermute(x, ('row', 'col'), pairs)  11.6 us
    ppermute x6, starting transfers between devices, swap(): return lax.ppermute(x, ('row', 'col'), pairs)  7.03 us
    unnamed x14, local copies, waits for them, and re-layouts  2.83 us
  transfers between devices with their start and end apart: 6, of which 5 were waited for; matrix products, arithmetic and copies ran while one was open for 1% of the time, Pallas kernels for 2%

profile of v1, /device:TPU:0, one launch (start us, length us, event | category | flops | bytes accessed | tf_op | source)
XLA Modules:
  0.0 46.7 jit_solution(7086204942179356625)
XLA Ops:
  0.6 0.0 copy-start.3
  0.7 0.0 copy-start.4
  0.7 0.0 copy-start.5
  0.7 0.1 stack.39.sc
  0.8 0.7 %copy-done.3 = f32[8,8,256]{2,1,0:T(8,128)S(1)} copy-done((f32[8,8,256]{2,1,0:T(8,128)S(1)}, f32[8,8,256]{2,1,0:T(8,128)}, u32[]{:S(2)}) %copy-start.3) | copy-done | bytes 65560
  1.5 0.0 copy-done.4
  1.5 0.0 copy-done.5
  1.5 0.0 copy-start
  1.5 1.2 %copy-done = f32[1,16,8,16,128]{4,3,2,1,0:T(8,128)S(1)} copy-done((f32[1,16,8,16,128]{4,3,2,1,0:T(8,128)S(1)}, f32[1,16,8,16,128]{4,3,2,1,0:T(8,128)}, u32[]{:S(2)}) %copy-start) | copy-done | bytes 1048600
  2.7 0.0 copy-start.2
  2.7 0.9 %copy-done.2 = f32[2,8,8,256]{3,2,1,0:T(8,128)S(1)} copy-done((f32[2,8,8,256]{3,2,1,0:T(8,128)S(1)}, f32[2,8,8,256]{3,2,1,0:T(8,128)}, u32[]{:S(2)}) %copy-start.2) | copy-done | bytes 131096
  3.6 0.0 copy-start.1
  3.6 2.5 %shard_map.85 = (f32[4,8,8,128]{3,2,1,0:T(8,128)S(1)}, f32[4,8,8,128]{3,2,1,0:T(8,128)S(1)}, f32[20,8,128]{2,1,0:T(8,128)S(1)}, f32[4,8,128]{2,1,0:T(8,128)S(1)}) custom-call(s32[6]{0:T(128)S(1)} %stack.39.sc, f32[2,8,8,256]{3,2,1,0:T(8,128)S(1)} %copy-done.2, f32[8,8,256]{2,1,0:T(8,128)S(1)} %copy-done.3, f32[16,8,16,128]{3,2,1,0:T(8,128)S(1)} %bitcast.10, ...), custom_call_target="tpu_custom_call" | custom-call | tf_op jit(solution)/shard_map/pallas_call | solution.py:415
  6.1 0.5 %collective-permute-start = (f32[4,8,8,128]{3,2,1,0:T(8,128)S(1)}, f32[4,8,8,128]{3,2,1,0:T(8,128)S(1)}, u32[]{:S(2)}, u32[]{:S(2)}) collective-permute-start(f32[4,8,8,128]{3,2,1,0:T(8,128)S(1)} %get-tuple-element.18), channel_id=1, source_target_pairs={{0,4},{1,5},{2,6},{3,7},{4,0},{5,1},{6,2},{7,3},{8,12},{9,13},{10,... | collective-permute-start | bytes 393224 | tf_op jit(solution)/shard_map/ppermute | solution.py:458
  6.6 0.1 collective-permute-start.1
  6.7 0.9 %collective-permute-done.got = f32[4,8,8,128]{3,2,1,0:T(8,128)S(1)} collective-permute-done((f32[4,8,8,128]{3,2,1,0:T(8,128)S(1)}, f32[4,8,8,128]{3,2,1,0:T(8,128)S(1)}, u32[]{:S(2)}, u32[]{:S(2)}) %collective-permute-start) | collective-permute-done | bytes 131104 | tf_op jit(solution)/shard_map/ppermute | solution.py:458
  7.6 0.7 %shard_map.86 = (f32[4,16,8,128]{3,2,1,0:T(8,128)S(1)}, f32[20,8,128]{2,1,0:T(8,128)S(1)}) custom-call(s32[6]{0:T(128)S(1)} %stack.39.sc, f32[4,8,8,128]{3,2,1,0:T(8,128)S(1)} %get-tuple-element.17.mine, f32[4,8,8,128]{3,2,1,0:T(8,128)S(1)} %collective-permute-done.got, f32[20,8,128]{2,1,0:T(8,128)S(1)} %get-tuple-element.19.g_send), custom_call_target="tpu_custom_call" | custom-call | tf_op jit(solution)/shard_map/pallas_call | solution.py:415
  8.3 2.9 %collective-permute-start.2 = (f32[20,8,128]{2,1,0:T(8,128)S(1)}, f32[20,8,128]{2,1,0:T(8,128)S(1)}, u32[]{:S(2)}, u32[]{:S(2)}) collective-permute-start(f32[20,8,128]{2,1,0:T(8,128)S(1)} %get-tuple-element.22.g_in), channel_id=1, source_target_pairs={{0,8},{1,4},{2,5},{3,6},{4,1},{5,2},{6,3},{7,15},{8,0},{9,12},{10,... | collective-permute-start | bytes 245768 | tf_op jit(solution)/shard_map/ppermute | solution.py:458
  11.2 0.0 collective-permute-done.1.g_partner
  11.2 2.4 %collective-permute-done.2.g_outer = f32[20,8,128]{2,1,0:T(8,128)S(1)} collective-permute-done((f32[20,8,128]{2,1,0:T(8,128)S(1)}, f32[20,8,128]{2,1,0:T(8,128)S(1)}, u32[]{:S(2)}, u32[]{:S(2)}) %collective-permute-start.2) | collective-permute-done | bytes 81952 | tf_op jit(solution)/shard_map/ppermute | solution.py:458
  13.6 0.0 copy-done.1
  13.6 0.0 copy-start.6
  13.6 0.8 %shard_map.87 = (f32[20,8,128]{2,1,0:T(8,128)S(1)}, f32[41,8,128]{2,1,0:T(8,128)S(1)}, f32[41,8,128]{2,1,0:T(8,128)S(1)}) custom-call(s32[6]{0:T(128)S(1)} %stack.39.sc, f32[16,8,16,128]{3,2,1,0:T(8,128)S(1)} %bitcast.11, f32[4,16,8,128]{3,2,1,0:T(8,128)S(1)} %get-tuple-element.20.ocean, f32[20,8,128]{2,1,0:T(8,128)S(1)} %collective-permute-done.1.g_partner, ...), custom_call_target="tpu_custom_call" | custom-call | tf_op jit(solution)/shard_map/pallas_call | solution.py:415
  14.4 2.1 %collective-permute-start.3 = (f32[41,8,128]{2,1,0:T(8,128)S(1)}, f32[41,8,128]{2,1,0:T(8,128)S(1)}, u32[]{:S(2)}, u32[]{:S(2)}) collective-permute-start(f32[41,8,128]{2,1,0:T(8,128)S(1)} %get-tuple-element.24), channel_id=1, source_target_pairs={{0,8},{1,9},{2,10},{3,11},{4,12},{5,13},{6,14},{7,15},{8,0},{9,1},... | collective-permute-start | bytes 503816 | tf_op jit(solution)/shard_map/ppermute | solution.py:458
  16.5 1.5 %collective-permute-start.4 = (f32[41,8,128]{2,1,0:T(8,128)S(1)}, f32[41,8,128]{2,1,0:T(8,128)S(1)}, u32[]{:S(2)}, u32[]{:S(2)}) collective-permute-start(f32[41,8,128]{2,1,0:T(8,128)S(1)} %get-tuple-element.25), channel_id=1, source_target_pairs={{0,24},{1,25},{2,26},{3,27},{4,28},{5,29},{6,30},{7,31},{8,16},{9,... | collective-permute-start | bytes 503816 | tf_op jit(solution)/shard_map/ppermute | solution.py:458
  18.0 0.0 copy-done.6
  18.0 0.1 broadcast_multiply_fusion
  18.1 0.5 %mul.27.mix = f32[128,128]{1,0:T(8,128)S(1)} reshape(f32[16,8,16,8]{3,2,1,0:T(8,128)S(1)} %broadcast_multiply_fusion) | data formatting | bytes 131072 | tf_op jit(solution)/shard_map/jit(kron)/mul | solution.py:461
  18.6 3.0 %collective-permute-done.3.got_a = f32[41,8,128]{2,1,0:T(8,128)S(1)} collective-permute-done((f32[41,8,128]{2,1,0:T(8,128)S(1)}, f32[41,8,128]{2,1,0:T(8,128)S(1)}, u32[]{:S(2)}, u32[]{:S(2)}) %collective-permute-start.3) | collective-permute-done | bytes 167968 | tf_op jit(solution)/shard_map/ppermute | solution.py:458
  21.6 4.0 %collective-permute-done.4.got_b = f32[41,8,128]{2,1,0:T(8,128)S(1)} collective-permute-done((f32[41,8,128]{2,1,0:T(8,128)S(1)}, f32[41,8,128]{2,1,0:T(8,128)S(1)}, u32[]{:S(2)}, u32[]{:S(2)}) %collective-permute-start.4) | collective-permute-done | bytes 167968 | tf_op jit(solution)/shard_map/ppermute | solution.py:458
  25.6 18.5 %shard_map.88 = (f32[16,8,16,128]{3,2,1,0:T(8,128)}, f32[3,8,8,128]{3,2,1,0:T(8,128)S(1)}, f32[3,8,8,128]{3,2,1,0:T(8,128)S(1)}) custom-call(s32[6]{0:T(128)S(1)} %stack.39.sc, f32[16,8,16,128]{3,2,1,0:T(8,128)S(1)} %bitcast.12, f32[4,16,8,128]{3,2,1,0:T(8,128)S(1)} %get-tuple-element.20.ocean, f32[20,8,128]{2,1,0:T(8,128)S(1)} %get-tuple-element.23.z_in, ...), custom_call_target="tpu_custom_call" | custom-call | tf_op jit(solution)/shard_map/pallas_call | solution.py:415
  44.0 0.0 collective-permute-start.5
  44.1 1.3 %collective-permute-done.5.got = f32[3,8,8,128]{3,2,1,0:T(8,128)S(1)} collective-permute-done((f32[3,8,8,128]{3,2,1,0:T(8,128)S(1)}, f32[3,8,8,128]{3,2,1,0:T(8,128)S(1)}, u32[]{:S(2)}, u32[]{:S(2)}) %collective-permute-start.5) | collective-permute-done | bytes 98336 | tf_op jit(solution)/shard_map/ppermute | solution.py:458
  45.4 1.3 %shard_map.89 = (f32[2,8,8,256]{3,2,1,0:T(8,128)}, f32[8,8,256]{2,1,0:T(8,128)}) custom-call(s32[6]{0:T(128)S(1)} %stack.39.sc, f32[3,8,8,128]{3,2,1,0:T(8,128)S(1)} %get-tuple-element.26.keep, f32[3,8,8,128]{3,2,1,0:T(8,128)S(1)} %collective-permute-done.5.got), custom_call_target="tpu_custom_call" | custom-call | tf_op jit(solution)/shard_map/pallas_call | solution.py:415
  (1 shorter events, 0.0 us)
Async XLA Ops:
  0.6 0.8 %copy-start.3 = (f32[8,8,256]{2,1,0:T(8,128)S(1)}, f32[8,8,256]{2,1,0:T(8,128)}, u32[]{:S(2)}) copy-start(f32[8,8,256]{2,1,0:T(8,128)} %temp.1) | copy-start | bytes 196612
  0.7 0.8 %copy-start.4 = (s32[8,256]{1,0:T(8,128)S(1)}, s32[8,256]{1,0:T(8,128)}, u32[]{:S(2)}) copy-start(s32[8,256]{1,0:T(8,128)} %bottom.1) | copy-start | bytes 24580
  0.7 0.8 %copy-start.5 = (f32[8,256]{1,0:T(8,128)S(1)}, f32[8,256]{1,0:T(8,128)}, u32[]{:S(2)}) copy-start(f32[8,256]{1,0:T(8,128)} %sunlight.1) | copy-start | bytes 24580
  1.5 1.2 %copy-start = (f32[1,16,8,16,128]{4,3,2,1,0:T(8,128)S(1)}, f32[1,16,8,16,128]{4,3,2,1,0:T(8,128)}, u32[]{:S(2)}) copy-start(f32[1,16,8,16,128]{4,3,2,1,0:T(8,128)} %param.8) | copy-start | bytes 3145732
  2.7 0.9 %copy-start.2 = (f32[2,8,8,256]{3,2,1,0:T(8,128)S(1)}, f32[2,8,8,256]{3,2,1,0:T(8,128)}, u32[]{:S(2)}) copy-start(f32[2,8,8,256]{3,2,1,0:T(8,128)} %flow.1) | copy-start | bytes 393220
  3.6 10.0 %copy-start.1 = (f32[1,16,8,16,128]{4,3,2,1,0:T(8,128)S(1)}, f32[1,16,8,16,128]{4,3,2,1,0:T(8,128)}, u32[]{:S(2)}) copy-start(f32[1,16,8,16,128]{4,3,2,1,0:T(8,128)} %param.8) | copy-start | bytes 3145732
  6.1 1.5 %collective-permute-start = (f32[4,8,8,128]{3,2,1,0:T(8,128)S(1)}, f32[4,8,8,128]{3,2,1,0:T(8,128)S(1)}, u32[]{:S(2)}, u32[]{:S(2)}) collective-permute-start(f32[4,8,8,128]{3,2,1,0:T(8,128)S(1)} %get-tuple-element.18), channel_id=1, source_target_pairs={{0,4},{1,5},{2,6},{3,7},{4,0},{5,1},{6,2},{7,3},{8,12},{9,13},{10,... | collective-permute-start | bytes 393224 | tf_op jit(solution)/shard_map/ppermute | solution.py:458
  6.6 4.6 %collective-permute-start.1 = (f32[20,8,128]{2,1,0:T(8,128)S(1)}, f32[20,8,128]{2,1,0:T(8,128)S(1)}, u32[]{:S(2)}, u32[]{:S(2)}) collective-permute-start(f32[20,8,128]{2,1,0:T(8,128)S(1)} %get-tuple-element.19.g_send), channel_id=1, source_target_pairs={{0,4},{1,5},{2,6},{3,7},{4,0},{5,1},{6,2},{7,3},{8,12},{9,13},{10,... | collective-permute-start | bytes 245768 | tf_op jit(solution)/shard_map/ppermute | solution.py:458
  8.3 5.3 %collective-permute-start.2 = (f32[20,8,128]{2,1,0:T(8,128)S(1)}, f32[20,8,128]{2,1,0:T(8,128)S(1)}, u32[]{:S(2)}, u32[]{:S(2)}) collective-permute-start(f32[20,8,128]{2,1,0:T(8,128)S(1)} %get-tuple-element.22.g_in), channel_id=1, source_target_pairs={{0,8},{1,4},{2,5},{3,6},{4,1},{5,2},{6,3},{7,15},{8,0},{9,12},{10,... | collective-permute-start | bytes 245768 | tf_op jit(solution)/shard_map/ppermute | solution.py:458
  13.6 4.4 %copy-start.6 = (f32[16,16]{1,0:T(8,128)S(1)}, f32[16,16]{1,0:T(8,128)}, u32[]{:S(2)}) copy-start(f32[16,16]{1,0:T(8,128)} %param.11) | copy-start | bytes 3076
  14.4 7.2 %collective-permute-start.3 = (f32[41,8,128]{2,1,0:T(8,128)S(1)}, f32[41,8,128]{2,1,0:T(8,128)S(1)}, u32[]{:S(2)}, u32[]{:S(2)}) collective-permute-start(f32[41,8,128]{2,1,0:T(8,128)S(1)} %get-tuple-element.24), channel_id=1, source_target_pairs={{0,8},{1,9},{2,10},{3,11},{4,12},{5,13},{6,14},{7,15},{8,0},{9,1},... | collective-permute-start | bytes 503816 | tf_op jit(solution)/shard_map/ppermute | solution.py:458
  16.5 9.1 %collective-permute-start.4 = (f32[41,8,128]{2,1,0:T(8,128)S(1)}, f32[41,8,128]{2,1,0:T(8,128)S(1)}, u32[]{:S(2)}, u32[]{:S(2)}) collective-permute-start(f32[41,8,128]{2,1,0:T(8,128)S(1)} %get-tuple-element.25), channel_id=1, source_target_pairs={{0,24},{1,25},{2,26},{3,27},{4,28},{5,29},{6,30},{7,31},{8,16},{9,... | collective-permute-start | bytes 503816 | tf_op jit(solution)/shard_map/ppermute | solution.py:458
  44.0 1.3 %collective-permute-start.5 = (f32[3,8,8,128]{3,2,1,0:T(8,128)S(1)}, f32[3,8,8,128]{3,2,1,0:T(8,128)S(1)}, u32[]{:S(2)}, u32[]{:S(2)}) collective-permute-start(f32[3,8,8,128]{3,2,1,0:T(8,128)S(1)} %get-tuple-element.27), channel_id=1, source_target_pairs={{0,4},{1,5},{2,6},{3,7},{4,0},{5,1},{6,2},{7,3},{8,12},{9,13},{10,... | collective-permute-start | bytes 294920 | tf_op jit(solution)/shard_map/ppermute | solution.py:458

commit v2 on v1

v2 whole, which is shorter than its diff:
```python
import functools
import jax
import jax.numpy as jnp
from jax import lax
from jax.experimental import pallas as pl
from jax.experimental.pallas import tpu as pltpu
from jax.sharding import PartitionSpec as P

KL = 4
STEPS = 2

time_step = 0.2
viscosity = 0.2
expansion = 0.05
coriolis_base = 0.5
kappa_base = 0.05
kappa_shear = 0.2
react_step = 0.25
water_absorb = 0.1
pigment_absorb = 0.6
heat_gain = 1.0

EXTRA = 4
WIN = 4


def up(x):
    return pltpu.roll(x, 1, x.ndim - 2)


def down(x):
    return pltpu.roll(x, x.shape[-2] - 1, x.ndim - 2)


def lanes_of(shape):
    return lax.broadcasted_iota(jnp.int32, shape, len(shape) - 1)


def levels_of(shape):
    return lax.broadcasted_iota(jnp.int32, shape, len(shape) - 2)


def window(x, lat, into):
    lon = x.shape[1]
    lane = lanes_of(x.shape)
    base = WIN * (lat + 1)
    moved = pltpu.roll(x, (base + 2) % lon, 1)
    return jnp.where((lane >= base) & (lane < base + WIN), moved, into)


def place():
    row = lax.axis_index("row")
    return (row % 2, row // 2, lax.axis_index("col"))


def pack_kernel(surface, tracers_in, mine, other, g_send, g_other, turned, tracers, sem):
    _, lat_dev, lon_dev = surface.shape
    ntr, nz, lat_blk, lon = tracers.shape
    half, _, _ = place()
    first = half == 0
    big = [
        pltpu.make_async_copy(tracers_in.at[pl.ds(n, GROUP)], tracers.at[pl.ds(n, GROUP)], sem.at[n // GROUP])
        for n in range(0, ntr, GROUP)
    ]
    for copy in big:
        copy.start()
    zero = jnp.zeros((nz, lon), jnp.float32)
    level = levels_of((nz, lon_dev))
    own = [zero] * EXTRA
    far = [zero] * EXTRA
    for t in range(lat_dev):
        depth = jnp.broadcast_to(surface[3 * nz, t : t + 1, :], (nz, lon_dev))
        light = jnp.broadcast_to(surface[3 * nz + 1, t : t + 1, :], (nz, lon_dev))
        wet = (level.astype(jnp.float32) < depth).astype(jnp.float32)
        aux = jnp.where(level == 0, depth, jnp.where(level == 1, light, 0.0))
        for f, tile in enumerate([surface[f * nz : (f + 1) * nz, t, :] * wet for f in range(3)] + [aux]):
            low, high = (tile[:, :lon], tile[:, lon:])
            a, b = (jnp.where(first, low, high), jnp.where(first, high, low))
            mine[f, t] = a
            other[f, t] = b
            own[f] = window(a, t, own[f])
            far[f] = window(b, t, far[f])
    shift = half * (WIN * lat_dev)
    for f in range(EXTRA):
        g_send[ntr + f] = pltpu.roll(own[f], shift, 1)
        g_other[f] = pltpu.roll(far[f], shift, 1)
    for i, copy in enumerate(big):
        copy.wait()
        g = [zero] * GROUP
        for t in range(lat_blk):
            for k in range(GROUP):
                x = tracers[i * GROUP + k, :, t, :]
                turned[i * GROUP + k, t] = x
                g[k] = window(x, t, g[k])
        for k in range(GROUP):
            g_send[i * GROUP + k] = g[k]


def in_half(shape, half, lat_dev):
    lane = lanes_of(shape)
    base = WIN * (lat_dev * half + 1)
    return (lane >= base) & (lane < base + WIN * lat_dev)


def join_kernel(mine, got, g_send, ocean, g_own):
    _, lat_dev, nz, lon = mine.shape
    ntr = g_send.shape[0] - EXTRA
    half, _, _ = place()
    own_lanes = in_half((nz, lon), half, lat_dev)
    zero = jnp.zeros((nz, lon), jnp.float32)
    g_own[:ntr] = g_send[:ntr]
    shift = (1 - half) * (WIN * lat_dev)
    for f in range(EXTRA):
        g = zero
        for t in range(lat_dev):
            ocean[f, half * lat_dev + t] = mine[f, t]
            ocean[f, (1 - half) * lat_dev + t] = got[f, t]
            g = window(got[f, t], t, g)
        g_own[ntr + f] = jnp.where(own_lanes, g_send[ntr + f], pltpu.roll(g, shift, 1))


def edge_kernel(turned, ocean, g_partner, g_other, g_outer, z, to_a, to_b):
    ntr, lat_blk, nz, lon = turned.shape
    nf = ntr + EXTRA
    half, chip, column = place()
    n_col = lax.axis_size("col")
    tile = (nz, lon)
    own_lanes = in_half(tile, half, lat_blk // 2)
    west = lanes_of(tile) % WIN < 2
    outer_ok = jnp.where(half == 0, column > 0, column < n_col - 1)
    even = chip % 2 == 0
    lane = lanes_of(tile)
    low_corner = jnp.zeros(tile, jnp.float32)
    high_corner = low_corner
    for f in range(nf):
        partner = g_partner[f]
        if f >= ntr:
            partner = jnp.where(own_lanes, g_other[f - ntr], partner)
        outer = jnp.where(outer_ok, g_outer[f], 0.0)
        from_partner = (west.astype(jnp.int32) == half)
        cols = jnp.where(from_partner, partner, outer)
        z[f] = cols
        at = (lane >= WIN * f) & (lane < WIN * f + WIN)
        low_corner = jnp.where(at, pltpu.roll(cols, (WIN * f - WIN) % lon, 1), low_corner)
        high_corner = jnp.where(at, pltpu.roll(cols, (WIN * f - WIN * lat_blk) % lon, 1), high_corner)

    def fill(out, high):
        start = lat_blk - 2 if high else 0
        for i in range(2):
            for n in range(ntr):
                out[2 * n + i] = turned[n, start + i]
            for f in range(EXTRA):
                out[2 * (ntr + f) + i] = ocean[f, start + i]
        out[2 * nf] = high_corner if high else low_corner

    @pl.when(even)
    def _():
        fill(to_a, True)
        fill(to_b, False)

    @pl.when(jnp.logical_not(even))
    def _():
        fill(to_a, False)
        fill(to_b, True)


def kappa_of(u, v):
    du, dv = (u - down(u), v - down(v))
    sq = jnp.where(levels_of(u.shape) < u.shape[-2] - 1, du * du + dv * dv, 0.0)
    return kappa_base + kappa_shear * sq / (1.0 + sq)


def sum_above(x):
    level = levels_of(x.shape)
    k = 1
    while k < x.shape[-2]:
        x = x + jnp.where(level >= k, pltpu.roll(x, k, x.ndim - 2), 0.0)
        k *= 2
    return x


def sum_below(x):
    level, nz = (levels_of(x.shape), x.shape[-2])
    k = 1
    while k < nz:
        x = x + jnp.where(level < nz - k, pltpu.roll(x, nz - k, x.ndim - 2), 0.0)
        k *= 2
    return x


def pressure_of(heat):
    return -expansion * sum_above(heat)


def wet_of(aux):
    depth = jnp.broadcast_to(aux[..., 0:1, :], aux.shape)
    return (levels_of(aux.shape).astype(jnp.float32) < depth).astype(jnp.float32)


def light_of(aux):
    return jnp.broadcast_to(aux[..., 1:2, :], aux.shape)


def dynamics(u, v, wet, kap, prs, coriolis):
    um, ue, uw, un, us = u
    vm, ve, vw, vn, vs = v
    wm, we, ww, wn, ws = wet
    km, ke, kw, kn, ks = kap
    _, pe, pw, pn, ps = prs
    level, nz = (levels_of(um.shape), um.shape[-2])
    oe, ow, on, os_ = (wm * we, wm * ww, wm * wn, wm * ws)
    fe, fw, fn, fs = (0.5 * (um + ue) * oe, 0.5 * (um + uw) * ow, 0.5 * (vm + vn) * on, 0.5 * (vm + vs) * os_)
    ce, cw, cn, cs = (0.5 * (km + ke) * oe, 0.5 * (km + kw) * ow, 0.5 * (km + kn) * on, 0.5 * (km + ks) * os_)
    div = fe - fw + fn - fs
    total = sum_below(div)
    w_top = jnp.where(level >= 1, -total, 0.0)
    w_bot = jnp.where(level < nz - 1, -down(total), 0.0)
    weights = (
        wm * (1.0 - time_step * (ce + cw + cn + cs + 0.5 * (div + w_top - w_bot))),
        time_step * (ce - 0.5 * fe),
        time_step * (cw + 0.5 * fw),
        time_step * (cn - 0.5 * fn),
        time_step * (cs + 0.5 * fs),
        (-0.5 * time_step) * wm * w_top,
        (0.5 * time_step) * wm * w_bot,
    )
    lap_u = oe * (ue - um) + ow * (uw - um) + on * (un - um) + os_ * (us - um)
    lap_v = oe * (ve - vm) + ow * (vw - vm) + on * (vn - vm) + os_ * (vs - vm)
    new_u = wm * (um + time_step * (coriolis * vm - 0.5 * (pe - pw) + viscosity * lap_u))
    new_v = wm * (vm + time_step * (-coriolis * um - 0.5 * (pn - ps) + viscosity * lap_v))
    return (new_u, new_v, weights)


def transport(weights, x, east, west, north, south):
    a0, ae, aw, an, as_, at, ab = weights
    return (a0 * x + ae * east) + (aw * west + an * north) + (as_ * south + at * up(x)) + ab * down(x)


def saturated(x):
    return x * lax.rsqrt(1.0 + x * x)


def absorbed(pigment):
    level = levels_of(pigment.shape)
    sq = pigment * pigment
    depth = water_absorb + pigment_absorb * (sq / (1.0 + sq))
    above = jnp.where(level >= 1, up(depth), 0.0)
    k = 1
    while k < KL:
        above = above + jnp.where(level >= k, pltpu.roll(above, k, above.ndim - 2), 0.0)
        k *= 2
    return jnp.where(level < KL, jnp.exp(-above) * (1.0 - jnp.exp(-depth)), 0.0)


def two_parts(x):
    high = x.astype(jnp.bfloat16)
    return (high, (x - high.astype(jnp.float32)).astype(jnp.bfloat16))


def mix_matrix(mix):
    high, low = two_parts(mix)
    top = jnp.concatenate([high, high], axis=1)
    return jnp.concatenate([top, jnp.concatenate([low, jnp.zeros_like(low)], axis=1)], axis=0)


def beside(z, r, lon):
    return pltpu.roll(z, lon - 2 - WIN * (r - 1), z.ndim - 1)


def sides(x, edge):
    lane, lon = (lanes_of(x.shape), x.shape[-1])
    west = pltpu.roll(jnp.where(lane == lon - 1, edge, x), 1, x.ndim - 1)
    east = pltpu.roll(jnp.where(lane == 0, edge, x), lon - 1, x.ndim - 1)
    return (east, west)


def around_rows(m, f, z, r, count):
    x = m[f, pl.ds(r, count)]
    edge = jnp.stack([beside(z, r + i, x.shape[-1]) for i in range(count)])
    return (x, *sides(x, edge), m[f, pl.ds(r + 1, count)], m[f, pl.ds(r - 1, count)])


def around_columns(x, own):
    lane, lon = (lanes_of(x.shape), x.shape[-1])
    west = pltpu.roll(jnp.where(lane % WIN == 0, x, own), 1, x.ndim - 1)
    east = pltpu.roll(jnp.where(lane % WIN == WIN - 1, x, own), lon - 1, x.ndim - 1)
    return (x, east, west, pltpu.roll(x, lon - WIN, x.ndim - 1), pltpu.roll(x, WIN, x.ndim - 1))


KAP, PRS, WET = (0, 1, 2)
GROUP = 4


def chunks(start, stop, most, body):
    count = max(k for k in range(1, most + 1) if (stop - start) % k == 0)

    def one(i, _):
        body(start + i * count, count)
        return 0

    lax.fori_loop(0, (stop - start) // count, one, 0)


def derive_rows(m, dv, ntr, start, stop):
    def body(r, count):
        at = pl.ds(r, count)
        dv[KAP, at] = kappa_of(m[ntr, at], m[ntr + 1, at])
        dv[PRS, at] = pressure_of(m[ntr + 2, at])

    chunks(start, stop, 10, body)


def derive_columns(z, zd, ntr):
    zd[KAP] = kappa_of(z[ntr], z[ntr + 1])
    zd[PRS] = pressure_of(z[ntr + 2])


def ocean_rows(m, dv, z, zd, wts, new, coriolis_at, ntr, start, stop):
    def body(r, count):
        at = pl.ds(r, count)
        lat = lax.broadcasted_iota(jnp.int32, (count, *m.shape[2:]), 0) + (r - 2)
        new_u, new_v, weights = dynamics(
            around_rows(m, ntr, z[ntr], r, count),
            around_rows(m, ntr + 1, z[ntr + 1], r, count),
            around_rows(dv, WET, zd[WET], r, count),
            around_rows(dv, KAP, zd[KAP], r, count),
            around_rows(dv, PRS, zd[PRS], r, count),
            coriolis_at(lat),
        )
        new[ntr, at] = new_u
        new[ntr + 1, at] = new_v
        for i, w in enumerate(weights):
            wts[i, at] = w

    chunks(start, stop, 9, body)


def tracer_rows(m, z, wts, new, sat, ntr, start, stop):
    nz, lon = m.shape[2:]
    half = ntr * nz

    def row(r):
        weights = [wts[i, r] for i in range(7)]
        for n in range(0, ntr, GROUP):
            x = m[n : n + GROUP, r]
            edge = beside(z[n : n + GROUP], r, lon)
            moved = transport(weights, x, *sides(x, edge), m[n : n + GROUP, r + 1], m[n : n + GROUP, r - 1])
            new[n : n + GROUP, r] = moved
            high, low = two_parts(saturated(moved).reshape(GROUP * nz, lon))
            sat[r, n * nz : (n + GROUP) * nz, :] = high
            sat[r, half + n * nz : half + (n + GROUP) * nz, :] = low
        h = ntr + 2
        x = m[h, r]
        new[h, r] = transport(weights, x, *sides(x, beside(z[h], r, lon)), m[h, r + 1], m[h, r - 1])

    def body(r, count):
        for i in range(count):
            row(r + i)

    chunks(start, stop, 3, body)


def react_rows(dv, mix, new, sat, ntr, start, stop):
    nz, lon = new.shape[2:]
    half = ntr * nz

    def body(r, count):
        both = jnp.concatenate([sat[r + i] for i in range(count)], axis=1)
        res = jnp.dot(mix[...], both, preferred_element_type=jnp.float32)
        res = res[:half] + res[half:]
        for i in range(count):
            gain = react_step * dv[WET, r + i]
            for n in range(ntr):
                new[n, r + i] = new[n, r + i] + gain * res[n * nz : (n + 1) * nz, i * lon : (i + 1) * lon]

    chunks(start, stop, 18, body)


def light_rows(m, dv, new, ntr, start, stop):
    def body(r, count):
        at = pl.ds(r, count)
        new[ntr + 2, at] += heat_gain * light_of(m[ntr + 3, at]) * dv[WET, at] * absorbed(new[0, at])

    chunks(start, stop, 9, body)


def column_step(z0, g0, zd, gd, z1, mix, coriolis, ntr):
    nz, lon = z0.shape[1:]
    half = ntr * nz
    wet = zd[WET]
    new_u, new_v, weights = dynamics(
        around_columns(z0[ntr], g0[ntr]),
        around_columns(z0[ntr + 1], g0[ntr + 1]),
        around_columns(wet, gd[WET]),
        around_columns(zd[KAP], gd[KAP]),
        around_columns(zd[PRS], gd[PRS]),
        coriolis,
    )
    moved = transport(weights, *around_columns(z0[:ntr], g0[:ntr]))
    high, low = two_parts(saturated(moved).reshape(half, lon))
    res = jnp.dot(mix[...], jnp.concatenate([high, low], axis=0), preferred_element_type=jnp.float32)
    done = moved + (react_step * wet) * (res[:half] + res[half:]).reshape(ntr, nz, lon)
    z1[:ntr] = done
    z1[ntr] = new_u
    z1[ntr + 1] = new_v
    heat = transport(weights, *around_columns(z0[ntr + 2], g0[ntr + 2]))
    z1[ntr + 2] = heat + heat_gain * light_of(z0[ntr + 3]) * wet * absorbed(done[0])


def fill_ocean(ocean, got, m0, dv, ntr):
    lat_blk = ocean.shape[1]
    rows = lat_blk + 4
    for f in range(EXTRA):
        for i in range(2):
            m0[ntr + f, i] = got(False, 2 * (ntr + f) + i)
            m0[ntr + f, lat_blk + 2 + i] = got(True, 2 * (ntr + f) + i)
        m0[ntr + f, 2 : lat_blk + 2] = ocean[f]

    def wets(r, count):
        at = pl.ds(r, count)
        dv[WET, at] = wet_of(m0[ntr + 3, at])

    chunks(0, rows, 10, wets)


def fill_tracers(turned, got, m0, dv):
    ntr, lat_blk, _, _ = turned.shape
    for i in range(2):
        for n in range(ntr):
            m0[n, i] = got(False, 2 * n + i) * dv[WET, i]
            m0[n, lat_blk + 2 + i] = got(True, 2 * n + i) * dv[WET, lat_blk + 2 + i]

    def some(t, _):
        wet = dv[WET, t + 2]
        for n in range(ntr):
            m0[n, t + 2] = turned[n, t] * wet
        return 0

    lax.fori_loop(0, lat_blk, some, 0)


def fill_columns(z_in, g_in, got, z0, g0, zd, gd, ntr, lat_blk):
    nf = ntr + EXTRA
    nz, lon = z_in.shape[1:]
    lane = lanes_of((nz, lon))
    low_corner, high_corner = (got(False, 2 * nf), got(True, 2 * nf))
    at_low, at_high = (lane < WIN, (lane >= WIN * (lat_blk + 1)) & (lane < WIN * (lat_blk + 2)))
    for f in reversed(range(nf)):
        cols = jnp.where(at_low, pltpu.roll(low_corner, (-WIN * f) % lon, 1), z_in[f])
        cols = jnp.where(at_high, pltpu.roll(high_corner, (WIN * (lat_blk + 1) - WIN * f) % lon, 1), cols)
        own = g_in[f]
        if f == nf - 1:
            wet_z, wet_g = (wet_of(cols), wet_of(own))
            zd[WET] = wet_z
            gd[WET] = wet_g
        if f < ntr:
            cols, own = (cols * wet_z, own * wet_g)
        z0[f] = cols
        g0[f] = own


def write_out(m, out, ntr):
    lat_blk = out.shape[2]

    def some(t, _):
        for n in range(ntr):
            out[n, :, t, :] = m[n, t + 2]
        return 0

    lax.fori_loop(0, lat_blk, some, 0)


def steps_kernel(turned, ocean, z_in, g_in, got_a, got_b, rate_mix, out, keep, send, m0, m1, dv, wts, sat, mix, z0, z1, g0, zd, gd):
    ntr, lat_blk, nz, lon = turned.shape
    place_half, chip, _ = place()
    chips = lax.axis_size("row") // 2
    even = chip % 2 == 0
    south_ok, north_ok = (chip > 0, chip < chips - 1)
    rows = lat_blk + 4

    def got(high, index):
        a, b = (got_a[index], got_b[index])
        picked = jnp.where(even, a, b) if high else jnp.where(even, b, a)
        return jnp.where(north_ok if high else south_ok, picked, 0.0)

    def coriolis_at(lat):
        latitude = (lat + chip * lat_blk).astype(jnp.float32)
        return coriolis_base * (2.0 * (latitude + 0.5) / (chips * lat_blk) - 1.0)

    mix[...] = mix_matrix(rate_mix[...])
    fill_ocean(ocean, got, m0, dv, ntr)
    fill_tracers(turned, got, m0, dv)
    fill_columns(z_in, g_in, got, z0, g0, zd, gd, ntr, lat_blk)
    derive_rows(m0, dv, ntr, 0, rows)
    derive_columns(z0, zd, ntr)
    derive_columns(g0, gd, ntr)
    column_step(z0, g0, zd, gd, z1, mix, coriolis_at(lanes_of((nz, lon)) // WIN - 1), ntr)
    ocean_rows(m0, dv, z0, zd, wts, m1, coriolis_at, ntr, 1, rows - 1)
    tracer_rows(m0, z0, wts, m1, sat, ntr, 1, rows - 1)
    react_rows(dv, mix, m1, sat, ntr, 1, rows - 1)
    light_rows(m0, dv, m1, ntr, 1, rows - 1)
    derive_rows(m1, dv, ntr, 1, rows - 1)
    derive_columns(z1, zd, ntr)
    ocean_rows(m1, dv, z1, zd, wts, m0, coriolis_at, ntr, 2, rows - 2)
    tracer_rows(m1, z1, wts, m0, sat, ntr, 2, rows - 2)
    react_rows(dv, mix, m0, sat, ntr, 2, rows - 2)
    light_rows(m0, dv, m0, ntr, 2, rows - 2)
    write_out(m0, out, ntr)
    half = lat_blk // 2
    for f in range(3):
        keep[f] = m0[ntr + f, pl.ds(2 + place_half * half, half)]
        send[f] = m0[ntr + f, pl.ds(2 + (1 - place_half) * half, half)]


def unpack_kernel(keep, got, flow, temp):
    _, lat_dev, nz, lon = keep.shape
    first = place()[0] == 0
    for t in range(lat_dev):
        for f in range(3):
            a, b = (keep[f, t], got[f, t])
            low, high = (jnp.where(first, a, b), jnp.where(first, b, a))
            if f < 2:
                flow[f, :, t, :lon] = low
                flow[f, :, t, lon:] = high
            else:
                temp[:, t, :lon] = low
                temp[:, t, lon:] = high


def call(kernel, outs, *args, scratch=(), held=None):
    vmem = pl.BlockSpec(memory_space=pltpu.VMEM)
    held = held or [True] * len(args)
    return pl.pallas_call(
        kernel,
        out_shape=[jax.ShapeDtypeStruct(s, jnp.float32) for s in outs],
        in_specs=[vmem if h else pl.BlockSpec(memory_space=pl.ANY) for h in held],
        out_specs=[vmem] * len(outs),
        scratch_shapes=[pltpu.VMEM(s, jnp.float32) if isinstance(s, tuple) else s for s in scratch],
        compiler_params=pltpu.CompilerParams(vmem_limit_bytes=(40 if all(held) else 52) * 2**20),
    )(*args)


def both_ways(pairs):
    return sorted(pairs + [(b, a) for a, b in pairs])


def exchanges(n_row, n_col):
    chips = n_row // 2

    def dev(p, h, c):
        return (2 * p + h) * n_col + c

    partner = [(dev(p, 0, c), dev(p, 1, c)) for p in range(chips) for c in range(n_col)]
    outer = [(dev(p, 1, c), dev(p, 0, c + 1)) for p in range(chips) for c in range(n_col - 1)]
    for p in range(0, chips - 1, 2):
        outer += [(dev(p, 0, 0), dev(p + 1, 0, 0)), (dev(p, 1, n_col - 1), dev(p + 1, 1, n_col - 1))]
    lat_a = [(dev(p, h, c), dev(p + 1, h, c)) for p in range(0, chips - 1, 2) for h in (0, 1) for c in range(n_col)]
    lat_b = [(dev(p, h, c), dev(p + 1, h, c)) for p in range(1, chips - 1, 2) for h in (0, 1) for c in range(n_col)]
    if chips % 2 == 0 and chips > 2:
        lat_b += [(dev(0, h, c), dev(chips - 1, h, c)) for h in (0, 1) for c in range(n_col)]
    return [both_ways(x) for x in (partner, outer, lat_a, lat_b)]


def on_device(n_row, n_col, flow, temp, tracers, bottom, sunlight, rates):
    nz, lat_dev, lon_dev = temp.shape
    _, ntr, _, lat_blk, lon = tracers.shape
    nf = ntr + EXTRA
    partner, outer, lat_a, lat_b = exchanges(n_row, n_col)

    def swap(x, pairs):
        return lax.ppermute(x, ("row", "col"), pairs)

    block = tracers[0]
    parts = [flow.reshape(-1, lat_dev, lon_dev), temp, bottom[None], sunlight[None]]
    total = sum(part.shape[0] for part in parts)
    surface, start = (0.0, 0)
    for part in parts:
        count = part.shape[0]
        surface = surface + jnp.pad(part, ((start, total - start - count), (0, 0), (0, 0))).astype(jnp.float32)
        start += count
    mix = jnp.kron(rates, jnp.eye(nz, dtype=jnp.float32))
    half_shape = (EXTRA, lat_dev, nz, lon)
    mine, other, g_send, g_other, turned = call(
        pack_kernel,
        [half_shape, half_shape, (nf, nz, lon), (EXTRA, nz, lon), (ntr, lat_blk, nz, lon)],
        surface,
        block,
        scratch=[block.shape, pltpu.SemaphoreType.DMA((ntr // GROUP,))],
        held=[True, False],
    )
    got, g_partner = swap((other, g_send), partner)
    ocean, g_own = call(join_kernel, [(EXTRA, lat_blk, nz, lon), (nf, nz, lon)], mine, got, g_send)
    g_outer = swap(g_own, outer)
    edge_shape = (2 * nf + 1, nz, lon)
    z, to_a, to_b = call(
        edge_kernel, [(nf, nz, lon), edge_shape, edge_shape], turned, ocean, g_partner, g_other, g_outer
    )
    got_a, got_b = (swap(to_a, lat_a), swap(to_b, lat_b))
    rows = lat_blk + 4
    cols = (nf, nz, lon)
    third = (3, lat_dev, nz, lon)
    out, keep, send = call(
        steps_kernel,
        [(ntr, nz, lat_blk, lon), third, third],
        turned,
        ocean,
        z,
        g_own,
        got_a,
        got_b,
        mix,
        scratch=[
            (nf, rows, nz, lon),
            (nf, rows, nz, lon),
            (3, rows, nz, lon),
            (7, rows, nz, lon),
            pltpu.VMEM((rows, 2 * ntr * nz, lon), jnp.bfloat16),
            pltpu.VMEM((2 * ntr * nz, 2 * ntr * nz), jnp.bfloat16),
            cols,
            cols,
            cols,
            (3, nz, lon),
            (3, nz, lon),
        ],
    )
    flow_out, temp_out = call(
        unpack_kernel, [(2, nz, lat_dev, lon_dev), (nz, lat_dev, lon_dev)], keep, swap(send, partner)
    )
    return (flow_out, temp_out, out[None])


def solution(mesh):
    in_specs = (
        P(None, None, "row", "col"),
        P(None, "row", "col"),
        P("row", None, None, None, "col"),
        P("row", "col"),
        P("row", "col"),
        P(),
    )
    out_specs = (
        P(None, None, "row", "col"),
        P(None, "row", "col"),
        P("row", None, None, None, "col"),
    )
    return jax.shard_map(
        functools.partial(on_device, mesh.shape["row"], mesh.shape["col"]),
        mesh=mesh,
        in_specs=in_specs,
        out_specs=out_specs,
        check_vma=False,
    )
```

time: 46.9 us -> 33 us (0.70)
  Pallas kernels: 23.8 us -> 11.8 us
  local copies, waits for them, and re-layouts: 3.41 us -> 0.5 us
  other arithmetic: 0.14 us -> 1.12 us
    pallas_call x5, Pallas kernels: 23.8 us -> 11.8 us  [call(): pl.pallas_call(kernel, out_shape=[jax.ShapeDtypeStruct(s, jnp.float32) fo...]
    unnamed x14 -> x2, local copies, waits for them, and re-layouts: 2.83 us -> 0.01 us
    add x0 -> x1, other arithmetic: none -> 0.99 us  [on_device(): surface + jnp.pad(part, ((start, total - start - count), (0, 0), (0, 0)))...]
  transfers between devices with their start and end apart: 6 -> 6, of which waited for: 5 -> 5; matrix products, arithmetic and copies ran while one was open for 1% -> 2% of each run, Pallas kernels for 2% -> 1%
where the time goes in v2:
time: 33 us; the launch traced here: 32.8 us
  Pallas kernels  11.8 us (36%)
  waiting for transfers between devices  11.6 us (35%)
  starting transfers between devices  7.03 us (21%)
  other arithmetic  1.12 us (3%)
  between operations  0.67 us (2%)
  local copies, waits for them, and re-layouts  0.5 us (2%)
    pallas_call x5, Pallas kernels, call(): pl.pallas_call(kernel, out_shape=[jax.ShapeDtypeStruct(s, jnp.float32) fo...  11.8 us
    ppermute x6, waiting for transfers between devices, swap(): return lax.ppermute(x, ('row', 'col'), pairs)  11.6 us
    ppermute x6, starting transfers between devices, swap(): return lax.ppermute(x, ('row', 'col'), pairs)  7.03 us
    add x1, other arithmetic, on_device(): surface + jnp.pad(part, ((start, total - start - count), (0, 0), (0, 0)))...  0.99 us
  transfers between devices with their start and end apart: 6, of which 5 were waited for; matrix products, arithmetic and copies ran while one was open for 2% of the time, Pallas kernels for 1%

profile of v2, /device:TPU:0, one launch (start us, length us, event | category | flops | bytes accessed | tf_op | source)
XLA Modules:
  0.0 32.8 jit_solution(11097482105771835667)
XLA Ops:
  0.6 1.0 %pad_add_fusion.surface = f32[26,8,256]{2,1,0:T(8,128)S(1)} fusion(f32[1,8,256]{2,1,0:T(8,128)} %bitcast.9, s32[1,8,256]{2,1,0:T(8,128)} %bitcast.10, f32[8,8,256]{2,1,0:T(8,128)} %param.7, f32[16,8,256]{2,1,0:T(8,128)} %bitcast.8), kind=kLoop, calls=%fused_computation.1 | loop fusion | flops 212992 | bytes 425984 | tf_op jit(solution)/shard_map/add | solution.py:579
  1.6 2.1 %shard_map.85 = (f32[4,8,8,128]{3,2,1,0:T(8,128)S(1)}, f32[4,8,8,128]{3,2,1,0:T(8,128)S(1)}, f32[20,8,128]{2,1,0:T(8,128)S(1)}, f32[4,8,128]{2,1,0:T(8,128)S(1)}, f32[16,16,8,128]{3,2,1,0:T(8,128)S(1)}) custom-call(f32[26,8,256]{2,1,0:T(8,128)S(1)} %pad_add_fusion.surface, f32[16,8,16,128]{3,2,1,0:T(8,128)} %bitcast.7), custom_call_target="tpu_custom_call" | custom-call | tf_op jit(solution)/shard_map/pallas_call | solution.py:533
  3.7 0.5 %collective-permute-start = (f32[4,8,8,128]{3,2,1,0:T(8,128)S(1)}, f32[4,8,8,128]{3,2,1,0:T(8,128)S(1)}, u32[]{:S(2)}, u32[]{:S(2)}) collective-permute-start(f32[4,8,8,128]{3,2,1,0:T(8,128)S(1)} %get-tuple-element.20), channel_id=1, source_target_pairs={{0,4},{1,5},{2,6},{3,7},{4,0},{5,1},{6,2},{7,3},{8,12},{9,13},{10,... | collective-permute-start | bytes 393224 | tf_op jit(solution)/shard_map/ppermute | solution.py:571
  4.2 0.1 collective-permute-start.1
  4.3 0.9 %collective-permute-done.got = f32[4,8,8,128]{3,2,1,0:T(8,128)S(1)} collective-permute-done((f32[4,8,8,128]{3,2,1,0:T(8,128)S(1)}, f32[4,8,8,128]{3,2,1,0:T(8,128)S(1)}, u32[]{:S(2)}, u32[]{:S(2)}) %collective-permute-start) | collective-permute-done | bytes 131104 | tf_op jit(solution)/shard_map/ppermute | solution.py:571
  5.2 0.2 shard_map.86
  5.4 2.9 %collective-permute-start.2 = (f32[20,8,128]{2,1,0:T(8,128)S(1)}, f32[20,8,128]{2,1,0:T(8,128)S(1)}, u32[]{:S(2)}, u32[]{:S(2)}) collective-permute-start(f32[20,8,128]{2,1,0:T(8,128)S(1)} %get-tuple-element.24.g_in), channel_id=1, source_target_pairs={{0,8},{1,4},{2,5},{3,6},{4,1},{5,2},{6,3},{7,15},{8,0},{9,12},{10,... | collective-permute-start | bytes 245768 | tf_op jit(solution)/shard_map/ppermute | solution.py:571
  8.2 0.0 collective-permute-done.1.g_partner
  8.2 2.4 %collective-permute-done.2.g_outer = f32[20,8,128]{2,1,0:T(8,128)S(1)} collective-permute-done((f32[20,8,128]{2,1,0:T(8,128)S(1)}, f32[20,8,128]{2,1,0:T(8,128)S(1)}, u32[]{:S(2)}, u32[]{:S(2)}) %collective-permute-start.2) | collective-permute-done | bytes 81952 | tf_op jit(solution)/shard_map/ppermute | solution.py:571
  10.6 0.0 copy-start
  10.6 0.1 shard_map.87
  10.8 2.1 %collective-permute-start.3 = (f32[41,8,128]{2,1,0:T(8,128)S(1)}, f32[41,8,128]{2,1,0:T(8,128)S(1)}, u32[]{:S(2)}, u32[]{:S(2)}) collective-permute-start(f32[41,8,128]{2,1,0:T(8,128)S(1)} %get-tuple-element.26), channel_id=1, source_target_pairs={{0,8},{1,9},{2,10},{3,11},{4,12},{5,13},{6,14},{7,15},{8,0},{9,1},... | collective-permute-start | bytes 503816 | tf_op jit(solution)/shard_map/ppermute | solution.py:571
  12.9 1.5 %collective-permute-start.4 = (f32[41,8,128]{2,1,0:T(8,128)S(1)}, f32[41,8,128]{2,1,0:T(8,128)S(1)}, u32[]{:S(2)}, u32[]{:S(2)}) collective-permute-start(f32[41,8,128]{2,1,0:T(8,128)S(1)} %get-tuple-element.27), channel_id=1, source_target_pairs={{0,24},{1,25},{2,26},{3,27},{4,28},{5,29},{6,30},{7,31},{8,16},{9,... | collective-permute-start | bytes 503816 | tf_op jit(solution)/shard_map/ppermute | solution.py:571
  14.4 0.0 copy-done
  14.4 0.1 broadcast_multiply_fusion
  14.5 0.5 %mul.27.rate_mix = f32[128,128]{1,0:T(8,128)S(1)} reshape(f32[16,8,16,8]{3,2,1,0:T(8,128)S(1)} %broadcast_multiply_fusion) | data formatting | bytes 131072 | tf_op jit(solution)/shard_map/jit(kron)/mul | solution.py:581
  15.0 3.0 %collective-permute-done.3.got_a = f32[41,8,128]{2,1,0:T(8,128)S(1)} collective-permute-done((f32[41,8,128]{2,1,0:T(8,128)S(1)}, f32[41,8,128]{2,1,0:T(8,128)S(1)}, u32[]{:S(2)}, u32[]{:S(2)}) %collective-permute-start.3) | collective-permute-done | bytes 167968 | tf_op jit(solution)/shard_map/ppermute | solution.py:571
  18.0 4.0 %collective-permute-done.4.got_b = f32[41,8,128]{2,1,0:T(8,128)S(1)} collective-permute-done((f32[41,8,128]{2,1,0:T(8,128)S(1)}, f32[41,8,128]{2,1,0:T(8,128)S(1)}, u32[]{:S(2)}, u32[]{:S(2)}) %collective-permute-start.4) | collective-permute-done | bytes 167968 | tf_op jit(solution)/shard_map/ppermute | solution.py:571
  22.0 8.7 %shard_map.88 = (f32[16,8,16,128]{3,2,1,0:T(8,128)}, f32[3,8,8,128]{3,2,1,0:T(8,128)S(1)}, f32[3,8,8,128]{3,2,1,0:T(8,128)S(1)}) custom-call(f32[16,16,8,128]{3,2,1,0:T(8,128)S(1)} %get-tuple-element.18.turned, f32[4,16,8,128]{3,2,1,0:T(8,128)S(1)} %get-tuple-element.22.ocean, f32[20,8,128]{2,1,0:T(8,128)S(1)} %get-tuple-element.25.z_in, ...), custom_call_target="tpu_custom_call" | custom-call | tf_op jit(solution)/shard_map/pallas_call | solution.py:533
  30.7 0.0 collective-permute-start.5
  30.7 1.3 %collective-permute-done.5.got = f32[3,8,8,128]{3,2,1,0:T(8,128)S(1)} collective-permute-done((f32[3,8,8,128]{3,2,1,0:T(8,128)S(1)}, f32[3,8,8,128]{3,2,1,0:T(8,128)S(1)}, u32[]{:S(2)}, u32[]{:S(2)}) %collective-permute-start.5) | collective-permute-done | bytes 98336 | tf_op jit(solution)/shard_map/ppermute | solution.py:571
  32.0 0.8 %shard_map.89 = (f32[2,8,8,256]{3,2,1,0:T(8,128)}, f32[8,8,256]{2,1,0:T(8,128)}) custom-call(f32[3,8,8,128]{3,2,1,0:T(8,128)S(1)} %get-tuple-element.28.keep, f32[3,8,8,128]{3,2,1,0:T(8,128)S(1)} %collective-permute-done.5.got), custom_call_target="tpu_custom_call" | custom-call | tf_op jit(solution)/shard_map/pallas_call | solution.py:533
  (1 shorter events, 0.0 us)
Async XLA Ops:
  3.7 1.5 %collective-permute-start = (f32[4,8,8,128]{3,2,1,0:T(8,128)S(1)}, f32[4,8,8,128]{3,2,1,0:T(8,128)S(1)}, u32[]{:S(2)}, u32[]{:S(2)}) collective-permute-start(f32[4,8,8,128]{3,2,1,0:T(8,128)S(1)} %get-tuple-element.20), channel_id=1, source_target_pairs={{0,4},{1,5},{2,6},{3,7},{4,0},{5,1},{6,2},{7,3},{8,12},{9,13},{10,... | collective-permute-start | bytes 393224 | tf_op jit(solution)/shard_map/ppermute | solution.py:571
  4.2 4.0 %collective-permute-start.1 = (f32[20,8,128]{2,1,0:T(8,128)S(1)}, f32[20,8,128]{2,1,0:T(8,128)S(1)}, u32[]{:S(2)}, u32[]{:S(2)}) collective-permute-start(f32[20,8,128]{2,1,0:T(8,128)S(1)} %get-tuple-element.21.g_send), channel_id=1, source_target_pairs={{0,4},{1,5},{2,6},{3,7},{4,0},{5,1},{6,2},{7,3},{8,12},{9,13},{10,... | collective-permute-start | bytes 245768 | tf_op jit(solution)/shard_map/ppermute | solution.py:571
  5.4 5.3 %collective-permute-start.2 = (f32[20,8,128]{2,1,0:T(8,128)S(1)}, f32[20,8,128]{2,1,0:T(8,128)S(1)}, u32[]{:S(2)}, u32[]{:S(2)}) collective-permute-start(f32[20,8,128]{2,1,0:T(8,128)S(1)} %get-tuple-element.24.g_in), channel_id=1, source_target_pairs={{0,8},{1,4},{2,5},{3,6},{4,1},{5,2},{6,3},{7,15},{8,0},{9,12},{10,... | collective-permute-start | bytes 245768 | tf_op jit(solution)/shard_map/ppermute | solution.py:571
  10.6 3.7 %copy-start = (f32[16,16]{1,0:T(8,128)S(1)}, f32[16,16]{1,0:T(8,128)}, u32[]{:S(2)}) copy-start(f32[16,16]{1,0:T(8,128)} %param.11) | copy-start | bytes 3076
  10.8 7.2 %collective-permute-start.3 = (f32[41,8,128]{2,1,0:T(8,128)S(1)}, f32[41,8,128]{2,1,0:T(8,128)S(1)}, u32[]{:S(2)}, u32[]{:S(2)}) collective-permute-start(f32[41,8,128]{2,1,0:T(8,128)S(1)} %get-tuple-element.26), channel_id=1, source_target_pairs={{0,8},{1,9},{2,10},{3,11},{4,12},{5,13},{6,14},{7,15},{8,0},{9,1},... | collective-permute-start | bytes 503816 | tf_op jit(solution)/shard_map/ppermute | solution.py:571
  12.9 9.1 %collective-permute-start.4 = (f32[41,8,128]{2,1,0:T(8,128)S(1)}, f32[41,8,128]{2,1,0:T(8,128)S(1)}, u32[]{:S(2)}, u32[]{:S(2)}) collective-permute-start(f32[41,8,128]{2,1,0:T(8,128)S(1)} %get-tuple-element.27), channel_id=1, source_target_pairs={{0,24},{1,25},{2,26},{3,27},{4,28},{5,29},{6,30},{7,31},{8,16},{9,... | collective-permute-start | bytes 503816 | tf_op jit(solution)/shard_map/ppermute | solution.py:571
  30.7 1.3 %collective-permute-start.5 = (f32[3,8,8,128]{3,2,1,0:T(8,128)S(1)}, f32[3,8,8,128]{3,2,1,0:T(8,128)S(1)}, u32[]{:S(2)}, u32[]{:S(2)}) collective-permute-start(f32[3,8,8,128]{3,2,1,0:T(8,128)S(1)} %get-tuple-element.29), channel_id=1, source_target_pairs={{0,4},{1,5},{2,6},{3,7},{4,0},{5,1},{6,2},{7,3},{8,12},{9,13},{10,... | collective-permute-start | bytes 294920 | tf_op jit(solution)/shard_map/ppermute | solution.py:571

commit v3 on v2

v3 whole, which is shorter than its diff:
```python
import functools
import jax
import jax.numpy as jnp
from jax import lax
from jax.experimental import pallas as pl
from jax.experimental.pallas import tpu as pltpu
from jax.sharding import PartitionSpec as P

KL = 4
STEPS = 2

time_step = 0.2
viscosity = 0.2
expansion = 0.05
coriolis_base = 0.5
kappa_base = 0.05
kappa_shear = 0.2
react_step = 0.25
water_absorb = 0.1
pigment_absorb = 0.6
heat_gain = 1.0

EXTRA = 4
WIN = 4


def up(x):
    return pltpu.roll(x, 1, x.ndim - 2)


def down(x):
    return pltpu.roll(x, x.shape[-2] - 1, x.ndim - 2)


def lanes_of(shape):
    return lax.broadcasted_iota(jnp.int32, shape, len(shape) - 1)


def levels_of(shape):
    return lax.broadcasted_iota(jnp.int32, shape, len(shape) - 2)


def window(x, lat, into):
    lon = x.shape[1]
    lane = lanes_of(x.shape)
    base = WIN * (lat + 1)
    moved = pltpu.roll(x, (base + 2) % lon, 1)
    return jnp.where((lane >= base) & (lane < base + WIN), moved, into)


def place():
    row = lax.axis_index("row")
    return (row % 2, row // 2, lax.axis_index("col"))


def edge_starts(chip, lat_blk):
    odd = chip % 2
    return ((1 - odd) * (lat_blk - 2), odd * (lat_blk - 2))


def pack_ocean_kernel(surface, mine, to_partner, g_other):
    lat_dev, nz, lon = mine.shape[1:]
    lon_dev = surface.shape[2]
    half, _, _ = place()
    first = half == 0
    zero = jnp.zeros((nz, lon), jnp.float32)
    level = levels_of((nz, lon_dev))
    own = [zero] * EXTRA
    far = [zero] * EXTRA
    for t in range(lat_dev):
        depth = jnp.broadcast_to(surface[3 * nz, t : t + 1, :], (nz, lon_dev))
        light = jnp.broadcast_to(surface[3 * nz + 1, t : t + 1, :], (nz, lon_dev))
        wet = (level.astype(jnp.float32) < depth).astype(jnp.float32)
        aux = jnp.where(level == 0, depth, jnp.where(level == 1, light, 0.0))
        for f, tile in enumerate([surface[f * nz : (f + 1) * nz, t, :] * wet for f in range(3)] + [aux]):
            low, high = (tile[:, :lon], tile[:, lon:])
            a, b = (jnp.where(first, low, high), jnp.where(first, high, low))
            mine[f, t] = a
            to_partner[f * lat_dev + t] = b
            own[f] = window(a, t, own[f])
            far[f] = window(b, t, far[f])
    shift = half * (WIN * lat_dev)
    for f in range(EXTRA):
        to_partner[EXTRA * lat_dev + f] = pltpu.roll(own[f], shift, 1)
        g_other[f] = pltpu.roll(far[f], shift, 1)


def pack_tracers_kernel(tracers_in, turned, g_tracers, tracers, sem):
    ntr, nz, lat_blk, lon = tracers.shape
    copies = [
        pltpu.make_async_copy(tracers_in.at[pl.ds(n, GROUP)], tracers.at[pl.ds(n, GROUP)], sem.at[n // GROUP])
        for n in range(0, ntr, GROUP)
    ]
    for copy in copies:
        copy.start()
    for i, copy in enumerate(copies):
        copy.wait()
        g = [jnp.zeros((nz, lon), jnp.float32)] * GROUP
        for t in range(lat_blk):
            for k in range(GROUP):
                x = tracers[i * GROUP + k, :, t, :]
                turned[i * GROUP + k, t] = x
                g[k] = window(x, t, g[k])
        for k in range(GROUP):
            g_tracers[i * GROUP + k] = g[k]


def in_half(shape, half, lat_dev):
    lane = lanes_of(shape)
    base = WIN * (lat_dev * half + 1)
    return (lane >= base) & (lane < base + WIN * lat_dev)


def join_kernel(mine, got, to_partner, g_tracers, ocean, g_own, to_outer):
    _, lat_dev, nz, lon = mine.shape
    ntr = g_tracers.shape[0]
    nf = ntr + EXTRA
    half, _, _ = place()
    tile = (nz, lon)
    own_lanes = in_half(tile, half, lat_dev)
    shift = (1 - half) * (WIN * lat_dev)
    g_own[:ntr] = g_tracers[...]
    for f in range(EXTRA):
        g = jnp.zeros(tile, jnp.float32)
        for t in range(lat_dev):
            x = got[f * lat_dev + t]
            ocean[f, half * lat_dev + t] = mine[f, t]
            ocean[f, (1 - half) * lat_dev + t] = x
            g = window(x, t, g)
        g_own[ntr + f] = jnp.where(own_lanes, to_partner[EXTRA * lat_dev + f], pltpu.roll(g, shift, 1))
    lane = lanes_of(tile)
    front, near = (lane % WIN < 2, in_half(tile, 0, 2 * lat_dev))
    side = (1 - half) * (lon - 2)
    for i in range(nf // 4):
        a, b, c, d = [pltpu.roll(g_own[4 * i + k], side, 1) for k in range(4)]
        low = jnp.where(front, a, pltpu.roll(b, 2, 1))
        high = jnp.where(front, c, pltpu.roll(d, 2, 1))
        to_outer[i] = jnp.where(near, low, pltpu.roll(high, lon // 2, 1))


def edge_kernel(turned, ocean, g_partner, got, g_other, from_outer, z, to_a, to_b):
    ntr, lat_blk, nz, lon = turned.shape
    nf = ntr + EXTRA
    half, chip, column = place()
    tile = (nz, lon)
    lane = lanes_of(tile)
    own_lanes = in_half(tile, half, lat_blk // 2)
    outer_ok = jnp.where(half == 0, column > 0, column < lax.axis_size("col") - 1)
    from_partner = (lane % WIN < 2).astype(jnp.int32) == half
    outer_lanes = in_half(tile, 0, lat_blk) & outer_ok
    start_a, start_b = edge_starts(chip, lat_blk)
    corner_a = corner_b = jnp.zeros(tile, jnp.float32)
    for f in range(nf):
        if f < ntr:
            partner = g_partner[f]
        else:
            partner = jnp.where(own_lanes, g_other[f - ntr], got[EXTRA * (lat_blk // 2) + f - ntr])
        k = f % 4
        moved = pltpu.roll(from_outer[f // 4], lon + 2 * half - 2 * (k % 2) - lon // 2 * (k // 2), 1)
        cols = jnp.where(from_partner, partner, jnp.where(outer_lanes, moved, 0.0))
        z[f] = cols
        at = (lane >= WIN * f) & (lane < WIN * f + WIN)
        low = pltpu.roll(cols, (WIN * f - WIN) % lon, 1)
        high = pltpu.roll(cols, (WIN * f - WIN * lat_blk) % lon, 1)
        corner_a = jnp.where(at, jnp.where(start_a > 0, high, low), corner_a)
        corner_b = jnp.where(at, jnp.where(start_b > 0, high, low), corner_b)
    for out, start, corner in ((to_a, start_a, corner_a), (to_b, start_b, corner_b)):
        for n in range(ntr):
            out[2 * n : 2 * n + 2] = turned[n, pl.ds(start, 2)]
        for f in range(EXTRA):
            out[2 * (ntr + f) : 2 * (ntr + f) + 2] = ocean[f, pl.ds(start, 2)]
        out[2 * nf] = corner


def kappa_of(u, v):
    du, dv = (u - down(u), v - down(v))
    sq = jnp.where(levels_of(u.shape) < u.shape[-2] - 1, du * du + dv * dv, 0.0)
    return kappa_base + kappa_shear * sq / (1.0 + sq)


def sum_above(x):
    level = levels_of(x.shape)
    k = 1
    while k < x.shape[-2]:
        x = x + jnp.where(level >= k, pltpu.roll(x, k, x.ndim - 2), 0.0)
        k *= 2
    return x


def sum_below(x):
    level, nz = (levels_of(x.shape), x.shape[-2])
    k = 1
    while k < nz:
        x = x + jnp.where(level < nz - k, pltpu.roll(x, nz - k, x.ndim - 2), 0.0)
        k *= 2
    return x


def pressure_of(heat):
    return -expansion * sum_above(heat)


def wet_of(aux):
    depth = jnp.broadcast_to(aux[..., 0:1, :], aux.shape)
    return (levels_of(aux.shape).astype(jnp.float32) < depth).astype(jnp.float32)


def light_of(aux):
    return jnp.broadcast_to(aux[..., 1:2, :], aux.shape)


def dynamics(u, v, wet, kap, prs, coriolis):
    um, ue, uw, un, us = u
    vm, ve, vw, vn, vs = v
    wm, we, ww, wn, ws = wet
    km, ke, kw, kn, ks = kap
    _, pe, pw, pn, ps = prs
    level, nz = (levels_of(um.shape), um.shape[-2])
    oe, ow, on, os_ = (wm * we, wm * ww, wm * wn, wm * ws)
    fe, fw, fn, fs = (0.5 * (um + ue) * oe, 0.5 * (um + uw) * ow, 0.5 * (vm + vn) * on, 0.5 * (vm + vs) * os_)
    ce, cw, cn, cs = (0.5 * (km + ke) * oe, 0.5 * (km + kw) * ow, 0.5 * (km + kn) * on, 0.5 * (km + ks) * os_)
    div = fe - fw + fn - fs
    total = sum_below(div)
    w_top = jnp.where(level >= 1, -total, 0.0)
    w_bot = jnp.where(level < nz - 1, -down(total), 0.0)
    weights = (
        wm * (1.0 - time_step * (ce + cw + cn + cs + 0.5 * (div + w_top - w_bot))),
        time_step * (ce - 0.5 * fe),
        time_step * (cw + 0.5 * fw),
        time_step * (cn - 0.5 * fn),
        time_step * (cs + 0.5 * fs),
        (-0.5 * time_step) * wm * w_top,
        (0.5 * time_step) * wm * w_bot,
    )
    lap_u = oe * (ue - um) + ow * (uw - um) + on * (un - um) + os_ * (us - um)
    lap_v = oe * (ve - vm) + ow * (vw - vm) + on * (vn - vm) + os_ * (vs - vm)
    new_u = wm * (um + time_step * (coriolis * vm - 0.5 * (pe - pw) + viscosity * lap_u))
    new_v = wm * (vm + time_step * (-coriolis * um - 0.5 * (pn - ps) + viscosity * lap_v))
    return (new_u, new_v, weights)


def transport(weights, x, east, west, north, south):
    a0, ae, aw, an, as_, at, ab = weights
    return (a0 * x + ae * east) + (aw * west + an * north) + (as_ * south + at * up(x)) + ab * down(x)


def saturated(x):
    return x * lax.rsqrt(1.0 + x * x)


def absorbed(pigment):
    level = levels_of(pigment.shape)
    sq = pigment * pigment
    depth = water_absorb + pigment_absorb * (sq / (1.0 + sq))
    above = jnp.where(level >= 1, up(depth), 0.0)
    k = 1
    while k < KL:
        above = above + jnp.where(level >= k, pltpu.roll(above, k, above.ndim - 2), 0.0)
        k *= 2
    return jnp.where(level < KL, jnp.exp(-above) * (1.0 - jnp.exp(-depth)), 0.0)


def two_parts(x):
    high = x.astype(jnp.bfloat16)
    return (high, (x - high.astype(jnp.float32)).astype(jnp.bfloat16))


def mix_matrix(rates, nz):
    ntr = rates.shape[0]
    size = ntr * nz
    exact = dict(precision=lax.Precision.HIGHEST, preferred_element_type=jnp.float32)
    spread = lax.broadcasted_iota(jnp.int32, (size, ntr), 0) // nz == lax.broadcasted_iota(jnp.int32, (size, ntr), 1)
    spread = spread.astype(jnp.float32)
    wide = jnp.dot(spread, rates, **exact)
    full = lax.dot_general(wide, spread, (((1,), (1,)), ((), ())), **exact)
    same = lax.broadcasted_iota(jnp.int32, (size, size), 0) % nz == lax.broadcasted_iota(jnp.int32, (size, size), 1) % nz
    high, low = two_parts(jnp.where(same, full, 0.0))
    top = jnp.concatenate([high, high], axis=1)
    return jnp.concatenate([top, jnp.concatenate([low, jnp.zeros_like(low)], axis=1)], axis=0)


def beside(z, r, lon):
    return pltpu.roll(z, lon - 2 - WIN * (r - 1), z.ndim - 1)


def sides(x, edge):
    lane, lon = (lanes_of(x.shape), x.shape[-1])
    west = pltpu.roll(jnp.where(lane == lon - 1, edge, x), 1, x.ndim - 1)
    east = pltpu.roll(jnp.where(lane == 0, edge, x), lon - 1, x.ndim - 1)
    return (east, west)


def around_rows(m, f, z, r, count):
    x = m[f, pl.ds(r, count)]
    edge = jnp.stack([beside(z, r + i, x.shape[-1]) for i in range(count)])
    return (x, *sides(x, edge), m[f, pl.ds(r + 1, count)], m[f, pl.ds(r - 1, count)])


def around_columns(x, own):
    lane, lon = (lanes_of(x.shape), x.shape[-1])
    west = pltpu.roll(jnp.where(lane % WIN == 0, x, own), 1, x.ndim - 1)
    east = pltpu.roll(jnp.where(lane % WIN == WIN - 1, x, own), lon - 1, x.ndim - 1)
    return (x, east, west, pltpu.roll(x, lon - WIN, x.ndim - 1), pltpu.roll(x, WIN, x.ndim - 1))


def coriolis_at(lat, lat_blk):
    _, chip, _ = place()
    latitude = (lat + chip * lat_blk).astype(jnp.float32)
    return coriolis_base * (2.0 * (latitude + 0.5) / (lax.axis_size("row") // 2 * lat_blk) - 1.0)


KAP, PRS, WET = (0, 1, 2)
GROUP = 4


def span(start, stop):
    return (start, stop - start, 1, stop - start)


def chunks(rows, most, body):
    first, apart, times, size = rows
    count = max(k for k in range(1, min(most, size) + 1) if size % k == 0)
    if times == 1:
        apart, times = (count, size // count)
    elif count < size:
        raise ValueError(rows)

    def one(i, _):
        body(first + i * apart, count)
        return 0

    if times == 1:
        body(first, count)
    else:
        lax.fori_loop(0, times, one, 0)


def derive_rows(m, dv, ntr, rows):
    def body(r, count):
        at = pl.ds(r, count)
        dv[KAP, at] = kappa_of(m[ntr, at], m[ntr + 1, at])
        dv[PRS, at] = pressure_of(m[ntr + 2, at])

    chunks(rows, 10, body)


def derive_columns(z, zd, ntr):
    zd[KAP] = kappa_of(z[ntr], z[ntr + 1])
    zd[PRS] = pressure_of(z[ntr + 2])


def ocean_rows(m, dv, z, zd, wts, new, ntr, rows):
    def body(r, count):
        at = pl.ds(r, count)
        lat = lax.broadcasted_iota(jnp.int32, (count, *m.shape[2:]), 0) + (r - 2)
        new_u, new_v, weights = dynamics(
            around_rows(m, ntr, z[ntr], r, count),
            around_rows(m, ntr + 1, z[ntr + 1], r, count),
            around_rows(dv, WET, zd[WET], r, count),
            around_rows(dv, KAP, zd[KAP], r, count),
            around_rows(dv, PRS, zd[PRS], r, count),
            coriolis_at(lat, m.shape[1] - 4),
        )
        new[ntr, at] = new_u
        new[ntr + 1, at] = new_v
        for i, w in enumerate(weights):
            wts[i, at] = w

    chunks(rows, 9, body)


def tracer_rows(m, z, wts, new, sat, ntr, rows):
    nz, lon = m.shape[2:]
    half = ntr * nz

    def row(r):
        weights = [wts[i, r] for i in range(7)]
        for n in range(0, ntr, GROUP):
            x = m[n : n + GROUP, r]
            edge = beside(z[n : n + GROUP], r, lon)
            moved = transport(weights, x, *sides(x, edge), m[n : n + GROUP, r + 1], m[n : n + GROUP, r - 1])
            new[n : n + GROUP, r] = moved
            high, low = two_parts(saturated(moved).reshape(GROUP * nz, lon))
            sat[r, n * nz : (n + GROUP) * nz, :] = high
            sat[r, half + n * nz : half + (n + GROUP) * nz, :] = low
        h = ntr + 2
        x = m[h, r]
        new[h, r] = transport(weights, x, *sides(x, beside(z[h], r, lon)), m[h, r + 1], m[h, r - 1])

    def body(r, count):
        for i in range(count):
            row(r + i)

    chunks(rows, 3, body)


def react_rows(dv, mix, new, sat, ntr, rows):
    nz, lon = new.shape[2:]
    half = ntr * nz
    first, apart, times, size = rows
    every = [first + i * apart + k for i in range(times) for k in range(size)]
    both = jnp.concatenate([sat[r] for r in every], axis=1)
    res = jnp.dot(mix[...], both, preferred_element_type=jnp.float32)
    res = res[:half] + res[half:]
    for i, r in enumerate(every):
        gain = react_step * dv[WET, r]
        for n in range(ntr):
            new[n, r] = new[n, r] + gain * res[n * nz : (n + 1) * nz, i * lon : (i + 1) * lon]


def light_rows(m, dv, new, ntr, rows):
    def body(r, count):
        at = pl.ds(r, count)
        new[ntr + 2, at] += heat_gain * light_of(m[ntr + 3, at]) * dv[WET, at] * absorbed(new[0, at])

    chunks(rows, 9, body)


def column_step(z0, g0, zd, gd, z1, mix, ntr, lat_blk):
    nz, lon = z0.shape[1:]
    half = ntr * nz
    wet = zd[WET]
    new_u, new_v, weights = dynamics(
        around_columns(z0[ntr], g0[ntr]),
        around_columns(z0[ntr + 1], g0[ntr + 1]),
        around_columns(wet, gd[WET]),
        around_columns(zd[KAP], gd[KAP]),
        around_columns(zd[PRS], gd[PRS]),
        coriolis_at(lanes_of((nz, lon)) // WIN - 1, lat_blk),
    )
    moved = transport(weights, *around_columns(z0[:ntr], g0[:ntr]))
    high, low = two_parts(saturated(moved).reshape(half, lon))
    res = jnp.dot(mix[...], jnp.concatenate([high, low], axis=0), preferred_element_type=jnp.float32)
    done = moved + (react_step * wet) * (res[:half] + res[half:]).reshape(ntr, nz, lon)
    z1[:ntr] = done
    z1[ntr] = new_u
    z1[ntr + 1] = new_v
    heat = transport(weights, *around_columns(z0[ntr + 2], g0[ntr + 2]))
    z1[ntr + 2] = heat + heat_gain * light_of(z0[ntr + 3]) * wet * absorbed(done[0])


def fill_kernel(turned, ocean, g_own, rates, m0, dv, mix, g0, gd):
    ntr, lat_blk, nz, _ = turned.shape
    mix[...] = mix_matrix(rates[...], nz)
    own = span(2, lat_blk + 2)

    def wets(r, count):
        at = pl.ds(r, count)
        for f in range(EXTRA):
            m0[ntr + f, at] = ocean[f, pl.ds(r - 2, count)]
        dv[WET, at] = wet_of(ocean[EXTRA - 1, pl.ds(r - 2, count)])

    chunks(own, 8, wets)

    def some(r, count):
        wet = dv[WET, r]
        for n in range(ntr):
            m0[n, r] = turned[n, r - 2] * wet

    chunks(own, 1, some)
    derive_rows(m0, dv, ntr, own)
    mask_columns([g_own[f] for f in range(ntr + EXTRA)], g0, gd)


def mask_columns(fields, z, zd):
    ntr = len(fields) - EXTRA
    wet = wet_of(fields[-1])
    zd[WET] = wet
    for f, cols in enumerate(fields):
        z[f] = cols * wet if f < ntr else cols
    derive_columns(z, zd, ntr)


def inner_kernel(m0, dv, mix, g0, gd, z_in, m1, m2, dv1, wts, sat, z0, z1, zd):
    nf, rows, _, _ = m0.shape
    ntr = nf - EXTRA
    mask_columns([z_in[f] for f in range(nf)], z0, zd)
    column_step(z0, g0, zd, gd, z1, mix, ntr, rows - 4)
    now = span(3, rows - 3)
    ocean_rows(m0, dv, z0, zd, wts, m1, ntr, now)
    tracer_rows(m0, z0, wts, m1, sat, ntr, now)
    react_rows(dv, mix, m1, sat, ntr, now)
    light_rows(m0, dv, m1, ntr, now)
    dv1[WET, 3 : rows - 3] = dv[WET, 3 : rows - 3]
    derive_rows(m1, dv1, ntr, now)
    derive_columns(z1, zd, ntr)
    now = span(4, rows - 4)
    ocean_rows(m1, dv1, z1, zd, wts, m2, ntr, now)
    tracer_rows(m1, z1, wts, m2, sat, ntr, now)
    react_rows(dv1, mix, m2, sat, ntr, now)
    light_rows(m0, dv1, m2, ntr, now)


def outer_kernel(m_own, dv_own, mix, g0, gd, z_in, got_a, got_b, m1_in, m2_in, rim, keep, send, m0, m1, dv0, dv1, wts, sat, z0, z1, zd):
    nf, rows, nz, lon = m_own.shape
    ntr = nf - EXTRA
    lat_blk = rows - 4
    half, chip, _ = place()
    even = chip % 2 == 0
    south_ok, north_ok = (chip > 0, chip < lax.axis_size("row") // 2 - 1)

    def got(high, index):
        a, b = (got_a[index], got_b[index])
        picked = jnp.where(even, a, b) if high else jnp.where(even, b, a)
        return jnp.where(north_ok if high else south_ok, picked, 0.0)

    for high, start in ((False, 0), (True, rows - 2)):
        for f in range(EXTRA):
            m0[ntr + f, start : start + 2] = got(high, pl.ds(2 * (ntr + f), 2))
        wet = wet_of(m0[nf - 1, start : start + 2])
        dv0[WET, start : start + 2] = wet
        for n in range(ntr):
            m0[n, start : start + 2] = got(high, pl.ds(2 * n, 2)) * wet
        derive_rows(m0, dv0, ntr, span(start, start + 2))
    for start in (2, rows - 4):
        m0[:, start : start + 2] = m_own[:, start : start + 2]
        dv0[:, start : start + 2] = dv_own[:, start : start + 2]
    lane = lanes_of((nz, lon))
    low, high = (got(False, 2 * nf), got(True, 2 * nf))
    at_low, at_high = (lane < WIN, (lane >= WIN * (lat_blk + 1)) & (lane < WIN * (lat_blk + 2)))
    fields = []
    for f in range(nf):
        cols = jnp.where(at_low, pltpu.roll(low, (-WIN * f) % lon, 1), z_in[f])
        fields.append(jnp.where(at_high, pltpu.roll(high, (WIN * (lat_blk + 1) - WIN * f) % lon, 1), cols))
    mask_columns(fields, z0, zd)
    column_step(z0, g0, zd, gd, z1, mix, ntr, lat_blk)
    now = (1, lat_blk, 2, 2)
    ocean_rows(m0, dv0, z0, zd, wts, m1, ntr, now)
    tracer_rows(m0, z0, wts, m1, sat, ntr, now)
    react_rows(dv0, mix, m1, sat, ntr, now)
    light_rows(m0, dv0, m1, ntr, now)
    for start in (3, rows - 5):
        m1[:, start : start + 2] = m1_in[:, start : start + 2]
    for start in (1, rows - 3):
        dv1[WET, start : start + 2] = dv0[WET, start : start + 2]
    for start in (3, rows - 5):
        dv1[WET, start : start + 2] = dv_own[WET, start : start + 2]
    derive_rows(m1, dv1, ntr, (1, rows - 6, 2, 4))
    derive_columns(z1, zd, ntr)
    now = (2, rows - 6, 2, 2)
    ocean_rows(m1, dv1, z1, zd, wts, m0, ntr, now)
    tracer_rows(m1, z1, wts, m0, sat, ntr, now)
    react_rows(dv1, mix, m0, sat, ntr, now)
    light_rows(m0, dv1, m0, ntr, now)

    rim[:, 0:2] = m0[:ntr, 2:4]
    rim[:, 2:4] = m0[:ntr, rows - 4 : rows - 2]
    m0[ntr : ntr + 3, 4 : rows - 4] = m2_in[ntr : ntr + 3, 4 : rows - 4]
    count = lat_blk // 2
    for f in range(3):
        keep[f] = m0[ntr + f, pl.ds(2 + half * count, count)]
        send[f] = m0[ntr + f, pl.ds(2 + (1 - half) * count, count)]


def write_kernel(rim, m, out, block, sem):
    ntr, nz, lat_blk, lon = block.shape
    copies = []
    for n in range(0, ntr, GROUP):
        for k in range(n, n + GROUP):
            for t in range(lat_blk):
                edge = {0: 0, 1: 1, lat_blk - 2: 2, lat_blk - 1: 3}.get(t)
                block[k, :, t, :] = m[k, t + 2] if edge is None else rim[k, edge]
        copy = pltpu.make_async_copy(block.at[pl.ds(n, GROUP)], out.at[pl.ds(n, GROUP)], sem.at[n // GROUP])
        copy.start()
        copies.append(copy)
    for copy in copies:
        copy.wait()


def unpack_kernel(keep, got, flow, temp):
    _, lat_dev, nz, lon = keep.shape
    first = place()[0] == 0
    for t in range(lat_dev):
        for f in range(3):
            a, b = (keep[f, t], got[f, t])
            low, high = (jnp.where(first, a, b), jnp.where(first, b, a))
            if f < 2:
                flow[f, :, t, :lon] = low
                flow[f, :, t, lon:] = high
            else:
                temp[:, t, :lon] = low
                temp[:, t, lon:] = high


def call(kernel, outs, *args, scratch=(), held=True, away=False, limit=40):
    vmem = pl.BlockSpec(memory_space=pltpu.VMEM)
    return pl.pallas_call(
        kernel,
        out_shape=[jax.ShapeDtypeStruct(s, jnp.float32) if isinstance(s, tuple) else s for s in outs],
        in_specs=[vmem if held else pl.BlockSpec(memory_space=pl.ANY)] * len(args),
        out_specs=[pl.BlockSpec(memory_space=pl.ANY) if away else vmem] * len(outs),
        scratch_shapes=[pltpu.VMEM(s, jnp.float32) if isinstance(s, tuple) else s for s in scratch],
        compiler_params=pltpu.CompilerParams(vmem_limit_bytes=limit * 2**20),
    )(*args)


def both_ways(pairs):
    return sorted(pairs + [(b, a) for a, b in pairs])


def exchanges(n_row, n_col):
    chips = n_row // 2

    def dev(p, h, c):
        return (2 * p + h) * n_col + c

    partner = [(dev(p, 0, c), dev(p, 1, c)) for p in range(chips) for c in range(n_col)]
    outer = [(dev(p, 1, c), dev(p, 0, c + 1)) for p in range(chips) for c in range(n_col - 1)]
    outer += [(dev(p, 0, 0), dev(p, 1, n_col - 1)) for p in range(chips)]
    lat_a = [(dev(p, h, c), dev(p + 1, h, c)) for p in range(0, chips - 1, 2) for h in (0, 1) for c in range(n_col)]
    lat_b = [(dev(p, h, c), dev(p + 1, h, c)) for p in range(1, chips - 1, 2) for h in (0, 1) for c in range(n_col)]
    if chips % 2 == 0 and chips > 2:
        lat_b += [(dev(0, h, c), dev(chips - 1, h, c)) for h in (0, 1) for c in range(n_col)]
    return [both_ways(x) for x in (partner, outer, lat_a, lat_b)]


def on_device(n_row, n_col, flow, temp, tracers, bottom, sunlight, rates):
    nz, lat_dev, lon_dev = temp.shape
    _, ntr, _, lat_blk, lon = tracers.shape
    nf = ntr + EXTRA
    partner, outer, lat_a, lat_b = exchanges(n_row, n_col)

    def swap(x, pairs):
        return lax.ppermute(x, ("row", "col"), pairs)

    block = tracers[0]
    parts = [flow.reshape(-1, lat_dev, lon_dev), temp, bottom[None], sunlight[None]]
    total = sum(part.shape[0] for part in parts)
    surface, start = (0.0, 0)
    for part in parts:
        count = part.shape[0]
        surface = surface + jnp.pad(part, ((start, total - start - count), (0, 0), (0, 0))).astype(jnp.float32)
        start += count
    rows = lat_blk + 4
    cols, extra, some = ((nf, nz, lon), (EXTRA, nz, lon), (3, nz, lon))
    copies = pltpu.SemaphoreType.DMA((ntr // GROUP,))
    sent = (EXTRA * (lat_dev + 1), nz, lon)
    mine, to_partner, g_other = call(pack_ocean_kernel, [(EXTRA, lat_dev, nz, lon), sent, extra], surface)
    got = swap(to_partner, partner)
    turned, g_tracers = call(
        pack_tracers_kernel,
        [(ntr, lat_blk, nz, lon), (ntr, nz, lon)],
        block,
        scratch=[block.shape, copies],
        held=False,
        limit=52,
    )
    ocean, g_own, to_outer = call(
        join_kernel, [(EXTRA, lat_blk, nz, lon), cols, (nf // 4, nz, lon)], mine, got, to_partner, g_tracers
    )
    from_outer = swap(to_outer, outer)
    g_partner = swap(g_tracers, partner)
    full, derived = ((nf, rows, nz, lon), (3, rows, nz, lon))
    m0, dv, mix, g0, gd = call(
        fill_kernel,
        [full, derived, jax.ShapeDtypeStruct((2 * ntr * nz, 2 * ntr * nz), jnp.bfloat16), cols, some],
        turned,
        ocean,
        g_own,
        rates,
    )
    edge = (2 * nf + 1, nz, lon)
    z, to_a, to_b = call(edge_kernel, [cols, edge, edge], turned, ocean, g_partner, got, g_other, from_outer)
    got_a, got_b = (swap(to_a, lat_a), swap(to_b, lat_b))
    work = [(7, rows, nz, lon), pltpu.VMEM((rows, 2 * ntr * nz, lon), jnp.bfloat16), cols, cols, some]
    m1, m2 = call(inner_kernel, [full, full], m0, dv, mix, g0, gd, z, scratch=[derived] + work)
    third = (3, lat_dev, nz, lon)
    rim, keep, send = call(
        outer_kernel,
        [(ntr, 4, nz, lon), third, third],
        m0,
        dv,
        mix,
        g0,
        gd,
        z,
        got_a,
        got_b,
        m1,
        m2,
        scratch=[full, full, derived, derived] + work,
    )
    returned = swap(send, partner)
    (out,) = call(write_kernel, [(ntr, nz, lat_blk, lon)], rim, m2, scratch=[(ntr, nz, lat_blk, lon), copies], away=True)
    flow_out, temp_out = call(
        unpack_kernel, [(2, nz, lat_dev, lon_dev), (nz, lat_dev, lon_dev)], keep, returned
    )
    return (flow_out, temp_out, out[None])


def solution(mesh):
    in_specs = (
        P(None, None, "row", "col"),
        P(None, "row", "col"),
        P("row", None, None, None, "col"),
        P("row", "col"),
        P("row", "col"),
        P(),
    )
    out_specs = (
        P(None, None, "row", "col"),
        P(None, "row", "col"),
        P("row", None, None, None, "col"),
    )
    return jax.shard_map(
        functools.partial(on_device, mesh.shape["row"], mesh.shape["col"]),
        mesh=mesh,
        in_specs=in_specs,
        out_specs=out_specs,
        check_vma=False,
    )
```

time: 33 us -> 25.7 us (0.78)
  the two profiles are of different devices: /device:TPU:0 before, /device:TPU:1 now
where the time goes in v3:
time: 25.7 us; the launch traced here: 25.5 us
  Pallas kernels  13.5 us (53%)
  starting transfers between devices  8.78 us (34%)
  waiting for transfers between devices  1.48 us (6%)
  other arithmetic  0.99 us (4%)
  between operations  0.72 us (3%)
    pallas_call x9, Pallas kernels, call(): pl.pallas_call(kernel, out_shape=[jax.ShapeDtypeStruct(s, jnp.float32) if...  13.5 us
    ppermute x6, starting transfers between devices, swap(): return lax.ppermute(x, ('row', 'col'), pairs)  8.78 us
    ppermute x6, waiting for transfers between devices, swap(): return lax.ppermute(x, ('row', 'col'), pairs)  1.48 us
    add x1, other arithmetic, on_device(): surface + jnp.pad(part, ((start, total - start - count), (0, 0), (0, 0)))...  0.99 us
  transfers between devices with their start and end apart: 6, of which 1 were waited for; matrix products, arithmetic and copies ran while one was open for 0% of the time, Pallas kernels for 38%

profile of v3, /device:TPU:1, one launch (start us, length us, event | category | flops | bytes accessed | tf_op | source)
XLA Modules:
  0.0 25.5 jit_solution(4754486468268944727)
XLA Ops:
  0.6 1.0 %pad_add_fusion.surface = f32[26,8,256]{2,1,0:T(8,128)S(1)} fusion(f32[1,8,256]{2,1,0:T(8,128)} %bitcast.8, s32[1,8,256]{2,1,0:T(8,128)} %bitcast.9, f32[8,8,256]{2,1,0:T(8,128)} %param.7, f32[16,8,256]{2,1,0:T(8,128)} %bitcast.7), kind=kLoop, calls=%fused_computation | loop fusion | flops 212992 | bytes 425984 | tf_op jit(solution)/shard_map/add | solution.py:632
  1.6 0.0 copy-start
  1.6 0.2 shard_map.86
  1.9 0.1 collective-permute-start
  1.9 2.0 %shard_map.85 = (f32[16,16,8,128]{3,2,1,0:T(8,128)S(1)}, f32[16,8,128]{2,1,0:T(8,128)S(1)}) custom-call(f32[16,8,16,128]{3,2,1,0:T(8,128)} %bitcast.6), custom_call_target="tpu_custom_call" | custom-call | tf_op jit(solution)/shard_map/pallas_call | solution.py:587
  3.9 0.5 %collective-permute-start.1 = (f32[16,8,128]{2,1,0:T(8,128)S(1)}, f32[16,8,128]{2,1,0:T(8,128)S(1)}, u32[]{:S(2)}, u32[]{:S(2)}) collective-permute-start(f32[16,8,128]{2,1,0:T(8,128)S(1)} %get-tuple-element.29.g_tracers), channel_id=1, source_target_pairs={{0,4},{1,5},{2,6},{3,7},{4,0},{5,1},{6,2},{7,3},{8,12},{9,13},{10,... | collective-permute-start | bytes 196616 | tf_op jit(solution)/shard_map/ppermute | solution.py:624
  4.4 0.0 collective-permute-done.got
  4.4 0.3 %shard_map.87 = (f32[4,16,8,128]{3,2,1,0:T(8,128)S(1)}, f32[20,8,128]{2,1,0:T(8,128)S(1)}, f32[5,8,128]{2,1,0:T(8,128)S(1)}) custom-call(f32[4,8,8,128]{3,2,1,0:T(8,128)S(1)} %get-tuple-element.27.mine, f32[36,8,128]{2,1,0:T(8,128)S(1)} %collective-permute-done.got, f32[36,8,128]{2,1,0:T(8,128)S(1)} %get-tuple-element.28.to_partner, ...), custom_call_target="tpu_custom_call" | custom-call | tf_op jit(solution)/shard_map/pallas_call | solution.py:587
  4.8 2.7 %collective-permute-start.2 = (f32[5,8,128]{2,1,0:T(8,128)S(1)}, f32[5,8,128]{2,1,0:T(8,128)S(1)}, u32[]{:S(2)}, u32[]{:S(2)}) collective-permute-start(f32[5,8,128]{2,1,0:T(8,128)S(1)} %get-tuple-element.38), channel_id=1, source_target_pairs={{0,7},{1,4},{2,5},{3,6},{4,1},{5,2},{6,3},{7,0},{8,15},{9,12},{10,... | collective-permute-start | bytes 61448 | tf_op jit(solution)/shard_map/ppermute | solution.py:624
  7.5 0.0 collective-permute-done.1.g_partner
  7.5 1.5 %collective-permute-done.2.from_outer = f32[5,8,128]{2,1,0:T(8,128)S(1)} collective-permute-done((f32[5,8,128]{2,1,0:T(8,128)S(1)}, f32[5,8,128]{2,1,0:T(8,128)S(1)}, u32[]{:S(2)}, u32[]{:S(2)}) %collective-permute-start.2) | collective-permute-done | bytes 20512 | tf_op jit(solution)/shard_map/ppermute | solution.py:624
  9.0 0.2 shard_map.89
  9.1 1.3 %collective-permute-start.3 = (f32[41,8,128]{2,1,0:T(8,128)S(1)}, f32[41,8,128]{2,1,0:T(8,128)S(1)}, u32[]{:S(2)}, u32[]{:S(2)}) collective-permute-start(f32[41,8,128]{2,1,0:T(8,128)S(1)} %get-tuple-element.40), channel_id=1, source_target_pairs={{0,8},{1,9},{2,10},{3,11},{4,12},{5,13},{6,14},{7,15},{8,0},{9,1},... | collective-permute-start | bytes 503816 | tf_op jit(solution)/shard_map/ppermute | solution.py:624
  10.5 1.2 %collective-permute-start.4 = (f32[41,8,128]{2,1,0:T(8,128)S(1)}, f32[41,8,128]{2,1,0:T(8,128)S(1)}, u32[]{:S(2)}, u32[]{:S(2)}) collective-permute-start(f32[41,8,128]{2,1,0:T(8,128)S(1)} %get-tuple-element.41), channel_id=1, source_target_pairs={{0,24},{1,25},{2,26},{3,27},{4,28},{5,29},{6,30},{7,31},{8,16},{9,... | collective-permute-start | bytes 503816 | tf_op jit(solution)/shard_map/ppermute | solution.py:624
  11.7 0.0 copy-done
  11.7 0.7 %shard_map.88 = (f32[20,20,8,128]{3,2,1,0:T(8,128)S(1)}, f32[3,20,8,128]{3,2,1,0:T(8,128)S(1)}, bf16[256,256]{1,0:T(8,128)(2,1)S(1)}, f32[20,8,128]{2,1,0:T(8,128)S(1)}, f32[3,8,128]{2,1,0:T(8,128)S(1)}) custom-call(f32[16,16,8,128]{3,2,1,0:T(8,128)S(1)} %get-tuple-element.26.turned, f32[4,16,8,128]{3,2,1,0:T(8,128)S(1)} %get-tuple-element.30.ocean, ...), custom_call_target="tpu_custom_call" | custom-call | tf_op jit(solution)/shard_map/pallas_call | solution.py:587
  12.4 5.2 %shard_map.90 = (f32[20,20,8,128]{3,2,1,0:T(8,128)S(1)}, f32[20,20,8,128]{3,2,1,0:T(8,128)S(1)}) custom-call(f32[20,20,8,128]{3,2,1,0:T(8,128)S(1)} %get-tuple-element.32.m0.m_own, f32[3,20,8,128]{3,2,1,0:T(8,128)S(1)} %get-tuple-element.33.dv.dv_own, bf16[256,256]{1,0:T(8,128)(2,1)S(1)} %get-tuple-element.34.mix, f32[20,8,128]{2,1,0:T(8,128)S(1)} %get-tuple-element.35.g0, ...), custom_call_target="tpu_custom_call" | custom-call | tf_op jit(solution)/shard_map/pallas_call | solution.py:587
  17.7 0.0 collective-permute-done.3.got_a
  17.7 0.0 collective-permute-done.4.got_b
  17.7 2.7 %shard_map.91 = (f32[16,4,8,128]{3,2,1,0:T(8,128)S(1)}, f32[3,8,8,128]{3,2,1,0:T(8,128)S(1)}, f32[3,8,8,128]{3,2,1,0:T(8,128)S(1)}) custom-call(f32[20,20,8,128]{3,2,1,0:T(8,128)S(1)} %get-tuple-element.32.m0.m_own, f32[3,20,8,128]{3,2,1,0:T(8,128)S(1)} %get-tuple-element.33.dv.dv_own, bf16[256,256]{1,0:T(8,128)(2,1)S(1)} %get-tuple-element.34.mix, ...), custom_call_target="tpu_custom_call" | custom-call | tf_op jit(solution)/shard_map/pallas_call | solution.py:587
  20.5 2.9 %collective-permute-start.5 = (f32[3,8,8,128]{3,2,1,0:T(8,128)S(1)}, f32[3,8,8,128]{3,2,1,0:T(8,128)S(1)}, u32[]{:S(2)}, u32[]{:S(2)}) collective-permute-start(f32[3,8,8,128]{3,2,1,0:T(8,128)S(1)} %get-tuple-element.45), channel_id=1, source_target_pairs={{0,4},{1,5},{2,6},{3,7},{4,0},{5,1},{6,2},{7,3},{8,12},{9,13},{10,... | collective-permute-start | bytes 294920 | tf_op jit(solution)/shard_map/ppermute | solution.py:624
  23.4 1.3 %shard_map.93 = f32[16,8,16,128]{3,2,1,0:T(8,128)} custom-call(f32[16,4,8,128]{3,2,1,0:T(8,128)S(1)} %get-tuple-element.48.rim, f32[20,20,8,128]{3,2,1,0:T(8,128)S(1)} %get-tuple-element.43.m2_in.m), custom_call_target="tpu_custom_call" | custom-call | tf_op jit(solution)/shard_map/pallas_call | solution.py:587
  24.7 0.0 collective-permute-done.5.got
  24.7 0.8 %shard_map.92 = (f32[2,8,8,256]{3,2,1,0:T(8,128)}, f32[8,8,256]{2,1,0:T(8,128)}) custom-call(f32[3,8,8,128]{3,2,1,0:T(8,128)S(1)} %get-tuple-element.44.keep, f32[3,8,8,128]{3,2,1,0:T(8,128)S(1)} %collective-permute-done.5.got), custom_call_target="tpu_custom_call" | custom-call | tf_op jit(solution)/shard_map/pallas_call | solution.py:587
Async XLA Ops:
  1.6 10.1 %copy-start = (f32[16,16]{1,0:T(8,128)S(1)}, f32[16,16]{1,0:T(8,128)}, u32[]{:S(2)}) copy-start(f32[16,16]{1,0:T(8,128)} %rates.1) | copy-start | bytes 3076
  1.9 2.6 %collective-permute-start = (f32[36,8,128]{2,1,0:T(8,128)S(1)}, f32[36,8,128]{2,1,0:T(8,128)S(1)}, u32[]{:S(2)}, u32[]{:S(2)}) collective-permute-start(f32[36,8,128]{2,1,0:T(8,128)S(1)} %get-tuple-element.28.to_partner), channel_id=1, source_target_pairs={{0,4},{1,5},{2,6},{3,7},{4,0},{5,1},{6,2},{7,3},{8,12},{9,13},{10,... | collective-permute-start | bytes 442376 | tf_op jit(solution)/shard_map/ppermute | solution.py:624
  3.9 3.6 %collective-permute-start.1 = (f32[16,8,128]{2,1,0:T(8,128)S(1)}, f32[16,8,128]{2,1,0:T(8,128)S(1)}, u32[]{:S(2)}, u32[]{:S(2)}) collective-permute-start(f32[16,8,128]{2,1,0:T(8,128)S(1)} %get-tuple-element.29.g_tracers), channel_id=1, source_target_pairs={{0,4},{1,5},{2,6},{3,7},{4,0},{5,1},{6,2},{7,3},{8,12},{9,13},{10,... | collective-permute-start | bytes 196616 | tf_op jit(solution)/shard_map/ppermute | solution.py:624
  4.8 4.2 %collective-permute-start.2 = (f32[5,8,128]{2,1,0:T(8,128)S(1)}, f32[5,8,128]{2,1,0:T(8,128)S(1)}, u32[]{:S(2)}, u32[]{:S(2)}) collective-permute-start(f32[5,8,128]{2,1,0:T(8,128)S(1)} %get-tuple-element.38), channel_id=1, source_target_pairs={{0,7},{1,4},{2,5},{3,6},{4,1},{5,2},{6,3},{7,0},{8,15},{9,12},{10,... | collective-permute-start | bytes 61448 | tf_op jit(solution)/shard_map/ppermute | solution.py:624
  9.1 8.6 %collective-permute-start.3 = (f32[41,8,128]{2,1,0:T(8,128)S(1)}, f32[41,8,128]{2,1,0:T(8,128)S(1)}, u32[]{:S(2)}, u32[]{:S(2)}) collective-permute-start(f32[41,8,128]{2,1,0:T(8,128)S(1)} %get-tuple-element.40), channel_id=1, source_target_pairs={{0,8},{1,9},{2,10},{3,11},{4,12},{5,13},{6,14},{7,15},{8,0},{9,1},... | collective-permute-start | bytes 503816 | tf_op jit(solution)/shard_map/ppermute | solution.py:624
  10.5 7.2 %collective-permute-start.4 = (f32[41,8,128]{2,1,0:T(8,128)S(1)}, f32[41,8,128]{2,1,0:T(8,128)S(1)}, u32[]{:S(2)}, u32[]{:S(2)}) collective-permute-start(f32[41,8,128]{2,1,0:T(8,128)S(1)} %get-tuple-element.41), channel_id=1, source_target_pairs={{0,24},{1,25},{2,26},{3,27},{4,28},{5,29},{6,30},{7,31},{8,16},{9,... | collective-permute-start | bytes 503816 | tf_op jit(solution)/shard_map/ppermute | solution.py:624
  20.5 4.2 %collective-permute-start.5 = (f32[3,8,8,128]{3,2,1,0:T(8,128)S(1)}, f32[3,8,8,128]{3,2,1,0:T(8,128)S(1)}, u32[]{:S(2)}, u32[]{:S(2)}) collective-permute-start(f32[3,8,8,128]{3,2,1,0:T(8,128)S(1)} %get-tuple-element.45), channel_id=1, source_target_pairs={{0,4},{1,5},{2,6},{3,7},{4,0},{5,1},{6,2},{7,3},{8,12},{9,13},{10,... | collective-permute-start | bytes 294920 | tf_op jit(solution)/shard_map/ppermute | solution.py:624

commit v4 on v3

--- a/solution.py
+++ b/solution.py
@@ -138,38 +138,29 @@
         to_outer[i] = jnp.where(near, low, pltpu.roll(high, lon // 2, 1))
 
 
-def edge_kernel(turned, ocean, g_partner, got, g_other, from_outer, z, to_a, to_b):
-    ntr, lat_blk, nz, lon = turned.shape
-    nf = ntr + EXTRA
+def edge_kernel(lat_blk, inner, from_outer, z, to_a, to_b):
+    nf, nz, lon = z.shape
+
     half, chip, column = place()
     tile = (nz, lon)
     lane = lanes_of(tile)
-    own_lanes = in_half(tile, half, lat_blk // 2)
     outer_ok = jnp.where(half == 0, column > 0, column < lax.axis_size("col") - 1)
     from_partner = (lane % WIN < 2).astype(jnp.int32) == half
     outer_lanes = in_half(tile, 0, lat_blk) & outer_ok
     start_a, start_b = edge_starts(chip, lat_blk)
     corner_a = corner_b = jnp.zeros(tile, jnp.float32)
     for f in range(nf):
-        if f < ntr:
-            partner = g_partner[f]
-        else:
-            partner = jnp.where(own_lanes, g_other[f - ntr], got[EXTRA * (lat_blk // 2) + f - ntr])
         k = f % 4
         moved = pltpu.roll(from_outer[f // 4], lon + 2 * half - 2 * (k % 2) - lon // 2 * (k // 2), 1)
-        cols = jnp.where(from_partner, partner, jnp.where(outer_lanes, moved, 0.0))
+        cols = jnp.where(from_partner, inner[f], jnp.where(outer_lanes, moved, 0.0))
         z[f] = cols
         at = (lane >= WIN * f) & (lane < WIN * f + WIN)
         low = pltpu.roll(cols, (WIN * f - WIN) % lon, 1)
         high = pltpu.roll(cols, (WIN * f - WIN * lat_blk) % lon, 1)
         corner_a = jnp.where(at, jnp.where(start_a > 0, high, low), corner_a)
         corner_b = jnp.where(at, jnp.where(start_b > 0, high, low), corner_b)
-    for out, start, corner in ((to_a, start_a, corner_a), (to_b, start_b, corner_b)):
-        for n in range(ntr):
-            out[2 * n : 2 * n + 2] = turned[n, pl.ds(start, 2)]
-        for f in range(EXTRA):
-            out[2 * (ntr + f) : 2 * (ntr + f) + 2] = ocean[f, pl.ds(start, 2)]
-        out[2 * nf] = corner
+    to_a[...] = corner_a
+    to_b[...] = corner_b
 
 
 def kappa_of(u, v):
@@ -439,8 +430,18 @@
     z1[ntr + 2] = heat + heat_gain * light_of(z0[ntr + 3]) * wet * absorbed(done[0])
 
 
-def fill_kernel(turned, ocean, g_own, rates, m0, dv, mix, g0, gd):
-    ntr, lat_blk, nz, _ = turned.shape
+def fill_kernel(turned, ocean, g_own, g_partner, got, g_other, rates, rows_a, rows_b, m0, dv, mix, g0, gd, inner):
+    ntr, lat_blk, nz, lon = turned.shape
+    half, chip, _ = place()
+    inner[:ntr] = g_partner[...]
+    for f in range(EXTRA):
+        theirs = got[EXTRA * (lat_blk // 2) + f]
+        inner[ntr + f] = jnp.where(in_half((nz, lon), half, lat_blk // 2), g_other[f], theirs)
+    for out, start in zip((rows_a, rows_b), edge_starts(chip, lat_blk)):
+        for n in range(ntr):
+            out[2 * n : 2 * n + 2] = turned[n, pl.ds(start, 2)]
+        for f in range(EXTRA):
+            out[2 * (ntr + f) : 2 * (ntr + f) + 2] = ocean[f, pl.ds(start, 2)]
     mix[...] = mix_matrix(rates[...], nz)
     own = span(2, lat_blk + 2)
 
@@ -491,7 +492,7 @@
     light_rows(m0, dv1, m2, ntr, now)
 
 
-def outer_kernel(m_own, dv_own, mix, g0, gd, z_in, got_a, got_b, m1_in, m2_in, rim, keep, send, m0, m1, dv0, dv1, wts, sat, z0, z1, zd):
+def outer_kernel(m_own, dv_own, mix, g0, gd, z_in, rows_a, rows_b, edge_a, edge_b, m1_in, m2_in, rim, keep, send, m0, m1, dv0, dv1, wts, sat, z0, z1, zd):
     nf, rows, nz, lon = m_own.shape
     ntr = nf - EXTRA
     lat_blk = rows - 4
@@ -499,24 +500,24 @@
     even = chip % 2 == 0
     south_ok, north_ok = (chip > 0, chip < lax.axis_size("row") // 2 - 1)
 
-    def got(high, index):
-        a, b = (got_a[index], got_b[index])
+    def got(high, a, b, index):
+        a, b = (a[index], b[index])
         picked = jnp.where(even, a, b) if high else jnp.where(even, b, a)
         return jnp.where(north_ok if high else south_ok, picked, 0.0)
 
     for high, start in ((False, 0), (True, rows - 2)):
         for f in range(EXTRA):
-            m0[ntr + f, start : start + 2] = got(high, pl.ds(2 * (ntr + f), 2))
+            m0[ntr + f, start : start + 2] = got(high, rows_a, rows_b, pl.ds(2 * (ntr + f), 2))
         wet = wet_of(m0[nf - 1, start : start + 2])
         dv0[WET, start : start + 2] = wet
         for n in range(ntr):
-            m0[n, start : start + 2] = got(high, pl.ds(2 * n, 2)) * wet
+            m0[n, start : start + 2] = got(high, rows_a, rows_b, pl.ds(2 * n, 2)) * wet
         derive_rows(m0, dv0, ntr, span(start, start + 2))
     for start in (2, rows - 4):
         m0[:, start : start + 2] = m_own[:, start : start + 2]
         dv0[:, start : start + 2] = dv_own[:, start : start + 2]
     lane = lanes_of((nz, lon))
-    low, high = (got(False, 2 * nf), got(True, 2 * nf))
+    low, high = (got(False, edge_a, edge_b, ...), got(True, edge_a, edge_b, ...))
     at_low, at_high = (lane < WIN, (lane >= WIN * (lat_blk + 1)) & (lane < WIN * (lat_blk + 2)))
     fields = []
     for f in range(nf):
@@ -582,7 +583,7 @@
                 temp[:, t, lon:] = high
 
 
-def call(kernel, outs, *args, scratch=(), held=True, away=False, limit=40):
+def call(kernel, outs, *args, scratch=(), held=True, away=False, limit=40, cost=1):
     vmem = pl.BlockSpec(memory_space=pltpu.VMEM)
     return pl.pallas_call(
         kernel,
@@ -591,6 +592,7 @@
         out_specs=[pl.BlockSpec(memory_space=pl.ANY) if away else vmem] * len(outs),
         scratch_shapes=[pltpu.VMEM(s, jnp.float32) if isinstance(s, tuple) else s for s in scratch],
         compiler_params=pltpu.CompilerParams(vmem_limit_bytes=limit * 2**20),
+        cost_estimate=pl.CostEstimate(flops=int(cost * 10**9), transcendentals=0, bytes_accessed=int(cost * 4 * 2**20)),
     )(*args)
 
 
@@ -606,7 +608,8 @@
 
     partner = [(dev(p, 0, c), dev(p, 1, c)) for p in range(chips) for c in range(n_col)]
     outer = [(dev(p, 1, c), dev(p, 0, c + 1)) for p in range(chips) for c in range(n_col - 1)]
-    outer += [(dev(p, 0, 0), dev(p, 1, n_col - 1)) for p in range(chips)]
+    for p in range(0, chips - 1, 2):
+        outer += [(dev(p, 0, 0), dev(p + 1, 0, 0)), (dev(p, 1, n_col - 1), dev(p + 1, 1, n_col - 1))]
     lat_a = [(dev(p, h, c), dev(p + 1, h, c)) for p in range(0, chips - 1, 2) for h in (0, 1) for c in range(n_col)]
     lat_b = [(dev(p, h, c), dev(p + 1, h, c)) for p in range(1, chips - 1, 2) for h in (0, 1) for c in range(n_col)]
     if chips % 2 == 0 and chips > 2:
@@ -651,19 +654,25 @@
     from_outer = swap(to_outer, outer)
     g_partner = swap(g_tracers, partner)
     full, derived = ((nf, rows, nz, lon), (3, rows, nz, lon))
-    m0, dv, mix, g0, gd = call(
+    rim = (2 * nf, nz, lon)
+    rows_a, rows_b, m0, dv, mix, g0, gd, inner = call(
         fill_kernel,
-        [full, derived, jax.ShapeDtypeStruct((2 * ntr * nz, 2 * ntr * nz), jnp.bfloat16), cols, some],
+        [rim, rim, full, derived, jax.ShapeDtypeStruct((2 * ntr * nz, 2 * ntr * nz), jnp.bfloat16), cols, some, cols],
         turned,
         ocean,
         g_own,
+        g_partner,
+        got,
+        g_other,
         rates,
     )
-    edge = (2 * nf + 1, nz, lon)
-    z, to_a, to_b = call(edge_kernel, [cols, edge, edge], turned, ocean, g_partner, got, g_other, from_outer)
-    got_a, got_b = (swap(to_a, lat_a), swap(to_b, lat_b))
+    rows_a, rows_b = (swap(rows_a, lat_a), swap(rows_b, lat_b))
+    z, edge_a, edge_b = call(
+        functools.partial(edge_kernel, lat_blk), [cols, (nz, lon), (nz, lon)], inner, from_outer
+    )
+    edge_a, edge_b = (swap(edge_a, lat_a), swap(edge_b, lat_b))
     work = [(7, rows, nz, lon), pltpu.VMEM((rows, 2 * ntr * nz, lon), jnp.bfloat16), cols, cols, some]
-    m1, m2 = call(inner_kernel, [full, full], m0, dv, mix, g0, gd, z, scratch=[derived] + work)
+    m1, m2 = call(inner_kernel, [full, full], m0, dv, mix, g0, gd, z, scratch=[derived] + work, cost=20)
     third = (3, lat_dev, nz, lon)
     rim, keep, send = call(
         outer_kernel,
@@ -674,8 +683,10 @@
         g0,
         gd,
         z,
-        got_a,
-        got_b,
+        rows_a,
+        rows_b,
+        edge_a,
+        edge_b,
         m1,
         m2,
         scratch=[full, full, derived, derived] + work,

time: 25.7 us -> 24.7 us (0.961)
  waiting for transfers between devices: 1.48 us -> 0.78 us
  starting transfers between devices: 8.78 us -> 8.48 us
    ppermute x6 -> x8, waiting for transfers between devices: 1.48 us -> 0.78 us  [swap(): return lax.ppermute(x, ('row', 'col'), pairs)]
    ppermute x6 -> x8, starting transfers between devices: 8.78 us -> 8.48 us  [swap(): return lax.ppermute(x, ('row', 'col'), pairs)]
  transfers between devices with their start and end apart: 6 -> 8, of which waited for: 1 -> 1; matrix products, arithmetic and copies ran while one was open for 0% -> 0% of each run, Pallas kernels for 38% -> 40%
where the time goes in v4:
time: 24.7 us; the launch traced here: 24.5 us
  Pallas kernels  13.5 us (55%)
  starting transfers between devices  8.48 us (34%)
  other arithmetic  0.99 us (4%)
  waiting for transfers between devices  0.78 us (3%)
  between operations  0.7 us (3%)
    pallas_call x9, Pallas kernels, call(): pl.pallas_call(kernel, out_shape=[jax.ShapeDtypeStruct(s, jnp.float32) if...  13.5 us
    ppermute x8, starting transfers between devices, swap(): return lax.ppermute(x, ('row', 'col'), pairs)  8.48 us
    add x1, other arithmetic, on_device(): surface + jnp.pad(part, ((start, total - start - count), (0, 0), (0, 0)))...  0.99 us
    ppermute x8, waiting for transfers between devices, swap(): return lax.ppermute(x, ('row', 'col'), pairs)  0.78 us
  transfers between devices with their start and end apart: 8, of which 1 were waited for; matrix products, arithmetic and copies ran while one was open for 0% of the time, Pallas kernels for 40%

profile of v4, /device:TPU:1, one launch (start us, length us, event | category | flops | bytes accessed | tf_op | source)
XLA Modules:
  0.0 24.5 jit_solution(11342581657586660360)
XLA Ops:
  0.6 1.0 %pad_add_fusion.surface = f32[26,8,256]{2,1,0:T(8,128)S(1)} fusion(f32[1,8,256]{2,1,0:T(8,128)} %bitcast.6, s32[1,8,256]{2,1,0:T(8,128)} %bitcast.7, f32[8,8,256]{2,1,0:T(8,128)} %param.7, f32[16,8,256]{2,1,0:T(8,128)} %bitcast.5), kind=kLoop, calls=%fused_computation | loop fusion | flops 212992 | bytes 425984 | tf_op jit(solution)/shard_map/add | solution.py:635
  1.6 0.2 shard_map.86
  1.8 0.1 collective-permute-start
  1.9 2.0 %shard_map.85 = (f32[16,16,8,128]{3,2,1,0:T(8,128)S(1)}, f32[16,8,128]{2,1,0:T(8,128)S(1)}) custom-call(f32[16,8,16,128]{3,2,1,0:T(8,128)} %bitcast.8), custom_call_target="tpu_custom_call" | custom-call | flops 1000000000 | bytes 4194304 | tf_op jit(solution)/shard_map/pallas_call | solution.py:588
  3.9 0.5 %collective-permute-start.1 = (f32[16,8,128]{2,1,0:T(8,128)S(1)}, f32[16,8,128]{2,1,0:T(8,128)S(1)}, u32[]{:S(2)}, u32[]{:S(2)}) collective-permute-start(f32[16,8,128]{2,1,0:T(8,128)S(1)} %get-tuple-element.32.g_tracers), channel_id=1, source_target_pairs={{0,4},{1,5},{2,6},{3,7},{4,0},{5,1},{6,2},{7,3},{8,12},{9,13},{10,... | collective-permute-start | bytes 196616 | tf_op jit(solution)/shard_map/ppermute | solution.py:627
  4.4 0.0 collective-permute-done.got
  4.4 0.0 copy-start
  4.4 0.3 %shard_map.87 = (f32[4,16,8,128]{3,2,1,0:T(8,128)S(1)}, f32[20,8,128]{2,1,0:T(8,128)S(1)}, f32[5,8,128]{2,1,0:T(8,128)S(1)}) custom-call(f32[4,8,8,128]{3,2,1,0:T(8,128)S(1)} %get-tuple-element.30.mine, f32[36,8,128]{2,1,0:T(8,128)S(1)} %collective-permute-done.got, f32[36,8,128]{2,1,0:T(8,128)S(1)} %get-tuple-element.31.to_partner, ...), custom_call_target="tpu_custom_call" | custom-call | flops 1000000000 | bytes 4194304 | tf_op jit(solution)/shard_map/pallas_call | solution.py:588
  4.7 2.7 %collective-permute-start.2 = (f32[5,8,128]{2,1,0:T(8,128)S(1)}, f32[5,8,128]{2,1,0:T(8,128)S(1)}, u32[]{:S(2)}, u32[]{:S(2)}) collective-permute-start(f32[5,8,128]{2,1,0:T(8,128)S(1)} %get-tuple-element.42), channel_id=1, source_target_pairs={{0,8},{1,4},{2,5},{3,6},{4,1},{5,2},{6,3},{7,15},{8,0},{9,12},{10,... | collective-permute-start | bytes 61448 | tf_op jit(solution)/shard_map/ppermute | solution.py:627
  7.5 0.0 collective-permute-done.1.g_partner
  7.5 0.0 copy-done
  7.5 0.7 %shard_map.88 = (f32[40,8,128]{2,1,0:T(8,128)S(1)}, f32[40,8,128]{2,1,0:T(8,128)S(1)}, f32[20,20,8,128]{3,2,1,0:T(8,128)S(1)}, f32[3,20,8,128]{3,2,1,0:T(8,128)S...) custom-call(f32[16,16,8,128]{3,2,1,0:T(8,128)S(1)} %get-tuple-elemen, ...), custom_call_target="tpu_custom_call" | custom-call | flops 1000000000 | bytes 4194304 | tf_op jit(solution)/shard_map/pallas_call | solution.py:588
  8.2 1.3 %collective-permute-start.3 = (f32[40,8,128]{2,1,0:T(8,128)S(1)}, f32[40,8,128]{2,1,0:T(8,128)S(1)}, u32[]{:S(2)}, u32[]{:S(2)}) collective-permute-start(f32[40,8,128]{2,1,0:T(8,128)S(1)} %get-tuple-element.44), channel_id=1, source_target_pairs={{0,8},{1,9},{2,10},{3,11},{4,12},{5,13},{6,14},{7,15},{8,0},{9,1},... | collective-permute-start | bytes 491528 | tf_op jit(solution)/shard_map/ppermute | solution.py:627
  9.5 1.2 %collective-permute-start.4 = (f32[40,8,128]{2,1,0:T(8,128)S(1)}, f32[40,8,128]{2,1,0:T(8,128)S(1)}, u32[]{:S(2)}, u32[]{:S(2)}) collective-permute-start(f32[40,8,128]{2,1,0:T(8,128)S(1)} %get-tuple-element.45), channel_id=1, source_target_pairs={{0,24},{1,25},{2,26},{3,27},{4,28},{5,29},{6,30},{7,31},{8,16},{9,... | collective-permute-start | bytes 491528 | tf_op jit(solution)/shard_map/ppermute | solution.py:627
  10.7 0.0 collective-permute-done.2.from_outer
  10.7 0.2 shard_map.89
  10.9 1.3 %collective-permute-start.5 = (f32[8,128]{1,0:T(8,128)S(1)}, f32[8,128]{1,0:T(8,128)S(1)}, u32[]{:S(2)}, u32[]{:S(2)}) collective-permute-start(f32[8,128]{1,0:T(8,128)S(1)} %get-tuple-element.46), channel_id=1, source_target_pairs={{0,8},{1,9},{2,10},{3,11},{4,12},{5,13},{6,14},{7,15},{8,0},{9,1},... | collective-permute-start | bytes 12296 | tf_op jit(solution)/shard_map/ppermute | solution.py:627
  12.2 0.2 collective-permute-start.6
  12.4 5.3 %shard_map.90 = (f32[20,20,8,128]{3,2,1,0:T(8,128)S(1)}, f32[20,20,8,128]{3,2,1,0:T(8,128)S(1)}) custom-call(f32[20,20,8,128]{3,2,1,0:T(8,128)S(1)} %get-tuple-element.36.m0.m_own, f32[3,20,8,128]{3,2,1,0:T(8,128)S(1)} %get-tuple-element.37.dv.dv_own, bf16[256,256]{1,0:T(8,128)(2,1)S(1)} %get-tuple-element.38.mix, f32[20,8,128]{2,1,0:T(8,128)S(1)} %get-tuple-element.39.g0, ...), custom_call_target="tpu_custom_call" | custom-call | flops 20000000000 | bytes 83886080 | tf_op jit(solution)/shard_map/pallas_call | solution.py:588
  17.6 0.0 collective-permute-done.5.edge_a
  17.7 0.8 %collective-permute-done.6.edge_b = f32[8,128]{1,0:T(8,128)S(1)} collective-permute-done((f32[8,128]{1,0:T(8,128)S(1)}, f32[8,128]{1,0:T(8,128)S(1)}, u32[]{:S(2)}, u32[]{:S(2)}) %collective-permute-start.6) | collective-permute-done | bytes 4128 | tf_op jit(solution)/shard_map/ppermute | solution.py:627
  18.4 0.0 collective-permute-done.3.rows_a
  18.4 0.0 collective-permute-done.4.rows_b
  18.4 2.7 %shard_map.91 = (f32[16,4,8,128]{3,2,1,0:T(8,128)S(1)}, f32[3,8,8,128]{3,2,1,0:T(8,128)S(1)}, f32[3,8,8,128]{3,2,1,0:T(8,128)S(1)}) custom-call(f32[20,20,8,128]{3,2,1,0:T(8,128)S(1)} %get-tuple-element.36.m0.m_own, f32[3,20,8,128]{3,2,1,0:T(8,128)S(1)} %get-tuple-element.37.dv.dv_own, bf16[256,256]{1,0:T(8,128)(2,1)S(1)} %get-tuple-element.38.mix, ...), custom_call_target="tpu_custom_call" | custom-call | flops 1000000000 | bytes 4194304 | tf_op jit(solution)/shard_map/pallas_call | solution.py:588
  21.2 1.2 %collective-permute-start.7 = (f32[3,8,8,128]{3,2,1,0:T(8,128)S(1)}, f32[3,8,8,128]{3,2,1,0:T(8,128)S(1)}, u32[]{:S(2)}, u32[]{:S(2)}) collective-permute-start(f32[3,8,8,128]{3,2,1,0:T(8,128)S(1)} %get-tuple-element.51), channel_id=1, source_target_pairs={{0,4},{1,5},{2,6},{3,7},{4,0},{5,1},{6,2},{7,3},{8,12},{9,13},{10,... | collective-permute-start | bytes 294920 | tf_op jit(solution)/shard_map/ppermute | solution.py:627
  22.4 1.3 %shard_map.93 = f32[16,8,16,128]{3,2,1,0:T(8,128)} custom-call(f32[16,4,8,128]{3,2,1,0:T(8,128)S(1)} %get-tuple-element.54.rim, f32[20,20,8,128]{3,2,1,0:T(8,128)S(1)} %get-tuple-element.49.m2_in.m), custom_call_target="tpu_custom_call" | custom-call | flops 1000000000 | bytes 4194304 | tf_op jit(solution)/shard_map/pallas_call | solution.py:588
  23.7 0.0 collective-permute-done.7.got
  23.7 0.8 %shard_map.92 = (f32[2,8,8,256]{3,2,1,0:T(8,128)}, f32[8,8,256]{2,1,0:T(8,128)}) custom-call(f32[3,8,8,128]{3,2,1,0:T(8,128)S(1)} %get-tuple-element.50.keep, f32[3,8,8,128]{3,2,1,0:T(8,128)S(1)} %collective-permute-done.7.got), custom_call_target="tpu_custom_call" | custom-call | flops 1000000000 | bytes 4194304 | tf_op jit(solution)/shard_map/pallas_call | solution.py:588
Async XLA Ops:
  1.8 2.6 %collective-permute-start = (f32[36,8,128]{2,1,0:T(8,128)S(1)}, f32[36,8,128]{2,1,0:T(8,128)S(1)}, u32[]{:S(2)}, u32[]{:S(2)}) collective-permute-start(f32[36,8,128]{2,1,0:T(8,128)S(1)} %get-tuple-element.31.to_partner), channel_id=1, source_target_pairs={{0,4},{1,5},{2,6},{3,7},{4,0},{5,1},{6,2},{7,3},{8,12},{9,13},{10,... | collective-permute-start | bytes 442376 | tf_op jit(solution)/shard_map/ppermute | solution.py:627
  3.9 3.6 %collective-permute-start.1 = (f32[16,8,128]{2,1,0:T(8,128)S(1)}, f32[16,8,128]{2,1,0:T(8,128)S(1)}, u32[]{:S(2)}, u32[]{:S(2)}) collective-permute-start(f32[16,8,128]{2,1,0:T(8,128)S(1)} %get-tuple-element.32.g_tracers), channel_id=1, source_target_pairs={{0,4},{1,5},{2,6},{3,7},{4,0},{5,1},{6,2},{7,3},{8,12},{9,13},{10,... | collective-permute-start | bytes 196616 | tf_op jit(solution)/shard_map/ppermute | solution.py:627
  4.4 3.1 %copy-start = (f32[16,16]{1,0:T(8,128)S(1)}, f32[16,16]{1,0:T(8,128)}, u32[]{:S(2)}) copy-start(f32[16,16]{1,0:T(8,128)} %rates.1) | copy-start | bytes 3076
  4.7 6.0 %collective-permute-start.2 = (f32[5,8,128]{2,1,0:T(8,128)S(1)}, f32[5,8,128]{2,1,0:T(8,128)S(1)}, u32[]{:S(2)}, u32[]{:S(2)}) collective-permute-start(f32[5,8,128]{2,1,0:T(8,128)S(1)} %get-tuple-element.42), channel_id=1, source_target_pairs={{0,8},{1,4},{2,5},{3,6},{4,1},{5,2},{6,3},{7,15},{8,0},{9,12},{10,... | collective-permute-start | bytes 61448 | tf_op jit(solution)/shard_map/ppermute | solution.py:627
  8.2 10.2 %collective-permute-start.3 = (f32[40,8,128]{2,1,0:T(8,128)S(1)}, f32[40,8,128]{2,1,0:T(8,128)S(1)}, u32[]{:S(2)}, u32[]{:S(2)}) collective-permute-start(f32[40,8,128]{2,1,0:T(8,128)S(1)} %get-tuple-element.44), channel_id=1, source_target_pairs={{0,8},{1,9},{2,10},{3,11},{4,12},{5,13},{6,14},{7,15},{8,0},{9,1},... | collective-permute-start | bytes 491528 | tf_op jit(solution)/shard_map/ppermute | solution.py:627
  9.5 8.9 %collective-permute-start.4 = (f32[40,8,128]{2,1,0:T(8,128)S(1)}, f32[40,8,128]{2,1,0:T(8,128)S(1)}, u32[]{:S(2)}, u32[]{:S(2)}) collective-permute-start(f32[40,8,128]{2,1,0:T(8,128)S(1)} %get-tuple-element.45), channel_id=1, source_target_pairs={{0,24},{1,25},{2,26},{3,27},{4,28},{5,29},{6,30},{7,31},{8,16},{9,... | collective-permute-start | bytes 491528 | tf_op jit(solution)/shard_map/ppermute | solution.py:627
  10.9 6.7 %collective-permute-start.5 = (f32[8,128]{1,0:T(8,128)S(1)}, f32[8,128]{1,0:T(8,128)S(1)}, u32[]{:S(2)}, u32[]{:S(2)}) collective-permute-start(f32[8,128]{1,0:T(8,128)S(1)} %get-tuple-element.46), channel_id=1, source_target_pairs={{0,8},{1,9},{2,10},{3,11},{4,12},{5,13},{6,14},{7,15},{8,0},{9,1},... | collective-permute-start | bytes 12296 | tf_op jit(solution)/shard_map/ppermute | solution.py:627
  12.2 6.2 %collective-permute-start.6 = (f32[8,128]{1,0:T(8,128)S(1)}, f32[8,128]{1,0:T(8,128)S(1)}, u32[]{:S(2)}, u32[]{:S(2)}) collective-permute-start(f32[8,128]{1,0:T(8,128)S(1)} %get-tuple-element.47), channel_id=1, source_target_pairs={{0,24},{1,25},{2,26},{3,27},{4,28},{5,29},{6,30},{7,31},{8,16},{9,... | collective-permute-start | bytes 12296 | tf_op jit(solution)/shard_map/ppermute | solution.py:627
  21.2 2.5 %collective-permute-start.7 = (f32[3,8,8,128]{3,2,1,0:T(8,128)S(1)}, f32[3,8,8,128]{3,2,1,0:T(8,128)S(1)}, u32[]{:S(2)}, u32[]{:S(2)}) collective-permute-start(f32[3,8,8,128]{3,2,1,0:T(8,128)S(1)} %get-tuple-element.51), channel_id=1, source_target_pairs={{0,4},{1,5},{2,6},{3,7},{4,0},{5,1},{6,2},{7,3},{8,12},{9,13},{10,... | collective-permute-start | bytes 294920 | tf_op jit(solution)/shard_map/ppermute | solution.py:627

commit v5 on v4

--- a/solution.py
+++ b/solution.py
@@ -58,9 +58,19 @@
     return ((1 - odd) * (lat_blk - 2), odd * (lat_blk - 2))
 
 
-def pack_ocean_kernel(surface, mine, to_partner, g_other):
+def pack_ocean_kernel(flow_in, temp_in, bottom_in, sunlight_in, tracers_in, mine, to_partner, g_other, tracers, flow, temp, bottom, sunlight, sem):
+    copies = [
+        pltpu.make_async_copy(src, dst, sem.at[i])
+        for i, (src, dst) in enumerate(
+            ((flow_in, flow), (temp_in, temp), (bottom_in, bottom), (sunlight_in, sunlight), (tracers_in, tracers))
+        )
+    ]
+    for copy in copies:
+        copy.start()
+    for copy in copies[:-1]:
+        copy.wait()
     lat_dev, nz, lon = mine.shape[1:]
-    lon_dev = surface.shape[2]
+    lon_dev = temp.shape[2]
     half, _, _ = place()
     first = half == 0
     zero = jnp.zeros((nz, lon), jnp.float32)
@@ -68,11 +78,11 @@
     own = [zero] * EXTRA
     far = [zero] * EXTRA
     for t in range(lat_dev):
-        depth = jnp.broadcast_to(surface[3 * nz, t : t + 1, :], (nz, lon_dev))
-        light = jnp.broadcast_to(surface[3 * nz + 1, t : t + 1, :], (nz, lon_dev))
-        wet = (level.astype(jnp.float32) < depth).astype(jnp.float32)
-        aux = jnp.where(level == 0, depth, jnp.where(level == 1, light, 0.0))
-        for f, tile in enumerate([surface[f * nz : (f + 1) * nz, t, :] * wet for f in range(3)] + [aux]):
+        depth = jnp.broadcast_to(bottom[t : t + 1, :], (nz, lon_dev))
+        light = jnp.broadcast_to(sunlight[t : t + 1, :], (nz, lon_dev))
+        wet = (level < depth).astype(jnp.float32)
+        aux = jnp.where(level == 0, depth.astype(jnp.float32), jnp.where(level == 1, light, 0.0))
+        for f, tile in enumerate((flow[0, :, t, :] * wet, flow[1, :, t, :] * wet, temp[:, t, :] * wet, aux)):
             low, high = (tile[:, :lon], tile[:, lon:])
             a, b = (jnp.where(first, low, high), jnp.where(first, high, low))
             mine[f, t] = a
@@ -83,18 +93,13 @@
     for f in range(EXTRA):
         to_partner[EXTRA * lat_dev + f] = pltpu.roll(own[f], shift, 1)
         g_other[f] = pltpu.roll(far[f], shift, 1)
-
-
-def pack_tracers_kernel(tracers_in, turned, g_tracers, tracers, sem):
+    copies[-1].wait()
+
+
+def pack_tracers_kernel(tracers, turned, g_tracers):
     ntr, nz, lat_blk, lon = tracers.shape
-    copies = [
-        pltpu.make_async_copy(tracers_in.at[pl.ds(n, GROUP)], tracers.at[pl.ds(n, GROUP)], sem.at[n // GROUP])
-        for n in range(0, ntr, GROUP)
-    ]
-    for copy in copies:
-        copy.start()
-    for i, copy in enumerate(copies):
-        copy.wait()
+
+    def some(i, _):
         g = [jnp.zeros((nz, lon), jnp.float32)] * GROUP
         for t in range(lat_blk):
             for k in range(GROUP):
@@ -103,6 +108,9 @@
                 g[k] = window(x, t, g[k])
         for k in range(GROUP):
             g_tracers[i * GROUP + k] = g[k]
+        return 0
+
+    lax.fori_loop(0, ntr // GROUP, some, 0)
 
 
 def in_half(shape, half, lat_dev):
@@ -302,6 +310,7 @@
 
 KAP, PRS, WET = (0, 1, 2)
 GROUP = 4
+PIECE = 3
 
 
 def span(start, stop):
@@ -311,19 +320,16 @@
 def chunks(rows, most, body):
     first, apart, times, size = rows
     count = max(k for k in range(1, min(most, size) + 1) if size % k == 0)
-    if times == 1:
-        apart, times = (count, size // count)
-    elif count < size:
-        raise ValueError(rows)
-
-    def one(i, _):
-        body(first + i * apart, count)
-        return 0
-
-    if times == 1:
-        body(first, count)
+    if times > 1 or count == size:
+        for i in range(times):
+            body(first + i * apart, size)
     else:
-        lax.fori_loop(0, times, one, 0)
+
+        def one(i, _):
+            body(first + i * count, count)
+            return 0
+
+        lax.fori_loop(0, size // count, one, 0)
 
 
 def derive_rows(m, dv, ntr, rows):
@@ -360,49 +366,60 @@
     chunks(rows, 9, body)
 
 
-def tracer_rows(m, z, wts, new, sat, ntr, rows):
+def tracer_rows(m, z, wts, dv, mix, moved, sat, new, ntr, rows):
     nz, lon = m.shape[2:]
     half = ntr * nz
-
-    def row(r):
+    first, apart, times, count = rows
+    if times == 1:
+        count = max(k for k in range(1, PIECE + 1) if rows[3] % k == 0)
+        apart, times = (count, rows[3] // count)
+
+    def move(r):
         weights = [wts[i, r] for i in range(7)]
         for n in range(0, ntr, GROUP):
             x = m[n : n + GROUP, r]
             edge = beside(z[n : n + GROUP], r, lon)
-            moved = transport(weights, x, *sides(x, edge), m[n : n + GROUP, r + 1], m[n : n + GROUP, r - 1])
-            new[n : n + GROUP, r] = moved
-            high, low = two_parts(saturated(moved).reshape(GROUP * nz, lon))
+            done = transport(weights, x, *sides(x, edge), m[n : n + GROUP, r + 1], m[n : n + GROUP, r - 1])
+            moved[n : n + GROUP, r] = done
+            high, low = two_parts(saturated(done).reshape(GROUP * nz, lon))
             sat[r, n * nz : (n + GROUP) * nz, :] = high
             sat[r, half + n * nz : half + (n + GROUP) * nz, :] = low
         h = ntr + 2
         x = m[h, r]
-        new[h, r] = transport(weights, x, *sides(x, beside(z[h], r, lon)), m[h, r + 1], m[h, r - 1])
-
-    def body(r, count):
+        moved[ntr, r] = transport(weights, x, *sides(x, beside(z[h], r, lon)), m[h, r + 1], m[h, r - 1])
+
+    def react(r):
+        both = jnp.concatenate([sat[r + i] for i in range(count)], axis=1)
+        res = jnp.dot(mix[...], both, preferred_element_type=jnp.float32)
+        res = res[:half] + res[half:]
         for i in range(count):
-            row(r + i)
-
-    chunks(rows, 3, body)
-
-
-def react_rows(dv, mix, new, sat, ntr, rows):
-    nz, lon = new.shape[2:]
-    half = ntr * nz
-    first, apart, times, size = rows
-    every = [first + i * apart + k for i in range(times) for k in range(size)]
-    both = jnp.concatenate([sat[r] for r in every], axis=1)
-    res = jnp.dot(mix[...], both, preferred_element_type=jnp.float32)
-    res = res[:half] + res[half:]
-    for i, r in enumerate(every):
-        gain = react_step * dv[WET, r]
-        for n in range(ntr):
-            new[n, r] = new[n, r] + gain * res[n * nz : (n + 1) * nz, i * lon : (i + 1) * lon]
-
-
-def light_rows(m, dv, new, ntr, rows):
+            gain = react_step * dv[WET, r + i]
+            for n in range(ntr):
+                new[n, r + i] = moved[n, r + i] + gain * res[n * nz : (n + 1) * nz, i * lon : (i + 1) * lon]
+
+    def move_all(r):
+        for i in range(count):
+            move(r + i)
+
+    def both_parts(i, _):
+        react(first + (i - 1) * apart)
+        move_all(first + i * apart)
+        return 0
+
+    move_all(first)
+    if rows[2] > 1:
+        for i in range(1, times):
+            both_parts(i, 0)
+    else:
+        lax.fori_loop(1, times, both_parts, 0)
+    react(first + (times - 1) * apart)
+
+
+def light_rows(m, dv, moved, new, ntr, rows):
     def body(r, count):
         at = pl.ds(r, count)
-        new[ntr + 2, at] += heat_gain * light_of(m[ntr + 3, at]) * dv[WET, at] * absorbed(new[0, at])
+        light = light_of(m[ntr + 3, at]) * dv[WET, at] * absorbed(new[0, at])
+        new[ntr + 2, at] = moved[ntr, at] + heat_gain * light
 
     chunks(rows, 9, body)
 
@@ -472,27 +489,25 @@
     derive_columns(z, zd, ntr)
 
 
-def inner_kernel(m0, dv, mix, g0, gd, z_in, m1, m2, dv1, wts, sat, z0, z1, zd):
+def inner_kernel(m0, dv, mix, g0, gd, z_in, m1, m2, dv1, wts, sat, moved, z0, z1, zd):
     nf, rows, _, _ = m0.shape
     ntr = nf - EXTRA
     mask_columns([z_in[f] for f in range(nf)], z0, zd)
     column_step(z0, g0, zd, gd, z1, mix, ntr, rows - 4)
     now = span(3, rows - 3)
     ocean_rows(m0, dv, z0, zd, wts, m1, ntr, now)
-    tracer_rows(m0, z0, wts, m1, sat, ntr, now)
-    react_rows(dv, mix, m1, sat, ntr, now)
-    light_rows(m0, dv, m1, ntr, now)
+    tracer_rows(m0, z0, wts, dv, mix, moved, sat, m1, ntr, now)
+    light_rows(m0, dv, moved, m1, ntr, now)
     dv1[WET, 3 : rows - 3] = dv[WET, 3 : rows - 3]
     derive_rows(m1, dv1, ntr, now)
     derive_columns(z1, zd, ntr)
     now = span(4, rows - 4)
     ocean_rows(m1, dv1, z1, zd, wts, m2, ntr, now)
-    tracer_rows(m1, z1, wts, m2, sat, ntr, now)
-    react_rows(dv1, mix, m2, sat, ntr, now)
-    light_rows(m0, dv1, m2, ntr, now)
-
-
-def outer_kernel(m_own, dv_own, mix, g0, gd, z_in, rows_a, rows_b, edge_a, edge_b, m1_in, m2_in, rim, keep, send, m0, m1, dv0, dv1, wts, sat, z0, z1, zd):
+    tracer_rows(m1, z1, wts, dv1, mix, moved, sat, m2, ntr, now)
+    light_rows(m0, dv1, moved, m2, ntr, now)
+
+
+def outer_kernel(m_own, dv_own, mix, g0, gd, z_in, rows_a, rows_b, edge_a, edge_b, m1_in, m2_in, rim, keep, send, m0, m1, dv0, dv1, wts, sat, moved, z0, z1, zd):
     nf, rows, nz, lon = m_own.shape
     ntr = nf - EXTRA
     lat_blk = rows - 4
@@ -527,9 +542,8 @@
     column_step(z0, g0, zd, gd, z1, mix, ntr, lat_blk)
     now = (1, lat_blk, 2, 2)
     ocean_rows(m0, dv0, z0, zd, wts, m1, ntr, now)
-    tracer_rows(m0, z0, wts, m1, sat, ntr, now)
-    react_rows(dv0, mix, m1, sat, ntr, now)
-    light_rows(m0, dv0, m1, ntr, now)
+    tracer_rows(m0, z0, wts, dv0, mix, moved, sat, m1, ntr, now)
+    light_rows(m0, dv0, moved, m1, ntr, now)
     for start in (3, rows - 5):
         m1[:, start : start + 2] = m1_in[:, start : start + 2]
     for start in (1, rows - 3):
@@ -540,9 +554,8 @@
     derive_columns(z1, zd, ntr)
     now = (2, rows - 6, 2, 2)
     ocean_rows(m1, dv1, z1, zd, wts, m0, ntr, now)
-    tracer_rows(m1, z1, wts, m0, sat, ntr, now)
-    react_rows(dv1, mix, m0, sat, ntr, now)
-    light_rows(m0, dv1, m0, ntr, now)
+    tracer_rows(m1, z1, wts, dv1, mix, moved, sat, m0, ntr, now)
+    light_rows(m0, dv1, moved, m0, ntr, now)
 
     rim[:, 0:2] = m0[:ntr, 2:4]
     rim[:, 2:4] = m0[:ntr, rows - 4 : rows - 2]
@@ -612,8 +625,8 @@
         outer += [(dev(p, 0, 0), dev(p + 1, 0, 0)), (dev(p, 1, n_col - 1), dev(p + 1, 1, n_col - 1))]
     lat_a = [(dev(p, h, c), dev(p + 1, h, c)) for p in range(0, chips - 1, 2) for h in (0, 1) for c in range(n_col)]
     lat_b = [(dev(p, h, c), dev(p + 1, h, c)) for p in range(1, chips - 1, 2) for h in (0, 1) for c in range(n_col)]
-    if chips % 2 == 0 and chips > 2:
-        lat_b += [(dev(0, h, c), dev(chips - 1, h, c)) for h in (0, 1) for c in range(n_col)]
+    ends = [0] if chips % 2 else [0, chips - 1]
+    lat_b += [(dev(p, 0, c), dev(p, 1, c)) for p in ends for c in range(n_col)]
     return [both_ways(x) for x in (partner, outer, lat_a, lat_b)]
 
 
@@ -627,27 +640,26 @@
         return lax.ppermute(x, ("row", "col"), pairs)
 
     block = tracers[0]
-    parts = [flow.reshape(-1, lat_dev, lon_dev), temp, bottom[None], sunlight[None]]
-    total = sum(part.shape[0] for part in parts)
-    surface, start = (0.0, 0)
-    for part in parts:
-        count = part.shape[0]
-        surface = surface + jnp.pad(part, ((start, total - start - count), (0, 0), (0, 0))).astype(jnp.float32)
-        start += count
     rows = lat_blk + 4
     cols, extra, some = ((nf, nz, lon), (EXTRA, nz, lon), (3, nz, lon))
     copies = pltpu.SemaphoreType.DMA((ntr // GROUP,))
     sent = (EXTRA * (lat_dev + 1), nz, lon)
-    mine, to_partner, g_other = call(pack_ocean_kernel, [(EXTRA, lat_dev, nz, lon), sent, extra], surface)
+    given = (flow, temp, bottom, sunlight, block)
+    mine, to_partner, g_other, block = call(
+        pack_ocean_kernel,
+        [(EXTRA, lat_dev, nz, lon), sent, extra, block.shape],
+        *[pltpu.with_memory_space_constraint(x, pltpu.HBM) for x in given],
+        scratch=[
+            flow.shape,
+            temp.shape,
+            pltpu.VMEM(bottom.shape, jnp.int32),
+            sunlight.shape,
+            pltpu.SemaphoreType.DMA((len(given),)),
+        ],
+        held=False,
+    )
     got = swap(to_partner, partner)
-    turned, g_tracers = call(
-        pack_tracers_kernel,
-        [(ntr, lat_blk, nz, lon), (ntr, nz, lon)],
-        block,
-        scratch=[block.shape, copies],
-        held=False,
-        limit=52,
-    )
+    turned, g_tracers = call(pack_tracers_kernel, [(ntr, lat_blk, nz, lon), (ntr, nz, lon)], block)
     ocean, g_own, to_outer = call(
         join_kernel, [(EXTRA, lat_blk, nz, lon), cols, (nf // 4, nz, lon)], mine, got, to_partner, g_tracers
     )
@@ -671,7 +683,8 @@
         functools.partial(edge_kernel, lat_blk), [cols, (nz, lon), (nz, lon)], inner, from_outer
     )
     edge_a, edge_b = (swap(edge_a, lat_a), swap(edge_b, lat_b))
-    work = [(7, rows, nz, lon), pltpu.VMEM((rows, 2 * ntr * nz, lon), jnp.bfloat16), cols, cols, some]
+    work = [(7, rows, nz, lon), pltpu.VMEM((rows, 2 * ntr * nz, lon), jnp.bfloat16)]
+    work += [(ntr + 1, rows, nz, lon), cols, cols, some]
     m1, m2 = call(inner_kernel, [full, full], m0, dv, mix, g0, gd, z, scratch=[derived] + work, cost=20)
     third = (3, lat_dev, nz, lon)
     rim, keep, send = call(

time: 24.7 us -> 21.6 us (0.87)
  the two profiles are of different devices: /device:TPU:1 before, /device:TPU:3 now
where the time goes in v5:
time: 21.6 us; the launch traced here: 21.2 us
  Pallas kernels  12.2 us (56%)
  starting transfers between devices  6.3 us (29%)
  waiting for transfers between devices  2.02 us (9%)
  between operations  0.7 us (3%)
    pallas_call x9, Pallas kernels, call(): pl.pallas_call(kernel, out_shape=[jax.ShapeDtypeStruct(s, jnp.float32) if...  12.2 us
    ppermute x8, starting transfers between devices, swap(): return lax.ppermute(x, ('row', 'col'), pairs)  6.3 us
    ppermute x8, waiting for transfers between devices, swap(): return lax.ppermute(x, ('row', 'col'), pairs)  2.02 us
  transfers between devices with their start and end apart: 8, of which 2 were waited for; matrix products, arithmetic and copies ran while one was open for 0% of the time, Pallas kernels for 40%

profile of v5, /device:TPU:3, one launch (start us, length us, event | category | flops | bytes accessed | tf_op | source)
XLA Modules:
  0.0 21.2 jit_solution(8110127925335307275)
XLA Ops:
  0.6 1.4 %shard_map.85 = (f32[4,8,8,128]{3,2,1,0:T(8,128)S(1)}, f32[36,8,128]{2,1,0:T(8,128)S(1)}, f32[4,8,128]{2,1,0:T(8,128)S(1)}, f32[16,8,16,128]{3,2,1,0:T(8,128)S(1)}) custom-call(f32[2,8,8,256]{3,2,1,0:T(8,128)} %flow_in.1, f32[8,8,256]{2,1,0:T(8,128)} %temp_in.1, s32[8,256]{1,0:T(8,128)} %bottom_in.1, f32[8,256]{1,0:T(8,128)} %sunlight_in.1, ...), custom_call_target="tpu_custom_call" | custom-call | flops 1000000000 | bytes 4194304 | tf_op jit(solution)/shard_map/pallas_call | solution.py:601
  2.1 0.7 %collective-permute-start = (f32[36,8,128]{2,1,0:T(8,128)S(1)}, f32[36,8,128]{2,1,0:T(8,128)S(1)}, u32[]{:S(2)}, u32[]{:S(2)}) collective-permute-start(f32[36,8,128]{2,1,0:T(8,128)S(1)} %get-tuple-element.33.to_partner), channel_id=1, source_target_pairs={{0,4},{1,5},{2,6},{3,7},{4,0},{5,1},{6,2},{7,3},{8,12},{9,13},{10,... | collective-permute-start | bytes 442376 | tf_op jit(solution)/shard_map/ppermute | solution.py:640
  2.8 0.8 %shard_map.86 = (f32[16,16,8,128]{3,2,1,0:T(8,128)S(1)}, f32[16,8,128]{2,1,0:T(8,128)S(1)}) custom-call(f32[16,8,16,128]{3,2,1,0:T(8,128)S(1)} %get-tuple-element.30.tracers), custom_call_target="tpu_custom_call" | custom-call | flops 1000000000 | bytes 4194304 | tf_op jit(solution)/shard_map/pallas_call | solution.py:601
  3.6 0.1 collective-permute-start.1
  3.7 0.1 collective-permute-done.got
  3.8 0.0 copy-start
  3.8 0.3 %shard_map.87 = (f32[4,16,8,128]{3,2,1,0:T(8,128)S(1)}, f32[20,8,128]{2,1,0:T(8,128)S(1)}, f32[5,8,128]{2,1,0:T(8,128)S(1)}) custom-call(f32[4,8,8,128]{3,2,1,0:T(8,128)S(1)} %get-tuple-element.32.mine, f32[36,8,128]{2,1,0:T(8,128)S(1)} %collective-permute-done.got, f32[36,8,128]{2,1,0:T(8,128)S(1)} %get-tuple-element.33.to_partner, ...), custom_call_target="tpu_custom_call" | custom-call | flops 1000000000 | bytes 4194304 | tf_op jit(solution)/shard_map/pallas_call | solution.py:601
  4.1 1.6 %collective-permute-start.2 = (f32[5,8,128]{2,1,0:T(8,128)S(1)}, f32[5,8,128]{2,1,0:T(8,128)S(1)}, u32[]{:S(2)}, u32[]{:S(2)}) collective-permute-start(f32[5,8,128]{2,1,0:T(8,128)S(1)} %get-tuple-element.44), channel_id=1, source_target_pairs={{0,8},{1,4},{2,5},{3,6},{4,1},{5,2},{6,3},{7,15},{8,0},{9,12},{10,... | collective-permute-start | bytes 61448 | tf_op jit(solution)/shard_map/ppermute | solution.py:640
  5.8 0.0 collective-permute-done.1.g_partner
  5.8 0.0 copy-done
  5.8 0.7 %shard_map.88 = (f32[40,8,128]{2,1,0:T(8,128)S(1)}, f32[40,8,128]{2,1,0:T(8,128)S(1)}, f32[20,20,8,128]{3,2,1,0:T(8,128)S(1)}, f32[3,20,8,128]{3,2,1,0:T(8,128)S...) custom-call(f32[16,16,8,128]{3,2,1,0:T(8,128)S(1)} %get-tuple-elemen, ...), custom_call_target="tpu_custom_call" | custom-call | flops 1000000000 | bytes 4194304 | tf_op jit(solution)/shard_map/pallas_call | solution.py:601
  6.5 0.3 %collective-permute-start.3 = (f32[40,8,128]{2,1,0:T(8,128)S(1)}, f32[40,8,128]{2,1,0:T(8,128)S(1)}, u32[]{:S(2)}, u32[]{:S(2)}) collective-permute-start(f32[40,8,128]{2,1,0:T(8,128)S(1)} %get-tuple-element.46), channel_id=1, source_target_pairs={{0,8},{1,9},{2,10},{3,11},{4,12},{5,13},{6,14},{7,15},{8,0},{9,1},... | collective-permute-start | bytes 491528 | tf_op jit(solution)/shard_map/ppermute | solution.py:640
  6.9 2.2 %collective-permute-start.4 = (f32[40,8,128]{2,1,0:T(8,128)S(1)}, f32[40,8,128]{2,1,0:T(8,128)S(1)}, u32[]{:S(2)}, u32[]{:S(2)}) collective-permute-start(f32[40,8,128]{2,1,0:T(8,128)S(1)} %get-tuple-element.47), channel_id=1, source_target_pairs={{0,4},{1,5},{2,6},{3,7},{4,0},{5,1},{6,2},{7,3},{8,16},{9,17},{10,... | collective-permute-start | bytes 491528 | tf_op jit(solution)/shard_map/ppermute | solution.py:640
  9.0 0.0 collective-permute-done.2.from_outer
  9.0 0.2 shard_map.89
  9.2 0.1 collective-permute-start.5
  9.3 0.8 %collective-permute-start.6 = (f32[8,128]{1,0:T(8,128)S(1)}, f32[8,128]{1,0:T(8,128)S(1)}, u32[]{:S(2)}, u32[]{:S(2)}) collective-permute-start(f32[8,128]{1,0:T(8,128)S(1)} %get-tuple-element.49), channel_id=1, source_target_pairs={{0,4},{1,5},{2,6},{3,7},{4,0},{5,1},{6,2},{7,3},{8,16},{9,17},{10,... | collective-permute-start | bytes 12296 | tf_op jit(solution)/shard_map/ppermute | solution.py:640
  10.1 5.0 %shard_map.90 = (f32[20,20,8,128]{3,2,1,0:T(8,128)S(1)}, f32[20,20,8,128]{3,2,1,0:T(8,128)S(1)}) custom-call(f32[20,20,8,128]{3,2,1,0:T(8,128)S(1)} %get-tuple-element.38.m0.m_own, f32[3,20,8,128]{3,2,1,0:T(8,128)S(1)} %get-tuple-element.39.dv.dv_own, bf16[256,256]{1,0:T(8,128)(2,1)S(1)} %get-tuple-element.40.mix, f32[20,8,128]{2,1,0:T(8,128)S(1)} %get-tuple-element.41.g0, ...), custom_call_target="tpu_custom_call" | custom-call | flops 20000000000 | bytes 83886080 | tf_op jit(solution)/shard_map/pallas_call | solution.py:601
  15.2 0.0 collective-permute-done.5.edge_a
  15.2 1.9 %collective-permute-done.6.edge_b = f32[8,128]{1,0:T(8,128)S(1)} collective-permute-done((f32[8,128]{1,0:T(8,128)S(1)}, f32[8,128]{1,0:T(8,128)S(1)}, u32[]{:S(2)}, u32[]{:S(2)}) %collective-permute-start.6) | collective-permute-done | bytes 4128 | tf_op jit(solution)/shard_map/ppermute | solution.py:640
  17.1 0.0 collective-permute-done.3.rows_a
  17.1 0.0 collective-permute-done.4.rows_b
  17.1 1.5 %shard_map.91 = (f32[16,4,8,128]{3,2,1,0:T(8,128)S(1)}, f32[3,8,8,128]{3,2,1,0:T(8,128)S(1)}, f32[3,8,8,128]{3,2,1,0:T(8,128)S(1)}) custom-call(f32[20,20,8,128]{3,2,1,0:T(8,128)S(1)} %get-tuple-element.38.m0.m_own, f32[3,20,8,128]{3,2,1,0:T(8,128)S(1)} %get-tuple-element.39.dv.dv_own, bf16[256,256]{1,0:T(8,128)(2,1)S(1)} %get-tuple-element.40.mix, ...), custom_call_target="tpu_custom_call" | custom-call | flops 1000000000 | bytes 4194304 | tf_op jit(solution)/shard_map/pallas_call | solution.py:601
  18.6 0.5 %collective-permute-start.7 = (f32[3,8,8,128]{3,2,1,0:T(8,128)S(1)}, f32[3,8,8,128]{3,2,1,0:T(8,128)S(1)}, u32[]{:S(2)}, u32[]{:S(2)}) collective-permute-start(f32[3,8,8,128]{3,2,1,0:T(8,128)S(1)} %get-tuple-element.53), channel_id=1, source_target_pairs={{0,4},{1,5},{2,6},{3,7},{4,0},{5,1},{6,2},{7,3},{8,12},{9,13},{10,... | collective-permute-start | bytes 294920 | tf_op jit(solution)/shard_map/ppermute | solution.py:640
  19.1 1.3 %shard_map.93 = f32[16,8,16,128]{3,2,1,0:T(8,128)} custom-call(f32[16,4,8,128]{3,2,1,0:T(8,128)S(1)} %get-tuple-element.56.rim, f32[20,20,8,128]{3,2,1,0:T(8,128)S(1)} %get-tuple-element.51.m2_in.m), custom_call_target="tpu_custom_call" | custom-call | flops 1000000000 | bytes 4194304 | tf_op jit(solution)/shard_map/pallas_call | solution.py:601
  20.4 0.0 collective-permute-done.7.got
  20.4 0.8 %shard_map.92 = (f32[2,8,8,256]{3,2,1,0:T(8,128)}, f32[8,8,256]{2,1,0:T(8,128)}) custom-call(f32[3,8,8,128]{3,2,1,0:T(8,128)S(1)} %get-tuple-element.52.keep, f32[3,8,8,128]{3,2,1,0:T(8,128)S(1)} %collective-permute-done.7.got), custom_call_target="tpu_custom_call" | custom-call | flops 1000000000 | bytes 4194304 | tf_op jit(solution)/shard_map/pallas_call | solution.py:601
Async XLA Ops:
  2.1 1.7 %collective-permute-start = (f32[36,8,128]{2,1,0:T(8,128)S(1)}, f32[36,8,128]{2,1,0:T(8,128)S(1)}, u32[]{:S(2)}, u32[]{:S(2)}) collective-permute-start(f32[36,8,128]{2,1,0:T(8,128)S(1)} %get-tuple-element.33.to_partner), channel_id=1, source_target_pairs={{0,4},{1,5},{2,6},{3,7},{4,0},{5,1},{6,2},{7,3},{8,12},{9,13},{10,... | collective-permute-start | bytes 442376 | tf_op jit(solution)/shard_map/ppermute | solution.py:640
  3.6 2.1 %collective-permute-start.1 = (f32[16,8,128]{2,1,0:T(8,128)S(1)}, f32[16,8,128]{2,1,0:T(8,128)S(1)}, u32[]{:S(2)}, u32[]{:S(2)}) collective-permute-start(f32[16,8,128]{2,1,0:T(8,128)S(1)} %get-tuple-element.34.g_tracers), channel_id=1, source_target_pairs={{0,4},{1,5},{2,6},{3,7},{4,0},{5,1},{6,2},{7,3},{8,12},{9,13},{10,... | collective-permute-start | bytes 196616 | tf_op jit(solution)/shard_map/ppermute | solution.py:640
  3.8 2.0 %copy-start = (f32[16,16]{1,0:T(8,128)S(1)}, f32[16,16]{1,0:T(8,128)}, u32[]{:S(2)}) copy-start(f32[16,16]{1,0:T(8,128)} %rates.1) | copy-start | bytes 3076
  4.1 4.9 %collective-permute-start.2 = (f32[5,8,128]{2,1,0:T(8,128)S(1)}, f32[5,8,128]{2,1,0:T(8,128)S(1)}, u32[]{:S(2)}, u32[]{:S(2)}) collective-permute-start(f32[5,8,128]{2,1,0:T(8,128)S(1)} %get-tuple-element.44), channel_id=1, source_target_pairs={{0,8},{1,4},{2,5},{3,6},{4,1},{5,2},{6,3},{7,15},{8,0},{9,12},{10,... | collective-permute-start | bytes 61448 | tf_op jit(solution)/shard_map/ppermute | solution.py:640
  6.5 10.6 %collective-permute-start.3 = (f32[40,8,128]{2,1,0:T(8,128)S(1)}, f32[40,8,128]{2,1,0:T(8,128)S(1)}, u32[]{:S(2)}, u32[]{:S(2)}) collective-permute-start(f32[40,8,128]{2,1,0:T(8,128)S(1)} %get-tuple-element.46), channel_id=1, source_target_pairs={{0,8},{1,9},{2,10},{3,11},{4,12},{5,13},{6,14},{7,15},{8,0},{9,1},... | collective-permute-start | bytes 491528 | tf_op jit(solution)/shard_map/ppermute | solution.py:640
  6.9 10.2 %collective-permute-start.4 = (f32[40,8,128]{2,1,0:T(8,128)S(1)}, f32[40,8,128]{2,1,0:T(8,128)S(1)}, u32[]{:S(2)}, u32[]{:S(2)}) collective-permute-start(f32[40,8,128]{2,1,0:T(8,128)S(1)} %get-tuple-element.47), channel_id=1, source_target_pairs={{0,4},{1,5},{2,6},{3,7},{4,0},{5,1},{6,2},{7,3},{8,16},{9,17},{10,... | collective-permute-start | bytes 491528 | tf_op jit(solution)/shard_map/ppermute | solution.py:640
  9.2 5.9 %collective-permute-start.5 = (f32[8,128]{1,0:T(8,128)S(1)}, f32[8,128]{1,0:T(8,128)S(1)}, u32[]{:S(2)}, u32[]{:S(2)}) collective-permute-start(f32[8,128]{1,0:T(8,128)S(1)} %get-tuple-element.48), channel_id=1, source_target_pairs={{0,8},{1,9},{2,10},{3,11},{4,12},{5,13},{6,14},{7,15},{8,0},{9,1},... | collective-permute-start | bytes 12296 | tf_op jit(solution)/shard_map/ppermute | solution.py:640
  9.3 7.8 %collective-permute-start.6 = (f32[8,128]{1,0:T(8,128)S(1)}, f32[8,128]{1,0:T(8,128)S(1)}, u32[]{:S(2)}, u32[]{:S(2)}) collective-permute-start(f32[8,128]{1,0:T(8,128)S(1)} %get-tuple-element.49), channel_id=1, source_target_pairs={{0,4},{1,5},{2,6},{3,7},{4,0},{5,1},{6,2},{7,3},{8,16},{9,17},{10,... | collective-permute-start | bytes 12296 | tf_op jit(solution)/shard_map/ppermute | solution.py:640
  18.6 1.8 %collective-permute-start.7 = (f32[3,8,8,128]{3,2,1,0:T(8,128)S(1)}, f32[3,8,8,128]{3,2,1,0:T(8,128)S(1)}, u32[]{:S(2)}, u32[]{:S(2)}) collective-permute-start(f32[3,8,8,128]{3,2,1,0:T(8,128)S(1)} %get-tuple-element.53), channel_id=1, source_target_pairs={{0,4},{1,5},{2,6},{3,7},{4,0},{5,1},{6,2},{7,3},{8,12},{9,13},{10,... | collective-permute-start | bytes 294920 | tf_op jit(solution)/shard_map/ppermute | solution.py:640

commit v6 on v5

--- a/solution.py
+++ b/solution.py
@@ -119,11 +119,19 @@
     return (lane >= base) & (lane < base + WIN * lat_dev)
 
 
-def join_kernel(mine, got, to_partner, g_tracers, ocean, g_own, to_outer):
+def edge_rows(turned, ocean, start, out):
+    ntr = turned.shape[0]
+    for n in range(ntr):
+        out[2 * n : 2 * n + 2] = turned[n, pl.ds(start, 2)]
+    for f in range(EXTRA):
+        out[2 * (ntr + f) : 2 * (ntr + f) + 2] = ocean[f, pl.ds(start, 2)]
+
+
+def join_kernel(mine, got, to_partner, g_tracers, turned, ocean, g_own, to_outer, rows_a):
     _, lat_dev, nz, lon = mine.shape
     ntr = g_tracers.shape[0]
     nf = ntr + EXTRA
-    half, _, _ = place()
+    half, chip, _ = place()
     tile = (nz, lon)
     own_lanes = in_half(tile, half, lat_dev)
     shift = (1 - half) * (WIN * lat_dev)
@@ -136,6 +144,7 @@
             ocean[f, (1 - half) * lat_dev + t] = x
             g = window(x, t, g)
         g_own[ntr + f] = jnp.where(own_lanes, to_partner[EXTRA * lat_dev + f], pltpu.roll(g, shift, 1))
+    edge_rows(turned, ocean, edge_starts(chip, 2 * lat_dev)[0], rows_a)
     lane = lanes_of(tile)
     front, near = (lane % WIN < 2, in_half(tile, 0, 2 * lat_dev))
     side = (1 - half) * (lon - 2)
@@ -146,8 +155,9 @@
         to_outer[i] = jnp.where(near, low, pltpu.roll(high, lon // 2, 1))
 
 
-def edge_kernel(lat_blk, inner, from_outer, z, to_a, to_b):
+def edge_kernel(turned, ocean, inner, from_outer, z, to_a, to_b):
     nf, nz, lon = z.shape
+    lat_blk = turned.shape[1]
 
     half, chip, column = place()
     tile = (nz, lon)
@@ -168,7 +178,8 @@
         corner_a = jnp.where(at, jnp.where(start_a > 0, high, low), corner_a)
         corner_b = jnp.where(at, jnp.where(start_b > 0, high, low), corner_b)
     to_a[...] = corner_a
-    to_b[...] = corner_b
+    edge_rows(turned, ocean, start_b, to_b)
+    to_b[2 * nf] = corner_b
 
 
 def kappa_of(u, v):
@@ -447,18 +458,13 @@
     z1[ntr + 2] = heat + heat_gain * light_of(z0[ntr + 3]) * wet * absorbed(done[0])
 
 
-def fill_kernel(turned, ocean, g_own, g_partner, got, g_other, rates, rows_a, rows_b, m0, dv, mix, g0, gd, inner):
+def fill_kernel(turned, ocean, g_own, g_partner, got, g_other, rates, m0, dv, mix, g0, gd, inner):
     ntr, lat_blk, nz, lon = turned.shape
-    half, chip, _ = place()
+    half, _, _ = place()
     inner[:ntr] = g_partner[...]
     for f in range(EXTRA):
         theirs = got[EXTRA * (lat_blk // 2) + f]
         inner[ntr + f] = jnp.where(in_half((nz, lon), half, lat_blk // 2), g_other[f], theirs)
-    for out, start in zip((rows_a, rows_b), edge_starts(chip, lat_blk)):
-        for n in range(ntr):
-            out[2 * n : 2 * n + 2] = turned[n, pl.ds(start, 2)]
-        for f in range(EXTRA):
-            out[2 * (ntr + f) : 2 * (ntr + f) + 2] = ocean[f, pl.ds(start, 2)]
     mix[...] = mix_matrix(rates[...], nz)
     own = span(2, lat_blk + 2)
 
@@ -507,7 +513,7 @@
     light_rows(m0, dv1, moved, m2, ntr, now)
 
 
-def outer_kernel(m_own, dv_own, mix, g0, gd, z_in, rows_a, rows_b, edge_a, edge_b, m1_in, m2_in, rim, keep, send, m0, m1, dv0, dv1, wts, sat, moved, z0, z1, zd):
+def outer_kernel(m_own, dv_own, mix, g0, gd, z_in, rows_a, rows_b, edge_a, m1_in, m2_in, rim, keep, send, m0, m1, dv0, dv1, wts, sat, moved, z0, z1, zd):
     nf, rows, nz, lon = m_own.shape
     ntr = nf - EXTRA
     lat_blk = rows - 4
@@ -515,24 +521,23 @@
     even = chip % 2 == 0
     south_ok, north_ok = (chip > 0, chip < lax.axis_size("row") // 2 - 1)
 
-    def got(high, a, b, index):
-        a, b = (a[index], b[index])
+    def got(high, a, b):
         picked = jnp.where(even, a, b) if high else jnp.where(even, b, a)
         return jnp.where(north_ok if high else south_ok, picked, 0.0)
 
     for high, start in ((False, 0), (True, rows - 2)):
         for f in range(EXTRA):
-            m0[ntr + f, start : start + 2] = got(high, rows_a, rows_b, pl.ds(2 * (ntr + f), 2))
+            m0[ntr + f, start : start + 2] = got(high, *(x[pl.ds(2 * (ntr + f), 2)] for x in (rows_a, rows_b)))
         wet = wet_of(m0[nf - 1, start : start + 2])
         dv0[WET, start : start + 2] = wet
         for n in range(ntr):
-            m0[n, start : start + 2] = got(high, rows_a, rows_b, pl.ds(2 * n, 2)) * wet
+            m0[n, start : start + 2] = got(high, *(x[pl.ds(2 * n, 2)] for x in (rows_a, rows_b))) * wet
         derive_rows(m0, dv0, ntr, span(start, start + 2))
     for start in (2, rows - 4):
         m0[:, start : start + 2] = m_own[:, start : start + 2]
         dv0[:, start : start + 2] = dv_own[:, start : start + 2]
     lane = lanes_of((nz, lon))
-    low, high = (got(False, edge_a, edge_b, ...), got(True, edge_a, edge_b, ...))
+    low, high = (got(side, edge_a[...], rows_b[2 * nf]) for side in (False, True))
     at_low, at_high = (lane < WIN, (lane >= WIN * (lat_blk + 1)) & (lane < WIN * (lat_blk + 2)))
     fields = []
     for f in range(nf):
@@ -660,16 +665,23 @@
     )
     got = swap(to_partner, partner)
     turned, g_tracers = call(pack_tracers_kernel, [(ntr, lat_blk, nz, lon), (ntr, nz, lon)], block)
-    ocean, g_own, to_outer = call(
-        join_kernel, [(EXTRA, lat_blk, nz, lon), cols, (nf // 4, nz, lon)], mine, got, to_partner, g_tracers
-    )
+    rim = (2 * nf, nz, lon)
+    ocean, g_own, to_outer, rows_a = call(
+        join_kernel,
+        [(EXTRA, lat_blk, nz, lon), cols, (nf // 4, nz, lon), rim],
+        mine,
+        got,
+        to_partner,
+        g_tracers,
+        turned,
+    )
+    rows_a = swap(rows_a, lat_a)
     from_outer = swap(to_outer, outer)
     g_partner = swap(g_tracers, partner)
     full, derived = ((nf, rows, nz, lon), (3, rows, nz, lon))
-    rim = (2 * nf, nz, lon)
-    rows_a, rows_b, m0, dv, mix, g0, gd, inner = call(
+    m0, dv, mix, g0, gd, inner = call(
         fill_kernel,
-        [rim, rim, full, derived, jax.ShapeDtypeStruct((2 * ntr * nz, 2 * ntr * nz), jnp.bfloat16), cols, some, cols],
+        [full, derived, jax.ShapeDtypeStruct((2 * ntr * nz, 2 * ntr * nz), jnp.bfloat16), cols, some, cols],
         turned,
         ocean,
         g_own,
@@ -678,11 +690,10 @@
         g_other,
         rates,
     )
-    rows_a, rows_b = (swap(rows_a, lat_a), swap(rows_b, lat_b))
-    z, edge_a, edge_b = call(
-        functools.partial(edge_kernel, lat_blk), [cols, (nz, lon), (nz, lon)], inner, from_outer
-    )
-    edge_a, edge_b = (swap(edge_a, lat_a), swap(edge_b, lat_b))
+    z, edge_a, rows_b = call(
+        edge_kernel, [cols, (nz, lon), (2 * nf + 1, nz, lon)], turned, ocean, inner, from_outer
+    )
+    rows_b, edge_a = (swap(rows_b, lat_b), swap(edge_a, lat_a))
     work = [(7, rows, nz, lon), pltpu.VMEM((rows, 2 * ntr * nz, lon), jnp.bfloat16)]
     work += [(ntr + 1, rows, nz, lon), cols, cols, some]
     m1, m2 = call(inner_kernel, [full, full], m0, dv, mix, g0, gd, z, scratch=[derived] + work, cost=20)
@@ -699,7 +710,6 @@
         rows_a,
         rows_b,
         edge_a,
-        edge_b,
         m1,
         m2,
         scratch=[full, full, derived, derived] + work,

time: 21.6 us -> 20.7 us (0.958); the launches traced: 21.2 us -> 20.5 us
  starting transfers between devices: 6.3 us -> 5.7 us
    ppermute x8 -> x7, starting transfers between devices: 6.3 us -> 5.7 us  [swap(): return lax.ppermute(x, ('row', 'col'), pairs)]
    ppermute x8 -> x7, waiting for transfers between devices: 2.02 us -> 1.98 us  [swap(): return lax.ppermute(x, ('row', 'col'), pairs)]
  transfers between devices with their start and end apart: 8 -> 7, of which waited for: 2 -> 3; matrix products, arithmetic and copies ran while one was open for 0% -> 0% of each run, Pallas kernels for 40% -> 41%
where the time goes in v6:
time: 20.7 us; the launch traced here: 20.5 us
  Pallas kernels  12.2 us (59%)
  starting transfers between devices  5.7 us (28%)
  waiting for transfers between devices  1.98 us (10%)
  between operations  0.7 us (3%)
    pallas_call x9, Pallas kernels, call(): pl.pallas_call(kernel, out_shape=[jax.ShapeDtypeStruct(s, jnp.float32) if...  12.2 us
    ppermute x7, starting transfers between devices, swap(): return lax.ppermute(x, ('row', 'col'), pairs)  5.7 us
    ppermute x7, waiting for transfers between devices, swap(): return lax.ppermute(x, ('row', 'col'), pairs)  1.98 us
  transfers between devices with their start and end apart: 7, of which 3 were waited for; matrix products, arithmetic and copies ran while one was open for 0% of the time, Pallas kernels for 41%

profile of v6, /device:TPU:3, one launch (start us, length us, event | category | flops | bytes accessed | tf_op | source)
XLA Modules:
  0.0 20.5 jit_solution(12383227564105819202)
XLA Ops:
  0.6 1.4 %shard_map.85 = (f32[4,8,8,128]{3,2,1,0:T(8,128)S(1)}, f32[36,8,128]{2,1,0:T(8,128)S(1)}, f32[4,8,128]{2,1,0:T(8,128)S(1)}, f32[16,8,16,128]{3,2,1,0:T(8,128)S(1)}) custom-call(f32[2,8,8,256]{3,2,1,0:T(8,128)} %flow_in.1, f32[8,8,256]{2,1,0:T(8,128)} %temp_in.1, s32[8,256]{1,0:T(8,128)} %bottom_in.1, f32[8,256]{1,0:T(8,128)} %sunlight_in.1, ...), custom_call_target="tpu_custom_call" | custom-call | flops 1000000000 | bytes 4194304 | tf_op jit(solution)/shard_map/pallas_call | solution.py:606
  2.1 0.7 %collective-permute-start = (f32[36,8,128]{2,1,0:T(8,128)S(1)}, f32[36,8,128]{2,1,0:T(8,128)S(1)}, u32[]{:S(2)}, u32[]{:S(2)}) collective-permute-start(f32[36,8,128]{2,1,0:T(8,128)S(1)} %get-tuple-element.32.to_partner), channel_id=1, source_target_pairs={{0,4},{1,5},{2,6},{3,7},{4,0},{5,1},{6,2},{7,3},{8,12},{9,13},{10,... | collective-permute-start | bytes 442376 | tf_op jit(solution)/shard_map/ppermute | solution.py:645
  2.8 0.8 %shard_map.86 = (f32[16,16,8,128]{3,2,1,0:T(8,128)S(1)}, f32[16,8,128]{2,1,0:T(8,128)S(1)}) custom-call(f32[16,8,16,128]{3,2,1,0:T(8,128)S(1)} %get-tuple-element.29.tracers), custom_call_target="tpu_custom_call" | custom-call | flops 1000000000 | bytes 4194304 | tf_op jit(solution)/shard_map/pallas_call | solution.py:606
  3.6 0.1 collective-permute-start.1
  3.7 0.1 collective-permute-done.got
  3.8 0.0 copy-start
  3.8 0.3 %shard_map.87 = (f32[4,16,8,128]{3,2,1,0:T(8,128)S(1)}, f32[20,8,128]{2,1,0:T(8,128)S(1)}, f32[5,8,128]{2,1,0:T(8,128)S(1)}, f32[40,8,128]{2,1,0:T(8,128)S(1)}) custom-call(f32[4,8,8,128]{3,2,1,0:T(8,128)S(1)} %get-tuple-element.31.mine, f32[36,8,128]{2,1,0:T(8,128)S(1)} %collective-permute-done.got, f32[36,8,128]{2,1,0:T(8,128)S(1)} %get-tuple-element.32.to_partner, ...), custom_call_target="tpu_custom_call" | custom-call | flops 1000000000 | bytes 4194304 | tf_op jit(solution)/shard_map/pallas_call | solution.py:606
  4.1 1.6 %collective-permute-start.2 = (f32[5,8,128]{2,1,0:T(8,128)S(1)}, f32[5,8,128]{2,1,0:T(8,128)S(1)}, u32[]{:S(2)}, u32[]{:S(2)}) collective-permute-start(f32[5,8,128]{2,1,0:T(8,128)S(1)} %get-tuple-element.43), channel_id=1, source_target_pairs={{0,8},{1,4},{2,5},{3,6},{4,1},{5,2},{6,3},{7,15},{8,0},{9,12},{10,... | collective-permute-start | bytes 61448 | tf_op jit(solution)/shard_map/ppermute | solution.py:645
  5.8 0.3 %collective-permute-start.3 = (f32[40,8,128]{2,1,0:T(8,128)S(1)}, f32[40,8,128]{2,1,0:T(8,128)S(1)}, u32[]{:S(2)}, u32[]{:S(2)}) collective-permute-start(f32[40,8,128]{2,1,0:T(8,128)S(1)} %get-tuple-element.45), channel_id=1, source_target_pairs={{0,8},{1,9},{2,10},{3,11},{4,12},{5,13},{6,14},{7,15},{8,0},{9,1},... | collective-permute-start | bytes 491528 | tf_op jit(solution)/shard_map/ppermute | solution.py:645
  6.0 0.0 collective-permute-done.1.g_partner
  6.0 0.0 copy-done
  6.0 0.7 %shard_map.88 = (f32[20,20,8,128]{3,2,1,0:T(8,128)S(1)}, f32[3,20,8,128]{3,2,1,0:T(8,128)S(1)}, bf16[256,256]{1,0:T(8,128)(2,1)S(1)}, f32[20,8,128]{2,1,0:T(8,12...) custom-call(f32[16,16,8,128]{3,2,1,0:T(8,128)S(1)} %get-tuple-element.30.turned, ...), custom_call_target="tpu_custom_call" | custom-call | flops 1000000000 | bytes 4194304 | tf_op jit(solution)/shard_map/pallas_call | solution.py:606
  6.8 0.6 %collective-permute-done.2.from_outer = f32[5,8,128]{2,1,0:T(8,128)S(1)} collective-permute-done((f32[5,8,128]{2,1,0:T(8,128)S(1)}, f32[5,8,128]{2,1,0:T(8,128)S(1)}, u32[]{:S(2)}, u32[]{:S(2)}) %collective-permute-start.2) | collective-permute-done | bytes 20512 | tf_op jit(solution)/shard_map/ppermute | solution.py:645
  7.4 0.2 shard_map.89
  7.6 0.7 %collective-permute-start.5 = (f32[8,128]{1,0:T(8,128)S(1)}, f32[8,128]{1,0:T(8,128)S(1)}, u32[]{:S(2)}, u32[]{:S(2)}) collective-permute-start(f32[8,128]{1,0:T(8,128)S(1)} %get-tuple-element.47), channel_id=1, source_target_pairs={{0,8},{1,9},{2,10},{3,11},{4,12},{5,13},{6,14},{7,15},{8,0},{9,1},... | collective-permute-start | bytes 12296 | tf_op jit(solution)/shard_map/ppermute | solution.py:645
  8.3 1.8 %collective-permute-start.4 = (f32[41,8,128]{2,1,0:T(8,128)S(1)}, f32[41,8,128]{2,1,0:T(8,128)S(1)}, u32[]{:S(2)}, u32[]{:S(2)}) collective-permute-start(f32[41,8,128]{2,1,0:T(8,128)S(1)} %get-tuple-element.46), channel_id=1, source_target_pairs={{0,4},{1,5},{2,6},{3,7},{4,0},{5,1},{6,2},{7,3},{8,16},{9,17},{10,... | collective-permute-start | bytes 503816 | tf_op jit(solution)/shard_map/ppermute | solution.py:645
  10.1 5.0 %shard_map.90 = (f32[20,20,8,128]{3,2,1,0:T(8,128)S(1)}, f32[20,20,8,128]{3,2,1,0:T(8,128)S(1)}) custom-call(f32[20,20,8,128]{3,2,1,0:T(8,128)S(1)} %get-tuple-element.37.m0.m_own, f32[3,20,8,128]{3,2,1,0:T(8,128)S(1)} %get-tuple-element.38.dv.dv_own, bf16[256,256]{1,0:T(8,128)(2,1)S(1)} %get-tuple-element.39.mix, f32[20,8,128]{2,1,0:T(8,128)S(1)} %get-tuple-element.40.g0, ...), custom_call_target="tpu_custom_call" | custom-call | flops 20000000000 | bytes 83886080 | tf_op jit(solution)/shard_map/pallas_call | solution.py:606
  15.1 0.0 collective-permute-done.5.edge_a
  15.1 0.0 collective-permute-done.3.rows_a
  15.1 1.3 %collective-permute-done.4.rows_b = f32[41,8,128]{2,1,0:T(8,128)S(1)} collective-permute-done((f32[41,8,128]{2,1,0:T(8,128)S(1)}, f32[41,8,128]{2,1,0:T(8,128)S(1)}, u32[]{:S(2)}, u32[]{:S(2)}) %collective-permute-start.4) | collective-permute-done | bytes 167968 | tf_op jit(solution)/shard_map/ppermute | solution.py:645
  16.4 1.5 %shard_map.91 = (f32[16,4,8,128]{3,2,1,0:T(8,128)S(1)}, f32[3,8,8,128]{3,2,1,0:T(8,128)S(1)}, f32[3,8,8,128]{3,2,1,0:T(8,128)S(1)}) custom-call(f32[20,20,8,128]{3,2,1,0:T(8,128)S(1)} %get-tuple-element.37.m0.m_own, f32[3,20,8,128]{3,2,1,0:T(8,128)S(1)} %get-tuple-element.38.dv.dv_own, bf16[256,256]{1,0:T(8,128)(2,1)S(1)} %get-tuple-element.39.mix, ...), custom_call_target="tpu_custom_call" | custom-call | flops 1000000000 | bytes 4194304 | tf_op jit(solution)/shard_map/pallas_call | solution.py:606
  17.9 0.5 %collective-permute-start.6 = (f32[3,8,8,128]{3,2,1,0:T(8,128)S(1)}, f32[3,8,8,128]{3,2,1,0:T(8,128)S(1)}, u32[]{:S(2)}, u32[]{:S(2)}) collective-permute-start(f32[3,8,8,128]{3,2,1,0:T(8,128)S(1)} %get-tuple-element.51), channel_id=1, source_target_pairs={{0,4},{1,5},{2,6},{3,7},{4,0},{5,1},{6,2},{7,3},{8,12},{9,13},{10,... | collective-permute-start | bytes 294920 | tf_op jit(solution)/shard_map/ppermute | solution.py:645
  18.4 1.3 %shard_map.93 = f32[16,8,16,128]{3,2,1,0:T(8,128)} custom-call(f32[16,4,8,128]{3,2,1,0:T(8,128)S(1)} %get-tuple-element.54.rim, f32[20,20,8,128]{3,2,1,0:T(8,128)S(1)} %get-tuple-element.49.m2_in.m), custom_call_target="tpu_custom_call" | custom-call | flops 1000000000 | bytes 4194304 | tf_op jit(solution)/shard_map/pallas_call | solution.py:606
  19.7 0.0 collective-permute-done.6.got
  19.7 0.8 %shard_map.92 = (f32[2,8,8,256]{3,2,1,0:T(8,128)}, f32[8,8,256]{2,1,0:T(8,128)}) custom-call(f32[3,8,8,128]{3,2,1,0:T(8,128)S(1)} %get-tuple-element.50.keep, f32[3,8,8,128]{3,2,1,0:T(8,128)S(1)} %collective-permute-done.6.got), custom_call_target="tpu_custom_call" | custom-call | flops 1000000000 | bytes 4194304 | tf_op jit(solution)/shard_map/pallas_call | solution.py:606
Async XLA Ops:
  2.1 1.7 %collective-permute-start = (f32[36,8,128]{2,1,0:T(8,128)S(1)}, f32[36,8,128]{2,1,0:T(8,128)S(1)}, u32[]{:S(2)}, u32[]{:S(2)}) collective-permute-start(f32[36,8,128]{2,1,0:T(8,128)S(1)} %get-tuple-element.32.to_partner), channel_id=1, source_target_pairs={{0,4},{1,5},{2,6},{3,7},{4,0},{5,1},{6,2},{7,3},{8,12},{9,13},{10,... | collective-permute-start | bytes 442376 | tf_op jit(solution)/shard_map/ppermute | solution.py:645
  3.6 2.4 %collective-permute-start.1 = (f32[16,8,128]{2,1,0:T(8,128)S(1)}, f32[16,8,128]{2,1,0:T(8,128)S(1)}, u32[]{:S(2)}, u32[]{:S(2)}) collective-permute-start(f32[16,8,128]{2,1,0:T(8,128)S(1)} %get-tuple-element.33.g_tracers), channel_id=1, source_target_pairs={{0,4},{1,5},{2,6},{3,7},{4,0},{5,1},{6,2},{7,3},{8,12},{9,13},{10,... | collective-permute-start | bytes 196616 | tf_op jit(solution)/shard_map/ppermute | solution.py:645
  3.8 2.2 %copy-start = (f32[16,16]{1,0:T(8,128)S(1)}, f32[16,16]{1,0:T(8,128)}, u32[]{:S(2)}) copy-start(f32[16,16]{1,0:T(8,128)} %rates.1) | copy-start | bytes 3076
  4.1 3.2 %collective-permute-start.2 = (f32[5,8,128]{2,1,0:T(8,128)S(1)}, f32[5,8,128]{2,1,0:T(8,128)S(1)}, u32[]{:S(2)}, u32[]{:S(2)}) collective-permute-start(f32[5,8,128]{2,1,0:T(8,128)S(1)} %get-tuple-element.43), channel_id=1, source_target_pairs={{0,8},{1,4},{2,5},{3,6},{4,1},{5,2},{6,3},{7,15},{8,0},{9,12},{10,... | collective-permute-start | bytes 61448 | tf_op jit(solution)/shard_map/ppermute | solution.py:645
  5.8 9.4 %collective-permute-start.3 = (f32[40,8,128]{2,1,0:T(8,128)S(1)}, f32[40,8,128]{2,1,0:T(8,128)S(1)}, u32[]{:S(2)}, u32[]{:S(2)}) collective-permute-start(f32[40,8,128]{2,1,0:T(8,128)S(1)} %get-tuple-element.45), channel_id=1, source_target_pairs={{0,8},{1,9},{2,10},{3,11},{4,12},{5,13},{6,14},{7,15},{8,0},{9,1},... | collective-permute-start | bytes 491528 | tf_op jit(solution)/shard_map/ppermute | solution.py:645
  7.6 7.5 %collective-permute-start.5 = (f32[8,128]{1,0:T(8,128)S(1)}, f32[8,128]{1,0:T(8,128)S(1)}, u32[]{:S(2)}, u32[]{:S(2)}) collective-permute-start(f32[8,128]{1,0:T(8,128)S(1)} %get-tuple-element.47), channel_id=1, source_target_pairs={{0,8},{1,9},{2,10},{3,11},{4,12},{5,13},{6,14},{7,15},{8,0},{9,1},... | collective-permute-start | bytes 12296 | tf_op jit(solution)/shard_map/ppermute | solution.py:645
  8.3 8.1 %collective-permute-start.4 = (f32[41,8,128]{2,1,0:T(8,128)S(1)}, f32[41,8,128]{2,1,0:T(8,128)S(1)}, u32[]{:S(2)}, u32[]{:S(2)}) collective-permute-start(f32[41,8,128]{2,1,0:T(8,128)S(1)} %get-tuple-element.46), channel_id=1, source_target_pairs={{0,4},{1,5},{2,6},{3,7},{4,0},{5,1},{6,2},{7,3},{8,16},{9,17},{10,... | collective-permute-start | bytes 503816 | tf_op jit(solution)/shard_map/ppermute | solution.py:645
  17.9 1.8 %collective-permute-start.6 = (f32[3,8,8,128]{3,2,1,0:T(8,128)S(1)}, f32[3,8,8,128]{3,2,1,0:T(8,128)S(1)}, u32[]{:S(2)}, u32[]{:S(2)}) collective-permute-start(f32[3,8,8,128]{3,2,1,0:T(8,128)S(1)} %get-tuple-element.51), channel_id=1, source_target_pairs={{0,4},{1,5},{2,6},{3,7},{4,0},{5,1},{6,2},{7,3},{8,12},{9,13},{10,... | collective-permute-start | bytes 294920 | tf_op jit(solution)/shard_map/ppermute | solution.py:645

commit v7 on v6

--- a/solution.py
+++ b/solution.py
@@ -513,13 +513,18 @@
     light_rows(m0, dv1, moved, m2, ntr, now)
 
 
-def outer_kernel(m_own, dv_own, mix, g0, gd, z_in, rows_a, rows_b, edge_a, m1_in, m2_in, rim, keep, send, m0, m1, dv0, dv1, wts, sat, moved, z0, z1, zd):
+def outer_kernel(m_own, dv_own, mix, g0, gd, z_in, rows_a, rows_b, edge_a, m1_in, m2_in, out, rim, keep, send, m0, m1, dv0, dv1, wts, sat, moved, z0, z1, zd, sem):
     nf, rows, nz, lon = m_own.shape
     ntr = nf - EXTRA
     lat_blk = rows - 4
     half, chip, _ = place()
     even = chip % 2 == 0
     south_ok, north_ok = (chip > 0, chip < lax.axis_size("row") // 2 - 1)
+    copies = [
+        pltpu.make_async_copy(m2_in.at[pl.ds(0, ntr), r], out.at[:, :, r - 2, :], sem.at[r - 4]) for r in range(4, rows - 4)
+    ]
+    for copy in copies:
+        copy.start()
 
     def got(high, a, b):
         picked = jnp.where(even, a, b) if high else jnp.where(even, b, a)
@@ -569,28 +574,22 @@
     for f in range(3):
         keep[f] = m0[ntr + f, pl.ds(2 + half * count, count)]
         send[f] = m0[ntr + f, pl.ds(2 + (1 - half) * count, count)]
-
-
-def write_kernel(rim, m, out, block, sem):
-    ntr, nz, lat_blk, lon = block.shape
-    copies = []
-    for n in range(0, ntr, GROUP):
-        for k in range(n, n + GROUP):
-            for t in range(lat_blk):
-                edge = {0: 0, 1: 1, lat_blk - 2: 2, lat_blk - 1: 3}.get(t)
-                block[k, :, t, :] = m[k, t + 2] if edge is None else rim[k, edge]
-        copy = pltpu.make_async_copy(block.at[pl.ds(n, GROUP)], out.at[pl.ds(n, GROUP)], sem.at[n // GROUP])
-        copy.start()
-        copies.append(copy)
     for copy in copies:
         copy.wait()
 
 
-def unpack_kernel(keep, got, flow, temp):
+def finish_kernel(keep, got, rim, out_in, flow_out, temp_out, out, flow, temp, sem):
     _, lat_dev, nz, lon = keep.shape
+    lat_blk = 2 * lat_dev
+    copies = [
+        pltpu.make_async_copy(rim.at[:, i], out.at[:, :, t, :], sem.at[i])
+        for i, t in enumerate((0, 1, lat_blk - 2, lat_blk - 1))
+    ]
+    for copy in copies:
+        copy.start()
     first = place()[0] == 0
-    for t in range(lat_dev):
-        for f in range(3):
+    for f in range(3):
+        for t in range(lat_dev):
             a, b = (keep[f, t], got[f, t])
             low, high = (jnp.where(first, a, b), jnp.where(first, b, a))
             if f < 2:
@@ -599,18 +598,28 @@
             else:
                 temp[:, t, :lon] = low
                 temp[:, t, lon:] = high
-
-
-def call(kernel, outs, *args, scratch=(), held=True, away=False, limit=40, cost=1):
-    vmem = pl.BlockSpec(memory_space=pltpu.VMEM)
+        if f == 1:
+            copies.append(pltpu.make_async_copy(flow, flow_out, sem.at[4]))
+            copies[-1].start()
+    copies.append(pltpu.make_async_copy(temp, temp_out, sem.at[5]))
+    copies[-1].start()
+    for copy in copies:
+        copy.wait()
+
+
+def call(kernel, outs, *args, scratch=(), far=(), away=(), aliases=None, cost=1):
+    vmem, anywhere = (pl.BlockSpec(memory_space=pltpu.VMEM), pl.BlockSpec(memory_space=pl.ANY))
     return pl.pallas_call(
         kernel,
         out_shape=[jax.ShapeDtypeStruct(s, jnp.float32) if isinstance(s, tuple) else s for s in outs],
-        in_specs=[vmem if held else pl.BlockSpec(memory_space=pl.ANY)] * len(args),
-        out_specs=[pl.BlockSpec(memory_space=pl.ANY) if away else vmem] * len(outs),
+        in_specs=[anywhere if i in far else vmem for i in range(len(args))],
+        out_specs=[anywhere if i in away else vmem for i in range(len(outs))],
         scratch_shapes=[pltpu.VMEM(s, jnp.float32) if isinstance(s, tuple) else s for s in scratch],
-        compiler_params=pltpu.CompilerParams(vmem_limit_bytes=limit * 2**20),
-        cost_estimate=pl.CostEstimate(flops=int(cost * 10**9), transcendentals=0, bytes_accessed=int(cost * 4 * 2**20)),
+        input_output_aliases=aliases or {},
+        compiler_params=pltpu.CompilerParams(vmem_limit_bytes=40 * 2**20),
+        cost_estimate=pl.CostEstimate(
+            flops=int(cost * 10**9), transcendentals=0, bytes_accessed=int(cost * 4 * 2**20)
+        ),
     )(*args)
 
 
@@ -647,7 +656,6 @@
     block = tracers[0]
     rows = lat_blk + 4
     cols, extra, some = ((nf, nz, lon), (EXTRA, nz, lon), (3, nz, lon))
-    copies = pltpu.SemaphoreType.DMA((ntr // GROUP,))
     sent = (EXTRA * (lat_dev + 1), nz, lon)
     given = (flow, temp, bottom, sunlight, block)
     mine, to_partner, g_other, block = call(
@@ -661,7 +669,7 @@
             sunlight.shape,
             pltpu.SemaphoreType.DMA((len(given),)),
         ],
-        held=False,
+        far=range(len(given)),
     )
     got = swap(to_partner, partner)
     turned, g_tracers = call(pack_tracers_kernel, [(ntr, lat_blk, nz, lon), (ntr, nz, lon)], block)
@@ -698,9 +706,9 @@
     work += [(ntr + 1, rows, nz, lon), cols, cols, some]
     m1, m2 = call(inner_kernel, [full, full], m0, dv, mix, g0, gd, z, scratch=[derived] + work, cost=20)
     third = (3, lat_dev, nz, lon)
-    rim, keep, send = call(
+    out, rim, keep, send = call(
         outer_kernel,
-        [(ntr, 4, nz, lon), third, third],
+        [(ntr, nz, lat_blk, lon), (ntr, 4, nz, lon), third, third],
         m0,
         dv,
         mix,
@@ -712,12 +720,20 @@
         edge_a,
         m1,
         m2,
-        scratch=[full, full, derived, derived] + work,
-    )
-    returned = swap(send, partner)
-    (out,) = call(write_kernel, [(ntr, nz, lat_blk, lon)], rim, m2, scratch=[(ntr, nz, lat_blk, lon), copies], away=True)
-    flow_out, temp_out = call(
-        unpack_kernel, [(2, nz, lat_dev, lon_dev), (nz, lat_dev, lon_dev)], keep, returned
+        scratch=[full, full, derived, derived] + work + [pltpu.SemaphoreType.DMA((lat_blk - 4,))],
+        away=(0,),
+    )
+    flow_out, temp_out, out = call(
+        finish_kernel,
+        [flow.shape, temp.shape, out.shape],
+        keep,
+        swap(send, partner),
+        rim,
+        out,
+        scratch=[flow.shape, temp.shape, pltpu.SemaphoreType.DMA((6,))],
+        far=(3,),
+        away=(0, 1, 2),
+        aliases={3: 2},
     )
     return (flow_out, temp_out, out[None])
 

time: 20.7 us -> 20.5 us (level)
  Pallas kernels: 12.2 us -> 11 us
  waiting for transfers between devices: 1.98 us -> 2.92 us
    pallas_call x9 -> x8, Pallas kernels: 12.2 us -> 11 us  [call(): pl.pallas_call(kernel, out_shape=[jax.ShapeDtypeStruct(s, jnp.float32) if...]
    ppermute x7, waiting for transfers between devices: 1.98 us -> 2.92 us  [swap(): return lax.ppermute(x, ('row', 'col'), pairs)]
  transfers between devices with their start and end apart: 7 -> 7, of which waited for: 3 -> 4; matrix products, arithmetic and copies ran while one was open for 0% -> 0% of each run, Pallas kernels for 41% -> 35%
where the time goes in v7:
time: 20.5 us; the launch traced here: 20.3 us
  Pallas kernels  11 us (54%)
  starting transfers between devices  5.7 us (28%)
  waiting for transfers between devices  2.92 us (14%)
  between operations  0.69 us (3%)
    pallas_call x8, Pallas kernels, call(): pl.pallas_call(kernel, out_shape=[jax.ShapeDtypeStruct(s, jnp.float32) if...  11 us
    ppermute x7, starting transfers between devices, swap(): return lax.ppermute(x, ('row', 'col'), pairs)  5.7 us
    ppermute x7, waiting for transfers between devices, swap(): return lax.ppermute(x, ('row', 'col'), pairs)  2.92 us
  transfers between devices with their start and end apart: 7, of which 4 were waited for; matrix products, arithmetic and copies ran while one was open for 0% of the time, Pallas kernels for 35%

profile of v7, /device:TPU:3, one launch (start us, length us, event | category | flops | bytes accessed | tf_op | source)
XLA Modules:
  0.0 20.3 jit_solution(1699326250868861568)
XLA Ops:
  0.6 1.4 %shard_map.85 = (f32[4,8,8,128]{3,2,1,0:T(8,128)S(1)}, f32[36,8,128]{2,1,0:T(8,128)S(1)}, f32[4,8,128]{2,1,0:T(8,128)S(1)}, f32[16,8,16,128]{3,2,1,0:T(8,128)S(1)}) custom-call(f32[2,8,8,256]{3,2,1,0:T(8,128)} %flow_in.1, f32[8,8,256]{2,1,0:T(8,128)} %temp_in.1, s32[8,256]{1,0:T(8,128)} %bottom_in.1, f32[8,256]{1,0:T(8,128)} %sunlight_in.1, ...), custom_call_target="tpu_custom_call" | custom-call | flops 1000000000 | bytes 4194304 | tf_op jit(solution)/shard_map/pallas_call | solution.py:612
  2.1 0.7 %collective-permute-start = (f32[36,8,128]{2,1,0:T(8,128)S(1)}, f32[36,8,128]{2,1,0:T(8,128)S(1)}, u32[]{:S(2)}, u32[]{:S(2)}) collective-permute-start(f32[36,8,128]{2,1,0:T(8,128)S(1)} %get-tuple-element.34.to_partner), channel_id=1, source_target_pairs={{0,4},{1,5},{2,6},{3,7},{4,0},{5,1},{6,2},{7,3},{8,12},{9,13},{10,... | collective-permute-start | bytes 442376 | tf_op jit(solution)/shard_map/ppermute | solution.py:654
  2.8 0.8 %shard_map.86 = (f32[16,16,8,128]{3,2,1,0:T(8,128)S(1)}, f32[16,8,128]{2,1,0:T(8,128)S(1)}) custom-call(f32[16,8,16,128]{3,2,1,0:T(8,128)S(1)} %get-tuple-element.31.tracers), custom_call_target="tpu_custom_call" | custom-call | flops 1000000000 | bytes 4194304 | tf_op jit(solution)/shard_map/pallas_call | solution.py:612
  3.6 0.1 collective-permute-start.1
  3.7 0.1 collective-permute-done.got
  3.8 0.0 copy-start
  3.8 0.3 %shard_map.87 = (f32[4,16,8,128]{3,2,1,0:T(8,128)S(1)}, f32[20,8,128]{2,1,0:T(8,128)S(1)}, f32[5,8,128]{2,1,0:T(8,128)S(1)}, f32[40,8,128]{2,1,0:T(8,128)S(1)}) custom-call(f32[4,8,8,128]{3,2,1,0:T(8,128)S(1)} %get-tuple-element.33.mine, f32[36,8,128]{2,1,0:T(8,128)S(1)} %collective-permute-done.got, f32[36,8,128]{2,1,0:T(8,128)S(1)} %get-tuple-element.34.to_partner, ...), custom_call_target="tpu_custom_call" | custom-call | flops 1000000000 | bytes 4194304 | tf_op jit(solution)/shard_map/pallas_call | solution.py:612
  4.1 1.6 %collective-permute-start.2 = (f32[5,8,128]{2,1,0:T(8,128)S(1)}, f32[5,8,128]{2,1,0:T(8,128)S(1)}, u32[]{:S(2)}, u32[]{:S(2)}) collective-permute-start(f32[5,8,128]{2,1,0:T(8,128)S(1)} %get-tuple-element.45), channel_id=1, source_target_pairs={{0,8},{1,4},{2,5},{3,6},{4,1},{5,2},{6,3},{7,15},{8,0},{9,12},{10,... | collective-permute-start | bytes 61448 | tf_op jit(solution)/shard_map/ppermute | solution.py:654
  5.8 0.3 %collective-permute-start.3 = (f32[40,8,128]{2,1,0:T(8,128)S(1)}, f32[40,8,128]{2,1,0:T(8,128)S(1)}, u32[]{:S(2)}, u32[]{:S(2)}) collective-permute-start(f32[40,8,128]{2,1,0:T(8,128)S(1)} %get-tuple-element.47), channel_id=1, source_target_pairs={{0,8},{1,9},{2,10},{3,11},{4,12},{5,13},{6,14},{7,15},{8,0},{9,1},... | collective-permute-start | bytes 491528 | tf_op jit(solution)/shard_map/ppermute | solution.py:654
  6.0 0.0 collective-permute-done.1.g_partner
  6.0 0.0 copy-done
  6.0 0.7 %shard_map.88 = (f32[20,20,8,128]{3,2,1,0:T(8,128)S(1)}, f32[3,20,8,128]{3,2,1,0:T(8,128)S(1)}, bf16[256,256]{1,0:T(8,128)(2,1)S(1)}, f32[20,8,128]{2,1,0:T(8,12...) custom-call(f32[16,16,8,128]{3,2,1,0:T(8,128)S(1)} %get-tuple-element.32.turned, ...), custom_call_target="tpu_custom_call" | custom-call | flops 1000000000 | bytes 4194304 | tf_op jit(solution)/shard_map/pallas_call | solution.py:612
  6.8 0.6 %collective-permute-done.2.from_outer = f32[5,8,128]{2,1,0:T(8,128)S(1)} collective-permute-done((f32[5,8,128]{2,1,0:T(8,128)S(1)}, f32[5,8,128]{2,1,0:T(8,128)S(1)}, u32[]{:S(2)}, u32[]{:S(2)}) %collective-permute-start.2) | collective-permute-done | bytes 20512 | tf_op jit(solution)/shard_map/ppermute | solution.py:654
  7.4 0.2 shard_map.89
  7.6 0.7 %collective-permute-start.5 = (f32[8,128]{1,0:T(8,128)S(1)}, f32[8,128]{1,0:T(8,128)S(1)}, u32[]{:S(2)}, u32[]{:S(2)}) collective-permute-start(f32[8,128]{1,0:T(8,128)S(1)} %get-tuple-element.49), channel_id=1, source_target_pairs={{0,8},{1,9},{2,10},{3,11},{4,12},{5,13},{6,14},{7,15},{8,0},{9,1},... | collective-permute-start | bytes 12296 | tf_op jit(solution)/shard_map/ppermute | solution.py:654
  8.3 1.8 %collective-permute-start.4 = (f32[41,8,128]{2,1,0:T(8,128)S(1)}, f32[41,8,128]{2,1,0:T(8,128)S(1)}, u32[]{:S(2)}, u32[]{:S(2)}) collective-permute-start(f32[41,8,128]{2,1,0:T(8,128)S(1)} %get-tuple-element.48), channel_id=1, source_target_pairs={{0,4},{1,5},{2,6},{3,7},{4,0},{5,1},{6,2},{7,3},{8,16},{9,17},{10,... | collective-permute-start | bytes 503816 | tf_op jit(solution)/shard_map/ppermute | solution.py:654
  10.1 5.0 %shard_map.90 = (f32[20,20,8,128]{3,2,1,0:T(8,128)S(1)}, f32[20,20,8,128]{3,2,1,0:T(8,128)S(1)}) custom-call(f32[20,20,8,128]{3,2,1,0:T(8,128)S(1)} %get-tuple-element.39.m0.m_own, f32[3,20,8,128]{3,2,1,0:T(8,128)S(1)} %get-tuple-element.40.dv.dv_own, bf16[256,256]{1,0:T(8,128)(2,1)S(1)} %get-tuple-element.41.mix, f32[20,8,128]{2,1,0:T(8,128)S(1)} %get-tuple-element.42.g0, ...), custom_call_target="tpu_custom_call" | custom-call | flops 20000000000 | bytes 83886080 | tf_op jit(solution)/shard_map/pallas_call | solution.py:612
  15.1 0.0 collective-permute-done.5.edge_a
  15.1 0.0 collective-permute-done.3.rows_a
  15.1 1.3 %collective-permute-done.4.rows_b = f32[41,8,128]{2,1,0:T(8,128)S(1)} collective-permute-done((f32[41,8,128]{2,1,0:T(8,128)S(1)}, f32[41,8,128]{2,1,0:T(8,128)S(1)}, u32[]{:S(2)}, u32[]{:S(2)}) %collective-permute-start.4) | collective-permute-done | bytes 167968 | tf_op jit(solution)/shard_map/ppermute | solution.py:654
  16.4 1.7 %shard_map.91 = (f32[16,8,16,128]{3,2,1,0:T(8,128)}, f32[16,4,8,128]{3,2,1,0:T(8,128)S(1)}, f32[3,8,8,128]{3,2,1,0:T(8,128)S(1)}, f32[3,8,8,128]{3,2,1,0:T(8,128)S(1)}) custom-call(f32[20,20,8,128]{3,2,1,0:T(8,128)S(1)} %get-tuple-element.39.m0.m_own, f32[3,20,8,128]{3,2,1,0:T(8,128)S(1)} %get-tuple-element.40.dv.dv_own, ...), custom_call_target="tpu_custom_call" | custom-call | flops 1000000000 | bytes 4194304 | tf_op jit(solution)/shard_map/pallas_call | solution.py:612
  18.1 0.5 %collective-permute-start.6 = (f32[3,8,8,128]{3,2,1,0:T(8,128)S(1)}, f32[3,8,8,128]{3,2,1,0:T(8,128)S(1)}, u32[]{:S(2)}, u32[]{:S(2)}) collective-permute-start(f32[3,8,8,128]{3,2,1,0:T(8,128)S(1)} %get-tuple-element.53), channel_id=1, source_target_pairs={{0,4},{1,5},{2,6},{3,7},{4,0},{5,1},{6,2},{7,3},{8,12},{9,13},{10,... | collective-permute-start | bytes 294920 | tf_op jit(solution)/shard_map/ppermute | solution.py:654
  18.6 0.9 %collective-permute-done.6.got = f32[3,8,8,128]{3,2,1,0:T(8,128)S(1)} collective-permute-done((f32[3,8,8,128]{3,2,1,0:T(8,128)S(1)}, f32[3,8,8,128]{3,2,1,0:T(8,128)S(1)}, u32[]{:S(2)}, u32[]{:S(2)}) %collective-permute-start.6) | collective-permute-done | bytes 98336 | tf_op jit(solution)/shard_map/ppermute | solution.py:654
  19.5 0.8 %shard_map.92 = (f32[2,8,8,256]{3,2,1,0:T(8,128)}, f32[8,8,256]{2,1,0:T(8,128)}, f32[16,8,16,128]{3,2,1,0:T(8,128)}) custom-call(f32[3,8,8,128]{3,2,1,0:T(8,128)S(1)} %get-tuple-element.52.keep, f32[3,8,8,128]{3,2,1,0:T(8,128)S(1)} %collective-permute-done.6.got, f32[16,4,8,128]{3,2,1,0:T(8,128)S(1)} %get-tuple-element.54.rim, ...), custom_call_target="tpu_custom_call", output_to_operand_aliasing={{2}: (3, {})} | custom-call | flops 1000000000 | bytes 4194304 | tf_op jit(solution)/shard_map/pallas_call | solution.py:612
Async XLA Ops:
  2.1 1.7 %collective-permute-start = (f32[36,8,128]{2,1,0:T(8,128)S(1)}, f32[36,8,128]{2,1,0:T(8,128)S(1)}, u32[]{:S(2)}, u32[]{:S(2)}) collective-permute-start(f32[36,8,128]{2,1,0:T(8,128)S(1)} %get-tuple-element.34.to_partner), channel_id=1, source_target_pairs={{0,4},{1,5},{2,6},{3,7},{4,0},{5,1},{6,2},{7,3},{8,12},{9,13},{10,... | collective-permute-start | bytes 442376 | tf_op jit(solution)/shard_map/ppermute | solution.py:654
  3.6 2.4 %collective-permute-start.1 = (f32[16,8,128]{2,1,0:T(8,128)S(1)}, f32[16,8,128]{2,1,0:T(8,128)S(1)}, u32[]{:S(2)}, u32[]{:S(2)}) collective-permute-start(f32[16,8,128]{2,1,0:T(8,128)S(1)} %get-tuple-element.35.g_tracers), channel_id=1, source_target_pairs={{0,4},{1,5},{2,6},{3,7},{4,0},{5,1},{6,2},{7,3},{8,12},{9,13},{10,... | collective-permute-start | bytes 196616 | tf_op jit(solution)/shard_map/ppermute | solution.py:654
  3.8 2.2 %copy-start = (f32[16,16]{1,0:T(8,128)S(1)}, f32[16,16]{1,0:T(8,128)}, u32[]{:S(2)}) copy-start(f32[16,16]{1,0:T(8,128)} %rates.1) | copy-start | bytes 3076
  4.1 3.3 %collective-permute-start.2 = (f32[5,8,128]{2,1,0:T(8,128)S(1)}, f32[5,8,128]{2,1,0:T(8,128)S(1)}, u32[]{:S(2)}, u32[]{:S(2)}) collective-permute-start(f32[5,8,128]{2,1,0:T(8,128)S(1)} %get-tuple-element.45), channel_id=1, source_target_pairs={{0,8},{1,4},{2,5},{3,6},{4,1},{5,2},{6,3},{7,15},{8,0},{9,12},{10,... | collective-permute-start | bytes 61448 | tf_op jit(solution)/shard_map/ppermute | solution.py:654
  5.8 9.3 %collective-permute-start.3 = (f32[40,8,128]{2,1,0:T(8,128)S(1)}, f32[40,8,128]{2,1,0:T(8,128)S(1)}, u32[]{:S(2)}, u32[]{:S(2)}) collective-permute-start(f32[40,8,128]{2,1,0:T(8,128)S(1)} %get-tuple-element.47), channel_id=1, source_target_pairs={{0,8},{1,9},{2,10},{3,11},{4,12},{5,13},{6,14},{7,15},{8,0},{9,1},... | collective-permute-start | bytes 491528 | tf_op jit(solution)/shard_map/ppermute | solution.py:654
  7.6 7.5 %collective-permute-start.5 = (f32[8,128]{1,0:T(8,128)S(1)}, f32[8,128]{1,0:T(8,128)S(1)}, u32[]{:S(2)}, u32[]{:S(2)}) collective-permute-start(f32[8,128]{1,0:T(8,128)S(1)} %get-tuple-element.49), channel_id=1, source_target_pairs={{0,8},{1,9},{2,10},{3,11},{4,12},{5,13},{6,14},{7,15},{8,0},{9,1},... | collective-permute-start | bytes 12296 | tf_op jit(solution)/shard_map/ppermute | solution.py:654
  8.3 8.1 %collective-permute-start.4 = (f32[41,8,128]{2,1,0:T(8,128)S(1)}, f32[41,8,128]{2,1,0:T(8,128)S(1)}, u32[]{:S(2)}, u32[]{:S(2)}) collective-permute-start(f32[41,8,128]{2,1,0:T(8,128)S(1)} %get-tuple-element.48), channel_id=1, source_target_pairs={{0,4},{1,5},{2,6},{3,7},{4,0},{5,1},{6,2},{7,3},{8,16},{9,17},{10,... | collective-permute-start | bytes 503816 | tf_op jit(solution)/shard_map/ppermute | solution.py:654
  18.1 1.5 %collective-permute-start.6 = (f32[3,8,8,128]{3,2,1,0:T(8,128)S(1)}, f32[3,8,8,128]{3,2,1,0:T(8,128)S(1)}, u32[]{:S(2)}, u32[]{:S(2)}) collective-permute-start(f32[3,8,8,128]{3,2,1,0:T(8,128)S(1)} %get-tuple-element.53), channel_id=1, source_target_pairs={{0,4},{1,5},{2,6},{3,7},{4,0},{5,1},{6,2},{7,3},{8,12},{9,13},{10,... | collective-permute-start | bytes 294920 | tf_op jit(solution)/shard_map/ppermute | solution.py:654

commit v8 on v7

--- a/solution.py
+++ b/solution.py
@@ -86,12 +86,16 @@
             low, high = (tile[:, :lon], tile[:, lon:])
             a, b = (jnp.where(first, low, high), jnp.where(first, high, low))
             mine[f, t] = a
-            to_partner[f * lat_dev + t] = b
+            if f < EXTRA - 1:
+                to_partner[f * lat_dev + t] = b
             own[f] = window(a, t, own[f])
             far[f] = window(b, t, far[f])
+    flat = (EXTRA - 1) * lat_dev
+    for i, both in enumerate((bottom[...].astype(jnp.float32), sunlight[...])):
+        to_partner[flat + i, :lat_dev, :] = jnp.where(first, both[:, lon:], both[:, :lon])
     shift = half * (WIN * lat_dev)
     for f in range(EXTRA):
-        to_partner[EXTRA * lat_dev + f] = pltpu.roll(own[f], shift, 1)
+        to_partner[flat + 2 + f] = pltpu.roll(own[f], shift, 1)
         g_other[f] = pltpu.roll(far[f], shift, 1)
     copies[-1].wait()
 
@@ -100,17 +104,17 @@
     ntr, nz, lat_blk, lon = tracers.shape
 
     def some(i, _):
-        g = [jnp.zeros((nz, lon), jnp.float32)] * GROUP
+        g = [jnp.zeros((nz, lon), jnp.float32)] * PACK
         for t in range(lat_blk):
-            for k in range(GROUP):
-                x = tracers[i * GROUP + k, :, t, :]
-                turned[i * GROUP + k, t] = x
+            for k in range(PACK):
+                x = tracers[i * PACK + k, :, t, :]
+                turned[i * PACK + k, t] = x
                 g[k] = window(x, t, g[k])
-        for k in range(GROUP):
-            g_tracers[i * GROUP + k] = g[k]
+        for k in range(PACK):
+            g_tracers[i * PACK + k] = g[k]
         return 0
 
-    lax.fori_loop(0, ntr // GROUP, some, 0)
+    lax.fori_loop(0, ntr // PACK, some, 0)
 
 
 def in_half(shape, half, lat_dev):
@@ -135,15 +139,20 @@
     tile = (nz, lon)
     own_lanes = in_half(tile, half, lat_dev)
     shift = (1 - half) * (WIN * lat_dev)
+    flat, level = ((EXTRA - 1) * lat_dev, levels_of(tile))
     g_own[:ntr] = g_tracers[...]
     for f in range(EXTRA):
         g = jnp.zeros(tile, jnp.float32)
         for t in range(lat_dev):
-            x = got[f * lat_dev + t]
+            if f < EXTRA - 1:
+                x = got[f * lat_dev + t]
+            else:
+                depth, light = (jnp.broadcast_to(got[flat + i, t : t + 1, :], tile) for i in range(2))
+                x = jnp.where(level == 0, depth, jnp.where(level == 1, light, 0.0))
             ocean[f, half * lat_dev + t] = mine[f, t]
             ocean[f, (1 - half) * lat_dev + t] = x
             g = window(x, t, g)
-        g_own[ntr + f] = jnp.where(own_lanes, to_partner[EXTRA * lat_dev + f], pltpu.roll(g, shift, 1))
+        g_own[ntr + f] = jnp.where(own_lanes, to_partner[flat + 2 + f], pltpu.roll(g, shift, 1))
     edge_rows(turned, ocean, edge_starts(chip, 2 * lat_dev)[0], rows_a)
     lane = lanes_of(tile)
     front, near = (lane % WIN < 2, in_half(tile, 0, 2 * lat_dev))
@@ -321,6 +330,7 @@
 
 KAP, PRS, WET = (0, 1, 2)
 GROUP = 4
+PACK = 8
 PIECE = 3
 
 
@@ -463,7 +473,7 @@
     half, _, _ = place()
     inner[:ntr] = g_partner[...]
     for f in range(EXTRA):
-        theirs = got[EXTRA * (lat_blk // 2) + f]
+        theirs = got[(EXTRA - 1) * (lat_blk // 2) + 2 + f]
         inner[ntr + f] = jnp.where(in_half((nz, lon), half, lat_blk // 2), g_other[f], theirs)
     mix[...] = mix_matrix(rates[...], nz)
     own = span(2, lat_blk + 2)
@@ -656,7 +666,7 @@
     block = tracers[0]
     rows = lat_blk + 4
     cols, extra, some = ((nf, nz, lon), (EXTRA, nz, lon), (3, nz, lon))
-    sent = (EXTRA * (lat_dev + 1), nz, lon)
+    sent = ((EXTRA - 1) * lat_dev + 2 + EXTRA, nz, lon)
     given = (flow, temp, bottom, sunlight, block)
     mine, to_partner, g_other, block = call(
         pack_ocean_kernel,

time: 20.5 us -> 20.4 us (level)
  transfers between devices with their start and end apart: 7 -> 7, of which waited for: 4 -> 4; matrix products, arithmetic and copies ran while one was open for 0% -> 0% of each run, Pallas kernels for 35% -> 34%
where the time goes in v8:
time: 20.4 us; the launch traced here: 20.3 us
  Pallas kernels  10.9 us (53%)
  starting transfers between devices  5.67 us (28%)
  waiting for transfers between devices  3.02 us (15%)
  between operations  0.69 us (3%)
    pallas_call x8, Pallas kernels, call(): pl.pallas_call(kernel, out_shape=[jax.ShapeDtypeStruct(s, jnp.float32) if...  10.9 us
    ppermute x7, starting transfers between devices, swap(): return lax.ppermute(x, ('row', 'col'), pairs)  5.67 us
    ppermute x7, waiting for transfers between devices, swap(): return lax.ppermute(x, ('row', 'col'), pairs)  3.02 us
  transfers between devices with their start and end apart: 7, of which 4 were waited for; matrix products, arithmetic and copies ran while one was open for 0% of the time, Pallas kernels for 34%

profile of v8, /device:TPU:3, one launch (start us, length us, event | category | flops | bytes accessed | tf_op | source)
XLA Modules:
  0.0 20.3 jit_solution(13723930329611222430)
XLA Ops:
  0.6 1.4 %shard_map.85 = (f32[4,8,8,128]{3,2,1,0:T(8,128)S(1)}, f32[30,8,128]{2,1,0:T(8,128)S(1)}, f32[4,8,128]{2,1,0:T(8,128)S(1)}, f32[16,8,16,128]{3,2,1,0:T(8,128)S(1)}) custom-call(f32[2,8,8,256]{3,2,1,0:T(8,128)} %flow_in.1, f32[8,8,256]{2,1,0:T(8,128)} %temp_in.1, s32[8,256]{1,0:T(8,128)} %bottom_in.1, f32[8,256]{1,0:T(8,128)} %sunlight_in.1, ...), custom_call_target="tpu_custom_call" | custom-call | flops 1000000000 | bytes 4194304 | tf_op jit(solution)/shard_map/pallas_call | solution.py:622
  2.1 0.7 %collective-permute-start = (f32[30,8,128]{2,1,0:T(8,128)S(1)}, f32[30,8,128]{2,1,0:T(8,128)S(1)}, u32[]{:S(2)}, u32[]{:S(2)}) collective-permute-start(f32[30,8,128]{2,1,0:T(8,128)S(1)} %get-tuple-element.34.to_partner), channel_id=1, source_target_pairs={{0,4},{1,5},{2,6},{3,7},{4,0},{5,1},{6,2},{7,3},{8,12},{9,13},{10,... | collective-permute-start | bytes 368648 | tf_op jit(solution)/shard_map/ppermute | solution.py:664
  2.8 0.7 %shard_map.86 = (f32[16,16,8,128]{3,2,1,0:T(8,128)S(1)}, f32[16,8,128]{2,1,0:T(8,128)S(1)}) custom-call(f32[16,8,16,128]{3,2,1,0:T(8,128)S(1)} %get-tuple-element.31.tracers), custom_call_target="tpu_custom_call" | custom-call | flops 1000000000 | bytes 4194304 | tf_op jit(solution)/shard_map/pallas_call | solution.py:622
  3.5 0.1 collective-permute-start.1
  3.6 0.2 collective-permute-done.got
  3.8 0.0 copy-start
  3.8 0.3 %shard_map.87 = (f32[4,16,8,128]{3,2,1,0:T(8,128)S(1)}, f32[20,8,128]{2,1,0:T(8,128)S(1)}, f32[5,8,128]{2,1,0:T(8,128)S(1)}, f32[40,8,128]{2,1,0:T(8,128)S(1)}) custom-call(f32[4,8,8,128]{3,2,1,0:T(8,128)S(1)} %get-tuple-element.33.mine, f32[30,8,128]{2,1,0:T(8,128)S(1)} %collective-permute-done.got, f32[30,8,128]{2,1,0:T(8,128)S(1)} %get-tuple-element.34.to_partner, ...), custom_call_target="tpu_custom_call" | custom-call | flops 1000000000 | bytes 4194304 | tf_op jit(solution)/shard_map/pallas_call | solution.py:622
  4.1 1.6 %collective-permute-start.2 = (f32[5,8,128]{2,1,0:T(8,128)S(1)}, f32[5,8,128]{2,1,0:T(8,128)S(1)}, u32[]{:S(2)}, u32[]{:S(2)}) collective-permute-start(f32[5,8,128]{2,1,0:T(8,128)S(1)} %get-tuple-element.45), channel_id=1, source_target_pairs={{0,8},{1,4},{2,5},{3,6},{4,1},{5,2},{6,3},{7,15},{8,0},{9,12},{10,... | collective-permute-start | bytes 61448 | tf_op jit(solution)/shard_map/ppermute | solution.py:664
  5.7 0.3 %collective-permute-start.3 = (f32[40,8,128]{2,1,0:T(8,128)S(1)}, f32[40,8,128]{2,1,0:T(8,128)S(1)}, u32[]{:S(2)}, u32[]{:S(2)}) collective-permute-start(f32[40,8,128]{2,1,0:T(8,128)S(1)} %get-tuple-element.47), channel_id=1, source_target_pairs={{0,8},{1,9},{2,10},{3,11},{4,12},{5,13},{6,14},{7,15},{8,0},{9,1},... | collective-permute-start | bytes 491528 | tf_op jit(solution)/shard_map/ppermute | solution.py:664
  6.0 0.0 collective-permute-done.1.g_partner
  6.0 0.0 copy-done
  6.0 0.7 %shard_map.88 = (f32[20,20,8,128]{3,2,1,0:T(8,128)S(1)}, f32[3,20,8,128]{3,2,1,0:T(8,128)S(1)}, bf16[256,256]{1,0:T(8,128)(2,1)S(1)}, f32[20,8,128]{2,1,0:T(8,12...) custom-call(f32[16,16,8,128]{3,2,1,0:T(8,128)S(1)} %get-tuple-element.32.turned, ...), custom_call_target="tpu_custom_call" | custom-call | flops 1000000000 | bytes 4194304 | tf_op jit(solution)/shard_map/pallas_call | solution.py:622
  6.7 0.7 %collective-permute-done.2.from_outer = f32[5,8,128]{2,1,0:T(8,128)S(1)} collective-permute-done((f32[5,8,128]{2,1,0:T(8,128)S(1)}, f32[5,8,128]{2,1,0:T(8,128)S(1)}, u32[]{:S(2)}, u32[]{:S(2)}) %collective-permute-start.2) | collective-permute-done | bytes 20512 | tf_op jit(solution)/shard_map/ppermute | solution.py:664
  7.4 0.2 shard_map.89
  7.6 0.7 %collective-permute-start.5 = (f32[8,128]{1,0:T(8,128)S(1)}, f32[8,128]{1,0:T(8,128)S(1)}, u32[]{:S(2)}, u32[]{:S(2)}) collective-permute-start(f32[8,128]{1,0:T(8,128)S(1)} %get-tuple-element.49), channel_id=1, source_target_pairs={{0,8},{1,9},{2,10},{3,11},{4,12},{5,13},{6,14},{7,15},{8,0},{9,1},... | collective-permute-start | bytes 12296 | tf_op jit(solution)/shard_map/ppermute | solution.py:664
  8.2 1.8 %collective-permute-start.4 = (f32[41,8,128]{2,1,0:T(8,128)S(1)}, f32[41,8,128]{2,1,0:T(8,128)S(1)}, u32[]{:S(2)}, u32[]{:S(2)}) collective-permute-start(f32[41,8,128]{2,1,0:T(8,128)S(1)} %get-tuple-element.48), channel_id=1, source_target_pairs={{0,4},{1,5},{2,6},{3,7},{4,0},{5,1},{6,2},{7,3},{8,16},{9,17},{10,... | collective-permute-start | bytes 503816 | tf_op jit(solution)/shard_map/ppermute | solution.py:664
  10.0 5.0 %shard_map.90 = (f32[20,20,8,128]{3,2,1,0:T(8,128)S(1)}, f32[20,20,8,128]{3,2,1,0:T(8,128)S(1)}) custom-call(f32[20,20,8,128]{3,2,1,0:T(8,128)S(1)} %get-tuple-element.39.m0.m_own, f32[3,20,8,128]{3,2,1,0:T(8,128)S(1)} %get-tuple-element.40.dv.dv_own, bf16[256,256]{1,0:T(8,128)(2,1)S(1)} %get-tuple-element.41.mix, f32[20,8,128]{2,1,0:T(8,128)S(1)} %get-tuple-element.42.g0, ...), custom_call_target="tpu_custom_call" | custom-call | flops 20000000000 | bytes 83886080 | tf_op jit(solution)/shard_map/pallas_call | solution.py:622
  15.1 0.0 collective-permute-done.5.edge_a
  15.1 0.0 collective-permute-done.3.rows_a
  15.1 1.2 %collective-permute-done.4.rows_b = f32[41,8,128]{2,1,0:T(8,128)S(1)} collective-permute-done((f32[41,8,128]{2,1,0:T(8,128)S(1)}, f32[41,8,128]{2,1,0:T(8,128)S(1)}, u32[]{:S(2)}, u32[]{:S(2)}) %collective-permute-start.4) | collective-permute-done | bytes 167968 | tf_op jit(solution)/shard_map/ppermute | solution.py:664
  16.3 1.6 %shard_map.91 = (f32[16,8,16,128]{3,2,1,0:T(8,128)}, f32[16,4,8,128]{3,2,1,0:T(8,128)S(1)}, f32[3,8,8,128]{3,2,1,0:T(8,128)S(1)}, f32[3,8,8,128]{3,2,1,0:T(8,128)S(1)}) custom-call(f32[20,20,8,128]{3,2,1,0:T(8,128)S(1)} %get-tuple-element.39.m0.m_own, f32[3,20,8,128]{3,2,1,0:T(8,128)S(1)} %get-tuple-element.40.dv.dv_own, ...), custom_call_target="tpu_custom_call" | custom-call | flops 1000000000 | bytes 4194304 | tf_op jit(solution)/shard_map/pallas_call | solution.py:622
  18.0 0.5 %collective-permute-start.6 = (f32[3,8,8,128]{3,2,1,0:T(8,128)S(1)}, f32[3,8,8,128]{3,2,1,0:T(8,128)S(1)}, u32[]{:S(2)}, u32[]{:S(2)}) collective-permute-start(f32[3,8,8,128]{3,2,1,0:T(8,128)S(1)} %get-tuple-element.53), channel_id=1, source_target_pairs={{0,4},{1,5},{2,6},{3,7},{4,0},{5,1},{6,2},{7,3},{8,12},{9,13},{10,... | collective-permute-start | bytes 294920 | tf_op jit(solution)/shard_map/ppermute | solution.py:664
  18.5 0.9 %collective-permute-done.6.got = f32[3,8,8,128]{3,2,1,0:T(8,128)S(1)} collective-permute-done((f32[3,8,8,128]{3,2,1,0:T(8,128)S(1)}, f32[3,8,8,128]{3,2,1,0:T(8,128)S(1)}, u32[]{:S(2)}, u32[]{:S(2)}) %collective-permute-start.6) | collective-permute-done | bytes 98336 | tf_op jit(solution)/shard_map/ppermute | solution.py:664
  19.4 0.8 %shard_map.92 = (f32[2,8,8,256]{3,2,1,0:T(8,128)}, f32[8,8,256]{2,1,0:T(8,128)}, f32[16,8,16,128]{3,2,1,0:T(8,128)}) custom-call(f32[3,8,8,128]{3,2,1,0:T(8,128)S(1)} %get-tuple-element.52.keep, f32[3,8,8,128]{3,2,1,0:T(8,128)S(1)} %collective-permute-done.6.got, f32[16,4,8,128]{3,2,1,0:T(8,128)S(1)} %get-tuple-element.54.rim, ...), custom_call_target="tpu_custom_call", output_to_operand_aliasing={{2}: (3, {})} | custom-call | flops 1000000000 | bytes 4194304 | tf_op jit(solution)/shard_map/pallas_call | solution.py:622
Async XLA Ops:
  2.1 1.7 %collective-permute-start = (f32[30,8,128]{2,1,0:T(8,128)S(1)}, f32[30,8,128]{2,1,0:T(8,128)S(1)}, u32[]{:S(2)}, u32[]{:S(2)}) collective-permute-start(f32[30,8,128]{2,1,0:T(8,128)S(1)} %get-tuple-element.34.to_partner), channel_id=1, source_target_pairs={{0,4},{1,5},{2,6},{3,7},{4,0},{5,1},{6,2},{7,3},{8,12},{9,13},{10,... | collective-permute-start | bytes 368648 | tf_op jit(solution)/shard_map/ppermute | solution.py:664
  3.5 2.5 %collective-permute-start.1 = (f32[16,8,128]{2,1,0:T(8,128)S(1)}, f32[16,8,128]{2,1,0:T(8,128)S(1)}, u32[]{:S(2)}, u32[]{:S(2)}) collective-permute-start(f32[16,8,128]{2,1,0:T(8,128)S(1)} %get-tuple-element.35.g_tracers), channel_id=1, source_target_pairs={{0,4},{1,5},{2,6},{3,7},{4,0},{5,1},{6,2},{7,3},{8,12},{9,13},{10,... | collective-permute-start | bytes 196616 | tf_op jit(solution)/shard_map/ppermute | solution.py:664
  3.8 2.2 %copy-start = (f32[16,16]{1,0:T(8,128)S(1)}, f32[16,16]{1,0:T(8,128)}, u32[]{:S(2)}) copy-start(f32[16,16]{1,0:T(8,128)} %rates.1) | copy-start | bytes 3076
  4.1 3.3 %collective-permute-start.2 = (f32[5,8,128]{2,1,0:T(8,128)S(1)}, f32[5,8,128]{2,1,0:T(8,128)S(1)}, u32[]{:S(2)}, u32[]{:S(2)}) collective-permute-start(f32[5,8,128]{2,1,0:T(8,128)S(1)} %get-tuple-element.45), channel_id=1, source_target_pairs={{0,8},{1,4},{2,5},{3,6},{4,1},{5,2},{6,3},{7,15},{8,0},{9,12},{10,... | collective-permute-start | bytes 61448 | tf_op jit(solution)/shard_map/ppermute | solution.py:664
  5.7 9.4 %collective-permute-start.3 = (f32[40,8,128]{2,1,0:T(8,128)S(1)}, f32[40,8,128]{2,1,0:T(8,128)S(1)}, u32[]{:S(2)}, u32[]{:S(2)}) collective-permute-start(f32[40,8,128]{2,1,0:T(8,128)S(1)} %get-tuple-element.47), channel_id=1, source_target_pairs={{0,8},{1,9},{2,10},{3,11},{4,12},{5,13},{6,14},{7,15},{8,0},{9,1},... | collective-permute-start | bytes 491528 | tf_op jit(solution)/shard_map/ppermute | solution.py:664
  7.6 7.5 %collective-permute-start.5 = (f32[8,128]{1,0:T(8,128)S(1)}, f32[8,128]{1,0:T(8,128)S(1)}, u32[]{:S(2)}, u32[]{:S(2)}) collective-permute-start(f32[8,128]{1,0:T(8,128)S(1)} %get-tuple-element.49), channel_id=1, source_target_pairs={{0,8},{1,9},{2,10},{3,11},{4,12},{5,13},{6,14},{7,15},{8,0},{9,1},... | collective-permute-start | bytes 12296 | tf_op jit(solution)/shard_map/ppermute | solution.py:664
  8.2 8.1 %collective-permute-start.4 = (f32[41,8,128]{2,1,0:T(8,128)S(1)}, f32[41,8,128]{2,1,0:T(8,128)S(1)}, u32[]{:S(2)}, u32[]{:S(2)}) collective-permute-start(f32[41,8,128]{2,1,0:T(8,128)S(1)} %get-tuple-element.48), channel_id=1, source_target_pairs={{0,4},{1,5},{2,6},{3,7},{4,0},{5,1},{6,2},{7,3},{8,16},{9,17},{10,... | collective-permute-start | bytes 503816 | tf_op jit(solution)/shard_map/ppermute | solution.py:664
  18.0 1.5 %collective-permute-start.6 = (f32[3,8,8,128]{3,2,1,0:T(8,128)S(1)}, f32[3,8,8,128]{3,2,1,0:T(8,128)S(1)}, u32[]{:S(2)}, u32[]{:S(2)}) collective-permute-start(f32[3,8,8,128]{3,2,1,0:T(8,128)S(1)} %get-tuple-element.53), channel_id=1, source_target_pairs={{0,4},{1,5},{2,6},{3,7},{4,0},{5,1},{6,2},{7,3},{8,12},{9,13},{10,... | collective-permute-start | bytes 294920 | tf_op jit(solution)/shard_map/ppermute | solution.py:664

commit v9 on v8

--- a/solution.py
+++ b/solution.py
@@ -409,31 +409,34 @@
         x = m[h, r]
         moved[ntr, r] = transport(weights, x, *sides(x, beside(z[h], r, lon)), m[h, r + 1], m[h, r - 1])
 
-    def react(r):
-        both = jnp.concatenate([sat[r + i] for i in range(count)], axis=1)
+    def react(every):
+        both = jnp.concatenate([sat[r] for r in every], axis=1)
         res = jnp.dot(mix[...], both, preferred_element_type=jnp.float32)
         res = res[:half] + res[half:]
-        for i in range(count):
-            gain = react_step * dv[WET, r + i]
+        for i, r in enumerate(every):
+            gain = react_step * dv[WET, r]
             for n in range(ntr):
-                new[n, r + i] = moved[n, r + i] + gain * res[n * nz : (n + 1) * nz, i * lon : (i + 1) * lon]
-
-    def move_all(r):
-        for i in range(count):
-            move(r + i)
+                new[n, r] = moved[n, r] + gain * res[n * nz : (n + 1) * nz, i * lon : (i + 1) * lon]
+
+    def piece(i):
+        return [first + i * apart + k for k in range(count)]
 
     def both_parts(i, _):
-        react(first + (i - 1) * apart)
-        move_all(first + i * apart)
+        react(piece(i - 1))
+        for r in piece(i):
+            move(r)
         return 0
 
-    move_all(first)
     if rows[2] > 1:
-        for i in range(1, times):
-            both_parts(i, 0)
+        every = [r for i in range(times) for r in piece(i)]
+        for r in every:
+            move(r)
+        react(every)
     else:
+        for r in piece(0):
+            move(r)
         lax.fori_loop(1, times, both_parts, 0)
-    react(first + (times - 1) * apart)
+        react(piece(times - 1))
 
 
 def light_rows(m, dv, moved, new, ntr, rows):
@@ -588,31 +591,37 @@
         copy.wait()
 
 
-def finish_kernel(keep, got, rim, out_in, flow_out, temp_out, out, flow, temp, sem):
-    _, lat_dev, nz, lon = keep.shape
-    lat_blk = 2 * lat_dev
+def half_copies(part, core, buffer, flow_out, temp_out, sem):
+    _, lat_dev, _, lon = part.shape
+    for f in range(3):
+        for t in range(lat_dev):
+            buffer[f, :, t, :] = part[f, t]
+    at = pl.ds(pl.multiple_of(core * lon, lon), lon)
+    return [
+        pltpu.make_async_copy(buffer.at[pl.ds(0, 2)], flow_out.at[:, :, :, at], sem.at[0]),
+        pltpu.make_async_copy(buffer.at[2], temp_out.at[:, :, at], sem.at[1]),
+    ]
+
+
+def finish_own_kernel(keep, rim, out_in, flow_out, temp_out, out, buffer, sem):
+    lat_blk = 2 * keep.shape[1]
     copies = [
-        pltpu.make_async_copy(rim.at[:, i], out.at[:, :, t, :], sem.at[i])
+        pltpu.make_async_copy(rim.at[:, i], out.at[:, :, t, :], sem.at[2 + i])
         for i, t in enumerate((0, 1, lat_blk - 2, lat_blk - 1))
     ]
     for copy in copies:
         copy.start()
-    first = place()[0] == 0
-    for f in range(3):
-        for t in range(lat_dev):
-            a, b = (keep[f, t], got[f, t])
-            low, high = (jnp.where(first, a, b), jnp.where(first, b, a))
-            if f < 2:
-                flow[f, :, t, :lon] = low
-                flow[f, :, t, lon:] = high
-            else:
-                temp[:, t, :lon] = low
-                temp[:, t, lon:] = high
-        if f == 1:
-            copies.append(pltpu.make_async_copy(flow, flow_out, sem.at[4]))
-            copies[-1].start()
-    copies.append(pltpu.make_async_copy(temp, temp_out, sem.at[5]))
-    copies[-1].start()
+    more = half_copies(keep, place()[0], buffer, flow_out, temp_out, sem)
+    for copy in more:
+        copy.start()
+    for copy in copies + more:
+        copy.wait()
+
+
+def finish_other_kernel(got, flow_in, temp_in, flow_out, temp_out, buffer, sem):
+    copies = half_copies(got, 1 - place()[0], buffer, flow_out, temp_out, sem)
+    for copy in copies:
+        copy.start()
     for copy in copies:
         copy.wait()
 
@@ -733,17 +742,29 @@
         scratch=[full, full, derived, derived] + work + [pltpu.SemaphoreType.DMA((lat_blk - 4,))],
         away=(0,),
     )
+    returned = swap(send, partner)
+    buffer = (3, nz, lat_dev, lon)
     flow_out, temp_out, out = call(
-        finish_kernel,
+        finish_own_kernel,
         [flow.shape, temp.shape, out.shape],
         keep,
-        swap(send, partner),
         rim,
         out,
-        scratch=[flow.shape, temp.shape, pltpu.SemaphoreType.DMA((6,))],
-        far=(3,),
+        scratch=[buffer, pltpu.SemaphoreType.DMA((6,))],
+        far=(2,),
         away=(0, 1, 2),
-        aliases={3: 2},
+        aliases={2: 2},
+    )
+    flow_out, temp_out = call(
+        finish_other_kernel,
+        [flow.shape, temp.shape],
+        returned,
+        flow_out,
+        temp_out,
+        scratch=[buffer, pltpu.SemaphoreType.DMA((2,))],
+        far=(1, 2),
+        away=(0, 1),
+        aliases={1: 0, 2: 1},
     )
     return (flow_out, temp_out, out[None])
 

time: 20.4 us -> 20.3 us (level)
  waiting for transfers between devices: 3.02 us -> 2.24 us
  Pallas kernels: 10.9 us -> 11.5 us
    ppermute x7, waiting for transfers between devices: 3.02 us -> 2.24 us  [swap(): return lax.ppermute(x, ('row', 'col'), pairs)]
    pallas_call x8 -> x9, Pallas kernels: 10.9 us -> 11.5 us  [call(): pl.pallas_call(kernel, out_shape=[jax.ShapeDtypeStruct(s, jnp.float32) if...]
  transfers between devices with their start and end apart: 7 -> 7, of which waited for: 4 -> 4; matrix products, arithmetic and copies ran while one was open for 0% -> 0% of each run, Pallas kernels for 34% -> 38%
where the time goes in v9:
time: 20.3 us; the launch traced here: 20.2 us
  Pallas kernels  11.5 us (57%)
  starting transfers between devices  5.67 us (28%)
  waiting for transfers between devices  2.24 us (11%)
  between operations  0.7 us (3%)
    pallas_call x9, Pallas kernels, call(): pl.pallas_call(kernel, out_shape=[jax.ShapeDtypeStruct(s, jnp.float32) if...  11.5 us
    ppermute x7, starting transfers between devices, swap(): return lax.ppermute(x, ('row', 'col'), pairs)  5.67 us
    ppermute x7, waiting for transfers between devices, swap(): return lax.ppermute(x, ('row', 'col'), pairs)  2.24 us
  transfers between devices with their start and end apart: 7, of which 4 were waited for; matrix products, arithmetic and copies ran while one was open for 0% of the time, Pallas kernels for 38%

profile of v9, /device:TPU:3, one launch (start us, length us, event | category | flops | bytes accessed | tf_op | source)
XLA Modules:
  0.0 20.2 jit_solution(12606223725751754626)
XLA Ops:
  0.6 1.4 %shard_map.85 = (f32[4,8,8,128]{3,2,1,0:T(8,128)S(1)}, f32[30,8,128]{2,1,0:T(8,128)S(1)}, f32[4,8,128]{2,1,0:T(8,128)S(1)}, f32[16,8,16,128]{3,2,1,0:T(8,128)S(1)}) custom-call(f32[2,8,8,256]{3,2,1,0:T(8,128)} %flow_in.1, f32[8,8,256]{2,1,0:T(8,128)} %temp_in.1, s32[8,256]{1,0:T(8,128)} %bottom_in.1, f32[8,256]{1,0:T(8,128)} %sunlight_in.1, ...), custom_call_target="tpu_custom_call" | custom-call | flops 1000000000 | bytes 4194304 | tf_op jit(solution)/shard_map/pallas_call | solution.py:631
  2.1 0.7 %collective-permute-start = (f32[30,8,128]{2,1,0:T(8,128)S(1)}, f32[30,8,128]{2,1,0:T(8,128)S(1)}, u32[]{:S(2)}, u32[]{:S(2)}) collective-permute-start(f32[30,8,128]{2,1,0:T(8,128)S(1)} %get-tuple-element.36.to_partner), channel_id=1, source_target_pairs={{0,4},{1,5},{2,6},{3,7},{4,0},{5,1},{6,2},{7,3},{8,12},{9,13},{10,... | collective-permute-start | bytes 368648 | tf_op jit(solution)/shard_map/ppermute | solution.py:673
  2.8 0.7 %shard_map.86 = (f32[16,16,8,128]{3,2,1,0:T(8,128)S(1)}, f32[16,8,128]{2,1,0:T(8,128)S(1)}) custom-call(f32[16,8,16,128]{3,2,1,0:T(8,128)S(1)} %get-tuple-element.33.tracers), custom_call_target="tpu_custom_call" | custom-call | flops 1000000000 | bytes 4194304 | tf_op jit(solution)/shard_map/pallas_call | solution.py:631
  3.5 0.1 collective-permute-start.1
  3.6 0.2 collective-permute-done.got
  3.8 0.0 copy-start
  3.8 0.3 %shard_map.87 = (f32[4,16,8,128]{3,2,1,0:T(8,128)S(1)}, f32[20,8,128]{2,1,0:T(8,128)S(1)}, f32[5,8,128]{2,1,0:T(8,128)S(1)}, f32[40,8,128]{2,1,0:T(8,128)S(1)}) custom-call(f32[4,8,8,128]{3,2,1,0:T(8,128)S(1)} %get-tuple-element.35.mine, f32[30,8,128]{2,1,0:T(8,128)S(1)} %collective-permute-done.got, f32[30,8,128]{2,1,0:T(8,128)S(1)} %get-tuple-element.36.to_partner, ...), custom_call_target="tpu_custom_call" | custom-call | flops 1000000000 | bytes 4194304 | tf_op jit(solution)/shard_map/pallas_call | solution.py:631
  4.1 1.6 %collective-permute-start.2 = (f32[5,8,128]{2,1,0:T(8,128)S(1)}, f32[5,8,128]{2,1,0:T(8,128)S(1)}, u32[]{:S(2)}, u32[]{:S(2)}) collective-permute-start(f32[5,8,128]{2,1,0:T(8,128)S(1)} %get-tuple-element.47), channel_id=1, source_target_pairs={{0,8},{1,4},{2,5},{3,6},{4,1},{5,2},{6,3},{7,15},{8,0},{9,12},{10,... | collective-permute-start | bytes 61448 | tf_op jit(solution)/shard_map/ppermute | solution.py:673
  5.7 0.3 %collective-permute-start.3 = (f32[40,8,128]{2,1,0:T(8,128)S(1)}, f32[40,8,128]{2,1,0:T(8,128)S(1)}, u32[]{:S(2)}, u32[]{:S(2)}) collective-permute-start(f32[40,8,128]{2,1,0:T(8,128)S(1)} %get-tuple-element.49), channel_id=1, source_target_pairs={{0,8},{1,9},{2,10},{3,11},{4,12},{5,13},{6,14},{7,15},{8,0},{9,1},... | collective-permute-start | bytes 491528 | tf_op jit(solution)/shard_map/ppermute | solution.py:673
  6.0 0.0 collective-permute-done.1.g_partner
  6.0 0.0 copy-done
  6.0 0.7 %shard_map.88 = (f32[20,20,8,128]{3,2,1,0:T(8,128)S(1)}, f32[3,20,8,128]{3,2,1,0:T(8,128)S(1)}, bf16[256,256]{1,0:T(8,128)(2,1)S(1)}, f32[20,8,128]{2,1,0:T(8,12...) custom-call(f32[16,16,8,128]{3,2,1,0:T(8,128)S(1)} %get-tuple-element.34.turned, ...), custom_call_target="tpu_custom_call" | custom-call | flops 1000000000 | bytes 4194304 | tf_op jit(solution)/shard_map/pallas_call | solution.py:631
  6.7 0.7 %collective-permute-done.2.from_outer = f32[5,8,128]{2,1,0:T(8,128)S(1)} collective-permute-done((f32[5,8,128]{2,1,0:T(8,128)S(1)}, f32[5,8,128]{2,1,0:T(8,128)S(1)}, u32[]{:S(2)}, u32[]{:S(2)}) %collective-permute-start.2) | collective-permute-done | bytes 20512 | tf_op jit(solution)/shard_map/ppermute | solution.py:673
  7.4 0.2 shard_map.89
  7.6 0.7 %collective-permute-start.5 = (f32[8,128]{1,0:T(8,128)S(1)}, f32[8,128]{1,0:T(8,128)S(1)}, u32[]{:S(2)}, u32[]{:S(2)}) collective-permute-start(f32[8,128]{1,0:T(8,128)S(1)} %get-tuple-element.51), channel_id=1, source_target_pairs={{0,8},{1,9},{2,10},{3,11},{4,12},{5,13},{6,14},{7,15},{8,0},{9,1},... | collective-permute-start | bytes 12296 | tf_op jit(solution)/shard_map/ppermute | solution.py:673
  8.2 1.8 %collective-permute-start.4 = (f32[41,8,128]{2,1,0:T(8,128)S(1)}, f32[41,8,128]{2,1,0:T(8,128)S(1)}, u32[]{:S(2)}, u32[]{:S(2)}) collective-permute-start(f32[41,8,128]{2,1,0:T(8,128)S(1)} %get-tuple-element.50), channel_id=1, source_target_pairs={{0,4},{1,5},{2,6},{3,7},{4,0},{5,1},{6,2},{7,3},{8,16},{9,17},{10,... | collective-permute-start | bytes 503816 | tf_op jit(solution)/shard_map/ppermute | solution.py:673
  10.0 5.0 %shard_map.90 = (f32[20,20,8,128]{3,2,1,0:T(8,128)S(1)}, f32[20,20,8,128]{3,2,1,0:T(8,128)S(1)}) custom-call(f32[20,20,8,128]{3,2,1,0:T(8,128)S(1)} %get-tuple-element.41.m0.m_own, f32[3,20,8,128]{3,2,1,0:T(8,128)S(1)} %get-tuple-element.42.dv.dv_own, bf16[256,256]{1,0:T(8,128)(2,1)S(1)} %get-tuple-element.43.mix, f32[20,8,128]{2,1,0:T(8,128)S(1)} %get-tuple-element.44.g0, ...), custom_call_target="tpu_custom_call" | custom-call | flops 20000000000 | bytes 83886080 | tf_op jit(solution)/shard_map/pallas_call | solution.py:631
  15.1 0.0 collective-permute-done.5.edge_a
  15.1 0.0 collective-permute-done.3.rows_a
  15.1 1.2 %collective-permute-done.4.rows_b = f32[41,8,128]{2,1,0:T(8,128)S(1)} collective-permute-done((f32[41,8,128]{2,1,0:T(8,128)S(1)}, f32[41,8,128]{2,1,0:T(8,128)S(1)}, u32[]{:S(2)}, u32[]{:S(2)}) %collective-permute-start.4) | collective-permute-done | bytes 167968 | tf_op jit(solution)/shard_map/ppermute | solution.py:673
  16.3 1.6 %shard_map.91 = (f32[16,8,16,128]{3,2,1,0:T(8,128)}, f32[16,4,8,128]{3,2,1,0:T(8,128)S(1)}, f32[3,8,8,128]{3,2,1,0:T(8,128)S(1)}, f32[3,8,8,128]{3,2,1,0:T(8,128)S(1)}) custom-call(f32[20,20,8,128]{3,2,1,0:T(8,128)S(1)} %get-tuple-element.41.m0.m_own, f32[3,20,8,128]{3,2,1,0:T(8,128)S(1)} %get-tuple-element.42.dv.dv_own, ...), custom_call_target="tpu_custom_call" | custom-call | flops 1000000000 | bytes 4194304 | tf_op jit(solution)/shard_map/pallas_call | solution.py:631
  18.0 0.5 %collective-permute-start.6 = (f32[3,8,8,128]{3,2,1,0:T(8,128)S(1)}, f32[3,8,8,128]{3,2,1,0:T(8,128)S(1)}, u32[]{:S(2)}, u32[]{:S(2)}) collective-permute-start(f32[3,8,8,128]{3,2,1,0:T(8,128)S(1)} %get-tuple-element.54), channel_id=1, source_target_pairs={{0,4},{1,5},{2,6},{3,7},{4,0},{5,1},{6,2},{7,3},{8,12},{9,13},{10,... | collective-permute-start | bytes 294920 | tf_op jit(solution)/shard_map/ppermute | solution.py:673
  18.5 0.8 %shard_map.92 = (f32[2,8,8,256]{3,2,1,0:T(8,128)}, f32[8,8,256]{2,1,0:T(8,128)}, f32[16,8,16,128]{3,2,1,0:T(8,128)}) custom-call(f32[3,8,8,128]{3,2,1,0:T(8,128)S(1)} %get-tuple-element.55.keep, f32[16,4,8,128]{3,2,1,0:T(8,128)S(1)} %get-tuple-element.56.rim, f32[16,8,16,128]{3,2,1,0:T(8,128)} %get-tuple-element.57.out_in), custom_call_target="tpu_custom_call", output_to_operand_aliasing={{2}: (2, {})} | custom-call | flops 1000000000 | bytes 4194304 | tf_op jit(solution)/shard_map/pallas_call | solution.py:631
  19.3 0.2 collective-permute-done.6.got
  19.4 0.7 %shard_map.93 = (f32[2,8,8,256]{3,2,1,0:T(8,128)}, f32[8,8,256]{2,1,0:T(8,128)}) custom-call(f32[3,8,8,128]{3,2,1,0:T(8,128)S(1)} %collective-permute-done.6.got, f32[2,8,8,256]{3,2,1,0:T(8,128)} %get-tuple-element.58.flow_in, f32[8,8,256]{2,1,0:T(8,128)} %get-tuple-element.59.temp_in), custom_call_target="tpu_custom_call", output_to_operand_aliasing={{0}: (1, {}), {1}: (2, {})} | custom-call | flops 1000000000 | bytes 4194304 | tf_op jit(solution)/shard_map/pallas_call | solution.py:631
Async XLA Ops:
  2.1 1.7 %collective-permute-start = (f32[30,8,128]{2,1,0:T(8,128)S(1)}, f32[30,8,128]{2,1,0:T(8,128)S(1)}, u32[]{:S(2)}, u32[]{:S(2)}) collective-permute-start(f32[30,8,128]{2,1,0:T(8,128)S(1)} %get-tuple-element.36.to_partner), channel_id=1, source_target_pairs={{0,4},{1,5},{2,6},{3,7},{4,0},{5,1},{6,2},{7,3},{8,12},{9,13},{10,... | collective-permute-start | bytes 368648 | tf_op jit(solution)/shard_map/ppermute | solution.py:673
  3.5 2.5 %collective-permute-start.1 = (f32[16,8,128]{2,1,0:T(8,128)S(1)}, f32[16,8,128]{2,1,0:T(8,128)S(1)}, u32[]{:S(2)}, u32[]{:S(2)}) collective-permute-start(f32[16,8,128]{2,1,0:T(8,128)S(1)} %get-tuple-element.37.g_tracers), channel_id=1, source_target_pairs={{0,4},{1,5},{2,6},{3,7},{4,0},{5,1},{6,2},{7,3},{8,12},{9,13},{10,... | collective-permute-start | bytes 196616 | tf_op jit(solution)/shard_map/ppermute | solution.py:673
  3.8 2.2 %copy-start = (f32[16,16]{1,0:T(8,128)S(1)}, f32[16,16]{1,0:T(8,128)}, u32[]{:S(2)}) copy-start(f32[16,16]{1,0:T(8,128)} %rates.1) | copy-start | bytes 3076
  4.1 3.3 %collective-permute-start.2 = (f32[5,8,128]{2,1,0:T(8,128)S(1)}, f32[5,8,128]{2,1,0:T(8,128)S(1)}, u32[]{:S(2)}, u32[]{:S(2)}) collective-permute-start(f32[5,8,128]{2,1,0:T(8,128)S(1)} %get-tuple-element.47), channel_id=1, source_target_pairs={{0,8},{1,4},{2,5},{3,6},{4,1},{5,2},{6,3},{7,15},{8,0},{9,12},{10,... | collective-permute-start | bytes 61448 | tf_op jit(solution)/shard_map/ppermute | solution.py:673
  5.7 9.4 %collective-permute-start.3 = (f32[40,8,128]{2,1,0:T(8,128)S(1)}, f32[40,8,128]{2,1,0:T(8,128)S(1)}, u32[]{:S(2)}, u32[]{:S(2)}) collective-permute-start(f32[40,8,128]{2,1,0:T(8,128)S(1)} %get-tuple-element.49), channel_id=1, source_target_pairs={{0,8},{1,9},{2,10},{3,11},{4,12},{5,13},{6,14},{7,15},{8,0},{9,1},... | collective-permute-start | bytes 491528 | tf_op jit(solution)/shard_map/ppermute | solution.py:673
  7.6 7.5 %collective-permute-start.5 = (f32[8,128]{1,0:T(8,128)S(1)}, f32[8,128]{1,0:T(8,128)S(1)}, u32[]{:S(2)}, u32[]{:S(2)}) collective-permute-start(f32[8,128]{1,0:T(8,128)S(1)} %get-tuple-element.51), channel_id=1, source_target_pairs={{0,8},{1,9},{2,10},{3,11},{4,12},{5,13},{6,14},{7,15},{8,0},{9,1},... | collective-permute-start | bytes 12296 | tf_op jit(solution)/shard_map/ppermute | solution.py:673
  8.2 8.1 %collective-permute-start.4 = (f32[41,8,128]{2,1,0:T(8,128)S(1)}, f32[41,8,128]{2,1,0:T(8,128)S(1)}, u32[]{:S(2)}, u32[]{:S(2)}) collective-permute-start(f32[41,8,128]{2,1,0:T(8,128)S(1)} %get-tuple-element.50), channel_id=1, source_target_pairs={{0,4},{1,5},{2,6},{3,7},{4,0},{5,1},{6,2},{7,3},{8,16},{9,17},{10,... | collective-permute-start | bytes 503816 | tf_op jit(solution)/shard_map/ppermute | solution.py:673
  18.0 1.5 %collective-permute-start.6 = (f32[3,8,8,128]{3,2,1,0:T(8,128)S(1)}, f32[3,8,8,128]{3,2,1,0:T(8,128)S(1)}, u32[]{:S(2)}, u32[]{:S(2)}) collective-permute-start(f32[3,8,8,128]{3,2,1,0:T(8,128)S(1)} %get-tuple-element.54), channel_id=1, source_target_pairs={{0,4},{1,5},{2,6},{3,7},{4,0},{5,1},{6,2},{7,3},{8,12},{9,13},{10,... | collective-permute-start | bytes 294920 | tf_op jit(solution)/shard_map/ppermute | solution.py:673

commit v10 on v9

--- a/solution.py
+++ b/solution.py
@@ -329,7 +329,7 @@
 
 
 KAP, PRS, WET = (0, 1, 2)
-GROUP = 4
+GROUP = 8
 PACK = 8
 PIECE = 3
 
@@ -534,7 +534,7 @@
     even = chip % 2 == 0
     south_ok, north_ok = (chip > 0, chip < lax.axis_size("row") // 2 - 1)
     copies = [
-        pltpu.make_async_copy(m2_in.at[pl.ds(0, ntr), r], out.at[:, :, r - 2, :], sem.at[r - 4]) for r in range(4, rows - 4)
+        pltpu.make_async_copy(m2_in.at[pl.ds(0, ntr), r], out.at[:, :, r - 2, :], sem.at[r - 4]) for r in range(4, rows // 2)
     ]
     for copy in copies:
         copy.start()
@@ -603,11 +603,16 @@
     ]
 
 
-def finish_own_kernel(keep, rim, out_in, flow_out, temp_out, out, buffer, sem):
+def finish_own_kernel(keep, rim, m, out_in, flow_out, temp_out, out, buffer, sem):
     lat_blk = 2 * keep.shape[1]
     copies = [
         pltpu.make_async_copy(rim.at[:, i], out.at[:, :, t, :], sem.at[2 + i])
         for i, t in enumerate((0, 1, lat_blk - 2, lat_blk - 1))
+    ]
+    rows, ntr = (m.shape[1], rim.shape[0])
+    copies += [
+        pltpu.make_async_copy(m.at[pl.ds(0, ntr), r], out.at[:, :, r - 2, :], sem.at[6 + r - rows // 2])
+        for r in range(rows // 2, rows - 4)
     ]
     for copy in copies:
         copy.start()
@@ -749,11 +754,12 @@
         [flow.shape, temp.shape, out.shape],
         keep,
         rim,
+        m2,
         out,
-        scratch=[buffer, pltpu.SemaphoreType.DMA((6,))],
-        far=(2,),
+        scratch=[buffer, pltpu.SemaphoreType.DMA((6 + rows // 2 - 4,))],
+        far=(3,),
         away=(0, 1, 2),
-        aliases={2: 2},
+        aliases={3: 2},
     )
     flow_out, temp_out = call(
         finish_other_kernel,

time: 20.3 us -> 20.3 us (level)
  transfers between devices with their start and end apart: 7 -> 7, of which waited for: 4 -> 3; matrix products, arithmetic and copies ran while one was open for 0% -> 0% of each run, Pallas kernels for 38% -> 39%
where the time goes in v10:
time: 20.3 us; the launch traced here: 20.2 us
  Pallas kernels  11.7 us (58%)
  starting transfers between devices  5.66 us (28%)
  waiting for transfers between devices  2.08 us (10%)
  between operations  0.71 us (3%)
    pallas_call x9, Pallas kernels, call(): pl.pallas_call(kernel, out_shape=[jax.ShapeDtypeStruct(s, jnp.float32) if...  11.7 us
    ppermute x7, starting transfers between devices, swap(): return lax.ppermute(x, ('row', 'col'), pairs)  5.66 us
    ppermute x7, waiting for transfers between devices, swap(): return lax.ppermute(x, ('row', 'col'), pairs)  2.08 us
  transfers between devices with their start and end apart: 7, of which 3 were waited for; matrix products, arithmetic and copies ran while one was open for 0% of the time, Pallas kernels for 39%

profile of v10, /device:TPU:3, one launch (start us, length us, event | category | flops | bytes accessed | tf_op | source)
XLA Modules:
  0.0 20.2 jit_solution(14691459819061864837)
XLA Ops:
  0.6 1.4 %shard_map.85 = (f32[4,8,8,128]{3,2,1,0:T(8,128)S(1)}, f32[30,8,128]{2,1,0:T(8,128)S(1)}, f32[4,8,128]{2,1,0:T(8,128)S(1)}, f32[16,8,16,128]{3,2,1,0:T(8,128)S(1)}) custom-call(f32[2,8,8,256]{3,2,1,0:T(8,128)} %flow_in.1, f32[8,8,256]{2,1,0:T(8,128)} %temp_in.1, s32[8,256]{1,0:T(8,128)} %bottom_in.1, f32[8,256]{1,0:T(8,128)} %sunlight_in.1, ...), custom_call_target="tpu_custom_call" | custom-call | flops 1000000000 | bytes 4194304 | tf_op jit(solution)/shard_map/pallas_call | solution.py:636
  2.1 0.7 %collective-permute-start = (f32[30,8,128]{2,1,0:T(8,128)S(1)}, f32[30,8,128]{2,1,0:T(8,128)S(1)}, u32[]{:S(2)}, u32[]{:S(2)}) collective-permute-start(f32[30,8,128]{2,1,0:T(8,128)S(1)} %get-tuple-element.36.to_partner), channel_id=1, source_target_pairs={{0,4},{1,5},{2,6},{3,7},{4,0},{5,1},{6,2},{7,3},{8,12},{9,13},{10,... | collective-permute-start | bytes 368648 | tf_op jit(solution)/shard_map/ppermute | solution.py:678
  2.8 0.7 %shard_map.86 = (f32[16,16,8,128]{3,2,1,0:T(8,128)S(1)}, f32[16,8,128]{2,1,0:T(8,128)S(1)}) custom-call(f32[16,8,16,128]{3,2,1,0:T(8,128)S(1)} %get-tuple-element.33.tracers), custom_call_target="tpu_custom_call" | custom-call | flops 1000000000 | bytes 4194304 | tf_op jit(solution)/shard_map/pallas_call | solution.py:636
  3.5 0.1 collective-permute-start.1
  3.6 0.2 collective-permute-done.got
  3.8 0.0 copy-start
  3.8 0.3 %shard_map.87 = (f32[4,16,8,128]{3,2,1,0:T(8,128)S(1)}, f32[20,8,128]{2,1,0:T(8,128)S(1)}, f32[5,8,128]{2,1,0:T(8,128)S(1)}, f32[40,8,128]{2,1,0:T(8,128)S(1)}) custom-call(f32[4,8,8,128]{3,2,1,0:T(8,128)S(1)} %get-tuple-element.35.mine, f32[30,8,128]{2,1,0:T(8,128)S(1)} %collective-permute-done.got, f32[30,8,128]{2,1,0:T(8,128)S(1)} %get-tuple-element.36.to_partner, ...), custom_call_target="tpu_custom_call" | custom-call | flops 1000000000 | bytes 4194304 | tf_op jit(solution)/shard_map/pallas_call | solution.py:636
  4.1 1.6 %collective-permute-start.2 = (f32[5,8,128]{2,1,0:T(8,128)S(1)}, f32[5,8,128]{2,1,0:T(8,128)S(1)}, u32[]{:S(2)}, u32[]{:S(2)}) collective-permute-start(f32[5,8,128]{2,1,0:T(8,128)S(1)} %get-tuple-element.47), channel_id=1, source_target_pairs={{0,8},{1,4},{2,5},{3,6},{4,1},{5,2},{6,3},{7,15},{8,0},{9,12},{10,... | collective-permute-start | bytes 61448 | tf_op jit(solution)/shard_map/ppermute | solution.py:678
  5.7 0.3 %collective-permute-start.3 = (f32[40,8,128]{2,1,0:T(8,128)S(1)}, f32[40,8,128]{2,1,0:T(8,128)S(1)}, u32[]{:S(2)}, u32[]{:S(2)}) collective-permute-start(f32[40,8,128]{2,1,0:T(8,128)S(1)} %get-tuple-element.49), channel_id=1, source_target_pairs={{0,8},{1,9},{2,10},{3,11},{4,12},{5,13},{6,14},{7,15},{8,0},{9,1},... | collective-permute-start | bytes 491528 | tf_op jit(solution)/shard_map/ppermute | solution.py:678
  6.0 0.0 collective-permute-done.1.g_partner
  6.0 0.0 copy-done
  6.0 0.7 %shard_map.88 = (f32[20,20,8,128]{3,2,1,0:T(8,128)S(1)}, f32[3,20,8,128]{3,2,1,0:T(8,128)S(1)}, bf16[256,256]{1,0:T(8,128)(2,1)S(1)}, f32[20,8,128]{2,1,0:T(8,12...) custom-call(f32[16,16,8,128]{3,2,1,0:T(8,128)S(1)} %get-tuple-element.34.turned, ...), custom_call_target="tpu_custom_call" | custom-call | flops 1000000000 | bytes 4194304 | tf_op jit(solution)/shard_map/pallas_call | solution.py:636
  6.7 0.7 %collective-permute-done.2.from_outer = f32[5,8,128]{2,1,0:T(8,128)S(1)} collective-permute-done((f32[5,8,128]{2,1,0:T(8,128)S(1)}, f32[5,8,128]{2,1,0:T(8,128)S(1)}, u32[]{:S(2)}, u32[]{:S(2)}) %collective-permute-start.2) | collective-permute-done | bytes 20512 | tf_op jit(solution)/shard_map/ppermute | solution.py:678
  7.4 0.2 shard_map.89
  7.5 0.7 %collective-permute-start.5 = (f32[8,128]{1,0:T(8,128)S(1)}, f32[8,128]{1,0:T(8,128)S(1)}, u32[]{:S(2)}, u32[]{:S(2)}) collective-permute-start(f32[8,128]{1,0:T(8,128)S(1)} %get-tuple-element.51), channel_id=1, source_target_pairs={{0,8},{1,9},{2,10},{3,11},{4,12},{5,13},{6,14},{7,15},{8,0},{9,1},... | collective-permute-start | bytes 12296 | tf_op jit(solution)/shard_map/ppermute | solution.py:678
  8.2 1.8 %collective-permute-start.4 = (f32[41,8,128]{2,1,0:T(8,128)S(1)}, f32[41,8,128]{2,1,0:T(8,128)S(1)}, u32[]{:S(2)}, u32[]{:S(2)}) collective-permute-start(f32[41,8,128]{2,1,0:T(8,128)S(1)} %get-tuple-element.50), channel_id=1, source_target_pairs={{0,4},{1,5},{2,6},{3,7},{4,0},{5,1},{6,2},{7,3},{8,16},{9,17},{10,... | collective-permute-start | bytes 503816 | tf_op jit(solution)/shard_map/ppermute | solution.py:678
  10.0 5.0 %shard_map.90 = (f32[20,20,8,128]{3,2,1,0:T(8,128)S(1)}, f32[20,20,8,128]{3,2,1,0:T(8,128)S(1)}) custom-call(f32[20,20,8,128]{3,2,1,0:T(8,128)S(1)} %get-tuple-element.41.m0.m_own, f32[3,20,8,128]{3,2,1,0:T(8,128)S(1)} %get-tuple-element.42.dv.dv_own, bf16[256,256]{1,0:T(8,128)(2,1)S(1)} %get-tuple-element.43.mix, f32[20,8,128]{2,1,0:T(8,128)S(1)} %get-tuple-element.44.g0, ...), custom_call_target="tpu_custom_call" | custom-call | flops 20000000000 | bytes 83886080 | tf_op jit(solution)/shard_map/pallas_call | solution.py:636
  15.1 0.0 collective-permute-done.5.edge_a
  15.1 0.0 collective-permute-done.3.rows_a
  15.1 1.2 %collective-permute-done.4.rows_b = f32[41,8,128]{2,1,0:T(8,128)S(1)} collective-permute-done((f32[41,8,128]{2,1,0:T(8,128)S(1)}, f32[41,8,128]{2,1,0:T(8,128)S(1)}, u32[]{:S(2)}, u32[]{:S(2)}) %collective-permute-start.4) | collective-permute-done | bytes 167968 | tf_op jit(solution)/shard_map/ppermute | solution.py:678
  16.3 1.6 %shard_map.91 = (f32[16,8,16,128]{3,2,1,0:T(8,128)}, f32[16,4,8,128]{3,2,1,0:T(8,128)S(1)}, f32[3,8,8,128]{3,2,1,0:T(8,128)S(1)}, f32[3,8,8,128]{3,2,1,0:T(8,128)S(1)}) custom-call(f32[20,20,8,128]{3,2,1,0:T(8,128)S(1)} %get-tuple-element.41.m0.m_own, f32[3,20,8,128]{3,2,1,0:T(8,128)S(1)} %get-tuple-element.42.dv.dv_own, ...), custom_call_target="tpu_custom_call" | custom-call | flops 1000000000 | bytes 4194304 | tf_op jit(solution)/shard_map/pallas_call | solution.py:636
  17.9 0.5 %collective-permute-start.6 = (f32[3,8,8,128]{3,2,1,0:T(8,128)S(1)}, f32[3,8,8,128]{3,2,1,0:T(8,128)S(1)}, u32[]{:S(2)}, u32[]{:S(2)}) collective-permute-start(f32[3,8,8,128]{3,2,1,0:T(8,128)S(1)} %get-tuple-element.54), channel_id=1, source_target_pairs={{0,4},{1,5},{2,6},{3,7},{4,0},{5,1},{6,2},{7,3},{8,12},{9,13},{10,... | collective-permute-start | bytes 294920 | tf_op jit(solution)/shard_map/ppermute | solution.py:678
  18.5 1.0 %shard_map.92 = (f32[2,8,8,256]{3,2,1,0:T(8,128)}, f32[8,8,256]{2,1,0:T(8,128)}, f32[16,8,16,128]{3,2,1,0:T(8,128)}) custom-call(f32[3,8,8,128]{3,2,1,0:T(8,128)S(1)} %get-tuple-element.55.keep, f32[16,4,8,128]{3,2,1,0:T(8,128)S(1)} %get-tuple-element.56.rim, f32[20,20,8,128]{3,2,1,0:T(8,128)S(1)} %get-tuple-element.53.m2_in.m, ...), custom_call_target="tpu_custom_call", output_to_operand_aliasing={{2}: (3, {})} | custom-call | flops 1000000000 | bytes 4194304 | tf_op jit(solution)/shard_map/pallas_call | solution.py:636
  19.4 0.0 collective-permute-done.6.got
  19.4 0.7 %shard_map.93 = (f32[2,8,8,256]{3,2,1,0:T(8,128)}, f32[8,8,256]{2,1,0:T(8,128)}) custom-call(f32[3,8,8,128]{3,2,1,0:T(8,128)S(1)} %collective-permute-done.6.got, f32[2,8,8,256]{3,2,1,0:T(8,128)} %get-tuple-element.58.flow_in, f32[8,8,256]{2,1,0:T(8,128)} %get-tuple-element.59.temp_in), custom_call_target="tpu_custom_call", output_to_operand_aliasing={{0}: (1, {}), {1}: (2, {})} | custom-call | flops 1000000000 | bytes 4194304 | tf_op jit(solution)/shard_map/pallas_call | solution.py:636
Async XLA Ops:
  2.1 1.7 %collective-permute-start = (f32[30,8,128]{2,1,0:T(8,128)S(1)}, f32[30,8,128]{2,1,0:T(8,128)S(1)}, u32[]{:S(2)}, u32[]{:S(2)}) collective-permute-start(f32[30,8,128]{2,1,0:T(8,128)S(1)} %get-tuple-element.36.to_partner), channel_id=1, source_target_pairs={{0,4},{1,5},{2,6},{3,7},{4,0},{5,1},{6,2},{7,3},{8,12},{9,13},{10,... | collective-permute-start | bytes 368648 | tf_op jit(solution)/shard_map/ppermute | solution.py:678
  3.5 2.5 %collective-permute-start.1 = (f32[16,8,128]{2,1,0:T(8,128)S(1)}, f32[16,8,128]{2,1,0:T(8,128)S(1)}, u32[]{:S(2)}, u32[]{:S(2)}) collective-permute-start(f32[16,8,128]{2,1,0:T(8,128)S(1)} %get-tuple-element.37.g_tracers), channel_id=1, source_target_pairs={{0,4},{1,5},{2,6},{3,7},{4,0},{5,1},{6,2},{7,3},{8,12},{9,13},{10,... | collective-permute-start | bytes 196616 | tf_op jit(solution)/shard_map/ppermute | solution.py:678
  3.8 2.2 %copy-start = (f32[16,16]{1,0:T(8,128)S(1)}, f32[16,16]{1,0:T(8,128)}, u32[]{:S(2)}) copy-start(f32[16,16]{1,0:T(8,128)} %rates.1) | copy-start | bytes 3076
  4.1 3.3 %collective-permute-start.2 = (f32[5,8,128]{2,1,0:T(8,128)S(1)}, f32[5,8,128]{2,1,0:T(8,128)S(1)}, u32[]{:S(2)}, u32[]{:S(2)}) collective-permute-start(f32[5,8,128]{2,1,0:T(8,128)S(1)} %get-tuple-element.47), channel_id=1, source_target_pairs={{0,8},{1,4},{2,5},{3,6},{4,1},{5,2},{6,3},{7,15},{8,0},{9,12},{10,... | collective-permute-start | bytes 61448 | tf_op jit(solution)/shard_map/ppermute | solution.py:678
  5.7 9.4 %collective-permute-start.3 = (f32[40,8,128]{2,1,0:T(8,128)S(1)}, f32[40,8,128]{2,1,0:T(8,128)S(1)}, u32[]{:S(2)}, u32[]{:S(2)}) collective-permute-start(f32[40,8,128]{2,1,0:T(8,128)S(1)} %get-tuple-element.49), channel_id=1, source_target_pairs={{0,8},{1,9},{2,10},{3,11},{4,12},{5,13},{6,14},{7,15},{8,0},{9,1},... | collective-permute-start | bytes 491528 | tf_op jit(solution)/shard_map/ppermute | solution.py:678
  7.5 7.5 %collective-permute-start.5 = (f32[8,128]{1,0:T(8,128)S(1)}, f32[8,128]{1,0:T(8,128)S(1)}, u32[]{:S(2)}, u32[]{:S(2)}) collective-permute-start(f32[8,128]{1,0:T(8,128)S(1)} %get-tuple-element.51), channel_id=1, source_target_pairs={{0,8},{1,9},{2,10},{3,11},{4,12},{5,13},{6,14},{7,15},{8,0},{9,1},... | collective-permute-start | bytes 12296 | tf_op jit(solution)/shard_map/ppermute | solution.py:678
  8.2 8.1 %collective-permute-start.4 = (f32[41,8,128]{2,1,0:T(8,128)S(1)}, f32[41,8,128]{2,1,0:T(8,128)S(1)}, u32[]{:S(2)}, u32[]{:S(2)}) collective-permute-start(f32[41,8,128]{2,1,0:T(8,128)S(1)} %get-tuple-element.50), channel_id=1, source_target_pairs={{0,4},{1,5},{2,6},{3,7},{4,0},{5,1},{6,2},{7,3},{8,16},{9,17},{10,... | collective-permute-start | bytes 503816 | tf_op jit(solution)/shard_map/ppermute | solution.py:678
  17.9 1.5 %collective-permute-start.6 = (f32[3,8,8,128]{3,2,1,0:T(8,128)S(1)}, f32[3,8,8,128]{3,2,1,0:T(8,128)S(1)}, u32[]{:S(2)}, u32[]{:S(2)}) collective-permute-start(f32[3,8,8,128]{3,2,1,0:T(8,128)S(1)} %get-tuple-element.54), channel_id=1, source_target_pairs={{0,4},{1,5},{2,6},{3,7},{4,0},{5,1},{6,2},{7,3},{8,12},{9,13},{10,... | collective-permute-start | bytes 294920 | tf_op jit(solution)/shard_map/ppermute | solution.py:678

commit v11 on v10

--- a/solution.py
+++ b/solution.py
@@ -330,7 +330,7 @@
 
 KAP, PRS, WET = (0, 1, 2)
 GROUP = 8
-PACK = 8
+PACK = 16
 PIECE = 3
 
 

time: 20.3 us -> 20.3 us (level)
  no operation moved by 1% of the time
where the time goes in v11:
time: 20.3 us; the launch traced here: 20.2 us
  Pallas kernels  11.6 us (57%)
  starting transfers between devices  5.66 us (28%)
  waiting for transfers between devices  2.14 us (11%)
  between operations  0.71 us (3%)
    pallas_call x9, Pallas kernels, call(): pl.pallas_call(kernel, out_shape=[jax.ShapeDtypeStruct(s, jnp.float32) if...  11.6 us
    ppermute x7, starting transfers between devices, swap(): return lax.ppermute(x, ('row', 'col'), pairs)  5.66 us
    ppermute x7, waiting for transfers between devices, swap(): return lax.ppermute(x, ('row', 'col'), pairs)  2.14 us
  transfers between devices with their start and end apart: 7, of which 3 were waited for; matrix products, arithmetic and copies ran while one was open for 0% of the time, Pallas kernels for 39%

profile of v11, /device:TPU:3, one launch (start us, length us, event | category | flops | bytes accessed | tf_op | source)
XLA Modules:
  0.0 20.2 jit_solution(261102263923373967)
XLA Ops:
  0.6 1.4 %shard_map.85 = (f32[4,8,8,128]{3,2,1,0:T(8,128)S(1)}, f32[30,8,128]{2,1,0:T(8,128)S(1)}, f32[4,8,128]{2,1,0:T(8,128)S(1)}, f32[16,8,16,128]{3,2,1,0:T(8,128)S(1)}) custom-call(f32[2,8,8,256]{3,2,1,0:T(8,128)} %flow_in.1, f32[8,8,256]{2,1,0:T(8,128)} %temp_in.1, s32[8,256]{1,0:T(8,128)} %bottom_in.1, f32[8,256]{1,0:T(8,128)} %sunlight_in.1, ...), custom_call_target="tpu_custom_call" | custom-call | flops 1000000000 | bytes 4194304 | tf_op jit(solution)/shard_map/pallas_call | solution.py:636
  2.1 0.7 %collective-permute-start = (f32[30,8,128]{2,1,0:T(8,128)S(1)}, f32[30,8,128]{2,1,0:T(8,128)S(1)}, u32[]{:S(2)}, u32[]{:S(2)}) collective-permute-start(f32[30,8,128]{2,1,0:T(8,128)S(1)} %get-tuple-element.36.to_partner), channel_id=1, source_target_pairs={{0,4},{1,5},{2,6},{3,7},{4,0},{5,1},{6,2},{7,3},{8,12},{9,13},{10,... | collective-permute-start | bytes 368648 | tf_op jit(solution)/shard_map/ppermute | solution.py:678
  2.8 0.6 %shard_map.86 = (f32[16,16,8,128]{3,2,1,0:T(8,128)S(1)}, f32[16,8,128]{2,1,0:T(8,128)S(1)}) custom-call(f32[16,8,16,128]{3,2,1,0:T(8,128)S(1)} %get-tuple-element.33.tracers), custom_call_target="tpu_custom_call" | custom-call | flops 1000000000 | bytes 4194304 | tf_op jit(solution)/shard_map/pallas_call | solution.py:636
  3.4 0.1 collective-permute-start.1
  3.5 0.3 %collective-permute-done.got = f32[30,8,128]{2,1,0:T(8,128)S(1)} collective-permute-done((f32[30,8,128]{2,1,0:T(8,128)S(1)}, f32[30,8,128]{2,1,0:T(8,128)S(1)}, u32[]{:S(2)}, u32[]{:S(2)}) %collective-permute-start) | collective-permute-done | bytes 122912 | tf_op jit(solution)/shard_map/ppermute | solution.py:678
  3.8 0.0 copy-start
  3.8 0.3 %shard_map.87 = (f32[4,16,8,128]{3,2,1,0:T(8,128)S(1)}, f32[20,8,128]{2,1,0:T(8,128)S(1)}, f32[5,8,128]{2,1,0:T(8,128)S(1)}, f32[40,8,128]{2,1,0:T(8,128)S(1)}) custom-call(f32[4,8,8,128]{3,2,1,0:T(8,128)S(1)} %get-tuple-element.35.mine, f32[30,8,128]{2,1,0:T(8,128)S(1)} %collective-permute-done.got, f32[30,8,128]{2,1,0:T(8,128)S(1)} %get-tuple-element.36.to_partner, ...), custom_call_target="tpu_custom_call" | custom-call | flops 1000000000 | bytes 4194304 | tf_op jit(solution)/shard_map/pallas_call | solution.py:636
  4.1 1.6 %collective-permute-start.2 = (f32[5,8,128]{2,1,0:T(8,128)S(1)}, f32[5,8,128]{2,1,0:T(8,128)S(1)}, u32[]{:S(2)}, u32[]{:S(2)}) collective-permute-start(f32[5,8,128]{2,1,0:T(8,128)S(1)} %get-tuple-element.47), channel_id=1, source_target_pairs={{0,8},{1,4},{2,5},{3,6},{4,1},{5,2},{6,3},{7,15},{8,0},{9,12},{10,... | collective-permute-start | bytes 61448 | tf_op jit(solution)/shard_map/ppermute | solution.py:678
  5.7 0.3 %collective-permute-start.3 = (f32[40,8,128]{2,1,0:T(8,128)S(1)}, f32[40,8,128]{2,1,0:T(8,128)S(1)}, u32[]{:S(2)}, u32[]{:S(2)}) collective-permute-start(f32[40,8,128]{2,1,0:T(8,128)S(1)} %get-tuple-element.49), channel_id=1, source_target_pairs={{0,8},{1,9},{2,10},{3,11},{4,12},{5,13},{6,14},{7,15},{8,0},{9,1},... | collective-permute-start | bytes 491528 | tf_op jit(solution)/shard_map/ppermute | solution.py:678
  6.0 0.0 collective-permute-done.1.g_partner
  6.0 0.0 copy-done
  6.0 0.7 %shard_map.88 = (f32[20,20,8,128]{3,2,1,0:T(8,128)S(1)}, f32[3,20,8,128]{3,2,1,0:T(8,128)S(1)}, bf16[256,256]{1,0:T(8,128)(2,1)S(1)}, f32[20,8,128]{2,1,0:T(8,12...) custom-call(f32[16,16,8,128]{3,2,1,0:T(8,128)S(1)} %get-tuple-element.34.turned, ...), custom_call_target="tpu_custom_call" | custom-call | flops 1000000000 | bytes 4194304 | tf_op jit(solution)/shard_map/pallas_call | solution.py:636
  6.7 0.7 %collective-permute-done.2.from_outer = f32[5,8,128]{2,1,0:T(8,128)S(1)} collective-permute-done((f32[5,8,128]{2,1,0:T(8,128)S(1)}, f32[5,8,128]{2,1,0:T(8,128)S(1)}, u32[]{:S(2)}, u32[]{:S(2)}) %collective-permute-start.2) | collective-permute-done | bytes 20512 | tf_op jit(solution)/shard_map/ppermute | solution.py:678
  7.4 0.2 shard_map.89
  7.5 0.7 %collective-permute-start.5 = (f32[8,128]{1,0:T(8,128)S(1)}, f32[8,128]{1,0:T(8,128)S(1)}, u32[]{:S(2)}, u32[]{:S(2)}) collective-permute-start(f32[8,128]{1,0:T(8,128)S(1)} %get-tuple-element.51), channel_id=1, source_target_pairs={{0,8},{1,9},{2,10},{3,11},{4,12},{5,13},{6,14},{7,15},{8,0},{9,1},... | collective-permute-start | bytes 12296 | tf_op jit(solution)/shard_map/ppermute | solution.py:678
  8.2 1.8 %collective-permute-start.4 = (f32[41,8,128]{2,1,0:T(8,128)S(1)}, f32[41,8,128]{2,1,0:T(8,128)S(1)}, u32[]{:S(2)}, u32[]{:S(2)}) collective-permute-start(f32[41,8,128]{2,1,0:T(8,128)S(1)} %get-tuple-element.50), channel_id=1, source_target_pairs={{0,4},{1,5},{2,6},{3,7},{4,0},{5,1},{6,2},{7,3},{8,16},{9,17},{10,... | collective-permute-start | bytes 503816 | tf_op jit(solution)/shard_map/ppermute | solution.py:678
  10.0 5.0 %shard_map.90 = (f32[20,20,8,128]{3,2,1,0:T(8,128)S(1)}, f32[20,20,8,128]{3,2,1,0:T(8,128)S(1)}) custom-call(f32[20,20,8,128]{3,2,1,0:T(8,128)S(1)} %get-tuple-element.41.m0.m_own, f32[3,20,8,128]{3,2,1,0:T(8,128)S(1)} %get-tuple-element.42.dv.dv_own, bf16[256,256]{1,0:T(8,128)(2,1)S(1)} %get-tuple-element.43.mix, f32[20,8,128]{2,1,0:T(8,128)S(1)} %get-tuple-element.44.g0, ...), custom_call_target="tpu_custom_call" | custom-call | flops 20000000000 | bytes 83886080 | tf_op jit(solution)/shard_map/pallas_call | solution.py:636
  15.1 0.0 collective-permute-done.5.edge_a
  15.1 0.0 collective-permute-done.3.rows_a
  15.1 1.2 %collective-permute-done.4.rows_b = f32[41,8,128]{2,1,0:T(8,128)S(1)} collective-permute-done((f32[41,8,128]{2,1,0:T(8,128)S(1)}, f32[41,8,128]{2,1,0:T(8,128)S(1)}, u32[]{:S(2)}, u32[]{:S(2)}) %collective-permute-start.4) | collective-permute-done | bytes 167968 | tf_op jit(solution)/shard_map/ppermute | solution.py:678
  16.3 1.6 %shard_map.91 = (f32[16,8,16,128]{3,2,1,0:T(8,128)}, f32[16,4,8,128]{3,2,1,0:T(8,128)S(1)}, f32[3,8,8,128]{3,2,1,0:T(8,128)S(1)}, f32[3,8,8,128]{3,2,1,0:T(8,128)S(1)}) custom-call(f32[20,20,8,128]{3,2,1,0:T(8,128)S(1)} %get-tuple-element.41.m0.m_own, f32[3,20,8,128]{3,2,1,0:T(8,128)S(1)} %get-tuple-element.42.dv.dv_own, ...), custom_call_target="tpu_custom_call" | custom-call | flops 1000000000 | bytes 4194304 | tf_op jit(solution)/shard_map/pallas_call | solution.py:636
  17.9 0.5 %collective-permute-start.6 = (f32[3,8,8,128]{3,2,1,0:T(8,128)S(1)}, f32[3,8,8,128]{3,2,1,0:T(8,128)S(1)}, u32[]{:S(2)}, u32[]{:S(2)}) collective-permute-start(f32[3,8,8,128]{3,2,1,0:T(8,128)S(1)} %get-tuple-element.54), channel_id=1, source_target_pairs={{0,4},{1,5},{2,6},{3,7},{4,0},{5,1},{6,2},{7,3},{8,12},{9,13},{10,... | collective-permute-start | bytes 294920 | tf_op jit(solution)/shard_map/ppermute | solution.py:678
  18.5 1.0 %shard_map.92 = (f32[2,8,8,256]{3,2,1,0:T(8,128)}, f32[8,8,256]{2,1,0:T(8,128)}, f32[16,8,16,128]{3,2,1,0:T(8,128)}) custom-call(f32[3,8,8,128]{3,2,1,0:T(8,128)S(1)} %get-tuple-element.55.keep, f32[16,4,8,128]{3,2,1,0:T(8,128)S(1)} %get-tuple-element.56.rim, f32[20,20,8,128]{3,2,1,0:T(8,128)S(1)} %get-tuple-element.53.m2_in.m, ...), custom_call_target="tpu_custom_call", output_to_operand_aliasing={{2}: (3, {})} | custom-call | flops 1000000000 | bytes 4194304 | tf_op jit(solution)/shard_map/pallas_call | solution.py:636
  19.4 0.0 collective-permute-done.6.got
  19.4 0.7 %shard_map.93 = (f32[2,8,8,256]{3,2,1,0:T(8,128)}, f32[8,8,256]{2,1,0:T(8,128)}) custom-call(f32[3,8,8,128]{3,2,1,0:T(8,128)S(1)} %collective-permute-done.6.got, f32[2,8,8,256]{3,2,1,0:T(8,128)} %get-tuple-element.58.flow_in, f32[8,8,256]{2,1,0:T(8,128)} %get-tuple-element.59.temp_in), custom_call_target="tpu_custom_call", output_to_operand_aliasing={{0}: (1, {}), {1}: (2, {})} | custom-call | flops 1000000000 | bytes 4194304 | tf_op jit(solution)/shard_map/pallas_call | solution.py:636
Async XLA Ops:
  2.1 1.7 %collective-permute-start = (f32[30,8,128]{2,1,0:T(8,128)S(1)}, f32[30,8,128]{2,1,0:T(8,128)S(1)}, u32[]{:S(2)}, u32[]{:S(2)}) collective-permute-start(f32[30,8,128]{2,1,0:T(8,128)S(1)} %get-tuple-element.36.to_partner), channel_id=1, source_target_pairs={{0,4},{1,5},{2,6},{3,7},{4,0},{5,1},{6,2},{7,3},{8,12},{9,13},{10,... | collective-permute-start | bytes 368648 | tf_op jit(solution)/shard_map/ppermute | solution.py:678
  3.4 2.5 %collective-permute-start.1 = (f32[16,8,128]{2,1,0:T(8,128)S(1)}, f32[16,8,128]{2,1,0:T(8,128)S(1)}, u32[]{:S(2)}, u32[]{:S(2)}) collective-permute-start(f32[16,8,128]{2,1,0:T(8,128)S(1)} %get-tuple-element.37.g_tracers), channel_id=1, source_target_pairs={{0,4},{1,5},{2,6},{3,7},{4,0},{5,1},{6,2},{7,3},{8,12},{9,13},{10,... | collective-permute-start | bytes 196616 | tf_op jit(solution)/shard_map/ppermute | solution.py:678
  3.8 2.2 %copy-start = (f32[16,16]{1,0:T(8,128)S(1)}, f32[16,16]{1,0:T(8,128)}, u32[]{:S(2)}) copy-start(f32[16,16]{1,0:T(8,128)} %rates.1) | copy-start | bytes 3076
  4.1 3.3 %collective-permute-start.2 = (f32[5,8,128]{2,1,0:T(8,128)S(1)}, f32[5,8,128]{2,1,0:T(8,128)S(1)}, u32[]{:S(2)}, u32[]{:S(2)}) collective-permute-start(f32[5,8,128]{2,1,0:T(8,128)S(1)} %get-tuple-element.47), channel_id=1, source_target_pairs={{0,8},{1,4},{2,5},{3,6},{4,1},{5,2},{6,3},{7,15},{8,0},{9,12},{10,... | collective-permute-start | bytes 61448 | tf_op jit(solution)/shard_map/ppermute | solution.py:678
  5.7 9.4 %collective-permute-start.3 = (f32[40,8,128]{2,1,0:T(8,128)S(1)}, f32[40,8,128]{2,1,0:T(8,128)S(1)}, u32[]{:S(2)}, u32[]{:S(2)}) collective-permute-start(f32[40,8,128]{2,1,0:T(8,128)S(1)} %get-tuple-element.49), channel_id=1, source_target_pairs={{0,8},{1,9},{2,10},{3,11},{4,12},{5,13},{6,14},{7,15},{8,0},{9,1},... | collective-permute-start | bytes 491528 | tf_op jit(solution)/shard_map/ppermute | solution.py:678
  7.5 7.5 %collective-permute-start.5 = (f32[8,128]{1,0:T(8,128)S(1)}, f32[8,128]{1,0:T(8,128)S(1)}, u32[]{:S(2)}, u32[]{:S(2)}) collective-permute-start(f32[8,128]{1,0:T(8,128)S(1)} %get-tuple-element.51), channel_id=1, source_target_pairs={{0,8},{1,9},{2,10},{3,11},{4,12},{5,13},{6,14},{7,15},{8,0},{9,1},... | collective-permute-start | bytes 12296 | tf_op jit(solution)/shard_map/ppermute | solution.py:678
  8.2 8.1 %collective-permute-start.4 = (f32[41,8,128]{2,1,0:T(8,128)S(1)}, f32[41,8,128]{2,1,0:T(8,128)S(1)}, u32[]{:S(2)}, u32[]{:S(2)}) collective-permute-start(f32[41,8,128]{2,1,0:T(8,128)S(1)} %get-tuple-element.50), channel_id=1, source_target_pairs={{0,4},{1,5},{2,6},{3,7},{4,0},{5,1},{6,2},{7,3},{8,16},{9,17},{10,... | collective-permute-start | bytes 503816 | tf_op jit(solution)/shard_map/ppermute | solution.py:678
  17.9 1.5 %collective-permute-start.6 = (f32[3,8,8,128]{3,2,1,0:T(8,128)S(1)}, f32[3,8,8,128]{3,2,1,0:T(8,128)S(1)}, u32[]{:S(2)}, u32[]{:S(2)}) collective-permute-start(f32[3,8,8,128]{3,2,1,0:T(8,128)S(1)} %get-tuple-element.54), channel_id=1, source_target_pairs={{0,4},{1,5},{2,6},{3,7},{4,0},{5,1},{6,2},{7,3},{8,12},{9,13},{10,... | collective-permute-start | bytes 294920 | tf_op jit(solution)/shard_map/ppermute | solution.py:678

commit v12 on v11

--- a/solution.py
+++ b/solution.py
@@ -331,7 +331,7 @@
 KAP, PRS, WET = (0, 1, 2)
 GROUP = 8
 PACK = 16
-PIECE = 3
+PIECE = 2
 
 
 def span(start, stop):

time: 20.3 us -> 20.3 us (level)
  no operation moved by 1% of the time
where the time goes in v12:
time: 20.3 us; the launch traced here: 20.2 us
  Pallas kernels  11.7 us (58%)
  starting transfers between devices  5.66 us (28%)
  waiting for transfers between devices  2.08 us (10%)
  between operations  0.71 us (3%)
    pallas_call x9, Pallas kernels, call(): pl.pallas_call(kernel, out_shape=[jax.ShapeDtypeStruct(s, jnp.float32) if...  11.7 us
    ppermute x7, starting transfers between devices, swap(): return lax.ppermute(x, ('row', 'col'), pairs)  5.66 us
    ppermute x7, waiting for transfers between devices, swap(): return lax.ppermute(x, ('row', 'col'), pairs)  2.08 us
  transfers between devices with their start and end apart: 7, of which 3 were waited for; matrix products, arithmetic and copies ran while one was open for 0% of the time, Pallas kernels for 39%

profile of v12, /device:TPU:3, one launch (start us, length us, event | category | flops | bytes accessed | tf_op | source)
XLA Modules:
  0.0 20.2 jit_solution(8696711864237189726)
XLA Ops:
  0.6 1.4 %shard_map.85 = (f32[4,8,8,128]{3,2,1,0:T(8,128)S(1)}, f32[30,8,128]{2,1,0:T(8,128)S(1)}, f32[4,8,128]{2,1,0:T(8,128)S(1)}, f32[16,8,16,128]{3,2,1,0:T(8,128)S(1)}) custom-call(f32[2,8,8,256]{3,2,1,0:T(8,128)} %flow_in.1, f32[8,8,256]{2,1,0:T(8,128)} %temp_in.1, s32[8,256]{1,0:T(8,128)} %bottom_in.1, f32[8,256]{1,0:T(8,128)} %sunlight_in.1, ...), custom_call_target="tpu_custom_call" | custom-call | flops 1000000000 | bytes 4194304 | tf_op jit(solution)/shard_map/pallas_call | solution.py:636
  2.1 0.7 %collective-permute-start = (f32[30,8,128]{2,1,0:T(8,128)S(1)}, f32[30,8,128]{2,1,0:T(8,128)S(1)}, u32[]{:S(2)}, u32[]{:S(2)}) collective-permute-start(f32[30,8,128]{2,1,0:T(8,128)S(1)} %get-tuple-element.36.to_partner), channel_id=1, source_target_pairs={{0,4},{1,5},{2,6},{3,7},{4,0},{5,1},{6,2},{7,3},{8,12},{9,13},{10,... | collective-permute-start | bytes 368648 | tf_op jit(solution)/shard_map/ppermute | solution.py:678
  2.8 0.6 %shard_map.86 = (f32[16,16,8,128]{3,2,1,0:T(8,128)S(1)}, f32[16,8,128]{2,1,0:T(8,128)S(1)}) custom-call(f32[16,8,16,128]{3,2,1,0:T(8,128)S(1)} %get-tuple-element.33.tracers), custom_call_target="tpu_custom_call" | custom-call | flops 1000000000 | bytes 4194304 | tf_op jit(solution)/shard_map/pallas_call | solution.py:636
  3.4 0.1 collective-permute-start.1
  3.5 0.3 %collective-permute-done.got = f32[30,8,128]{2,1,0:T(8,128)S(1)} collective-permute-done((f32[30,8,128]{2,1,0:T(8,128)S(1)}, f32[30,8,128]{2,1,0:T(8,128)S(1)}, u32[]{:S(2)}, u32[]{:S(2)}) %collective-permute-start) | collective-permute-done | bytes 122912 | tf_op jit(solution)/shard_map/ppermute | solution.py:678
  3.8 0.0 copy-start
  3.8 0.3 %shard_map.87 = (f32[4,16,8,128]{3,2,1,0:T(8,128)S(1)}, f32[20,8,128]{2,1,0:T(8,128)S(1)}, f32[5,8,128]{2,1,0:T(8,128)S(1)}, f32[40,8,128]{2,1,0:T(8,128)S(1)}) custom-call(f32[4,8,8,128]{3,2,1,0:T(8,128)S(1)} %get-tuple-element.35.mine, f32[30,8,128]{2,1,0:T(8,128)S(1)} %collective-permute-done.got, f32[30,8,128]{2,1,0:T(8,128)S(1)} %get-tuple-element.36.to_partner, ...), custom_call_target="tpu_custom_call" | custom-call | flops 1000000000 | bytes 4194304 | tf_op jit(solution)/shard_map/pallas_call | solution.py:636
  4.1 1.6 %collective-permute-start.2 = (f32[5,8,128]{2,1,0:T(8,128)S(1)}, f32[5,8,128]{2,1,0:T(8,128)S(1)}, u32[]{:S(2)}, u32[]{:S(2)}) collective-permute-start(f32[5,8,128]{2,1,0:T(8,128)S(1)} %get-tuple-element.47), channel_id=1, source_target_pairs={{0,8},{1,4},{2,5},{3,6},{4,1},{5,2},{6,3},{7,15},{8,0},{9,12},{10,... | collective-permute-start | bytes 61448 | tf_op jit(solution)/shard_map/ppermute | solution.py:678
  5.7 0.3 %collective-permute-start.3 = (f32[40,8,128]{2,1,0:T(8,128)S(1)}, f32[40,8,128]{2,1,0:T(8,128)S(1)}, u32[]{:S(2)}, u32[]{:S(2)}) collective-permute-start(f32[40,8,128]{2,1,0:T(8,128)S(1)} %get-tuple-element.49), channel_id=1, source_target_pairs={{0,8},{1,9},{2,10},{3,11},{4,12},{5,13},{6,14},{7,15},{8,0},{9,1},... | collective-permute-start | bytes 491528 | tf_op jit(solution)/shard_map/ppermute | solution.py:678
  6.0 0.0 collective-permute-done.1.g_partner
  6.0 0.0 copy-done
  6.0 0.7 %shard_map.88 = (f32[20,20,8,128]{3,2,1,0:T(8,128)S(1)}, f32[3,20,8,128]{3,2,1,0:T(8,128)S(1)}, bf16[256,256]{1,0:T(8,128)(2,1)S(1)}, f32[20,8,128]{2,1,0:T(8,12...) custom-call(f32[16,16,8,128]{3,2,1,0:T(8,128)S(1)} %get-tuple-element.34.turned, ...), custom_call_target="tpu_custom_call" | custom-call | flops 1000000000 | bytes 4194304 | tf_op jit(solution)/shard_map/pallas_call | solution.py:636
  6.7 0.7 %collective-permute-done.2.from_outer = f32[5,8,128]{2,1,0:T(8,128)S(1)} collective-permute-done((f32[5,8,128]{2,1,0:T(8,128)S(1)}, f32[5,8,128]{2,1,0:T(8,128)S(1)}, u32[]{:S(2)}, u32[]{:S(2)}) %collective-permute-start.2) | collective-permute-done | bytes 20512 | tf_op jit(solution)/shard_map/ppermute | solution.py:678
  7.4 0.2 shard_map.89
  7.5 0.7 %collective-permute-start.5 = (f32[8,128]{1,0:T(8,128)S(1)}, f32[8,128]{1,0:T(8,128)S(1)}, u32[]{:S(2)}, u32[]{:S(2)}) collective-permute-start(f32[8,128]{1,0:T(8,128)S(1)} %get-tuple-element.51), channel_id=1, source_target_pairs={{0,8},{1,9},{2,10},{3,11},{4,12},{5,13},{6,14},{7,15},{8,0},{9,1},... | collective-permute-start | bytes 12296 | tf_op jit(solution)/shard_map/ppermute | solution.py:678
  8.2 1.8 %collective-permute-start.4 = (f32[41,8,128]{2,1,0:T(8,128)S(1)}, f32[41,8,128]{2,1,0:T(8,128)S(1)}, u32[]{:S(2)}, u32[]{:S(2)}) collective-permute-start(f32[41,8,128]{2,1,0:T(8,128)S(1)} %get-tuple-element.50), channel_id=1, source_target_pairs={{0,4},{1,5},{2,6},{3,7},{4,0},{5,1},{6,2},{7,3},{8,16},{9,17},{10,... | collective-permute-start | bytes 503816 | tf_op jit(solution)/shard_map/ppermute | solution.py:678
  10.0 5.1 %shard_map.90 = (f32[20,20,8,128]{3,2,1,0:T(8,128)S(1)}, f32[20,20,8,128]{3,2,1,0:T(8,128)S(1)}) custom-call(f32[20,20,8,128]{3,2,1,0:T(8,128)S(1)} %get-tuple-element.41.m0.m_own, f32[3,20,8,128]{3,2,1,0:T(8,128)S(1)} %get-tuple-element.42.dv.dv_own, bf16[256,256]{1,0:T(8,128)(2,1)S(1)} %get-tuple-element.43.mix, f32[20,8,128]{2,1,0:T(8,128)S(1)} %get-tuple-element.44.g0, ...), custom_call_target="tpu_custom_call" | custom-call | flops 20000000000 | bytes 83886080 | tf_op jit(solution)/shard_map/pallas_call | solution.py:636
  15.1 0.0 collective-permute-done.5.edge_a
  15.2 0.0 collective-permute-done.3.rows_a
  15.2 1.2 %collective-permute-done.4.rows_b = f32[41,8,128]{2,1,0:T(8,128)S(1)} collective-permute-done((f32[41,8,128]{2,1,0:T(8,128)S(1)}, f32[41,8,128]{2,1,0:T(8,128)S(1)}, u32[]{:S(2)}, u32[]{:S(2)}) %collective-permute-start.4) | collective-permute-done | bytes 167968 | tf_op jit(solution)/shard_map/ppermute | solution.py:678
  16.3 1.6 %shard_map.91 = (f32[16,8,16,128]{3,2,1,0:T(8,128)}, f32[16,4,8,128]{3,2,1,0:T(8,128)S(1)}, f32[3,8,8,128]{3,2,1,0:T(8,128)S(1)}, f32[3,8,8,128]{3,2,1,0:T(8,128)S(1)}) custom-call(f32[20,20,8,128]{3,2,1,0:T(8,128)S(1)} %get-tuple-element.41.m0.m_own, f32[3,20,8,128]{3,2,1,0:T(8,128)S(1)} %get-tuple-element.42.dv.dv_own, ...), custom_call_target="tpu_custom_call" | custom-call | flops 1000000000 | bytes 4194304 | tf_op jit(solution)/shard_map/pallas_call | solution.py:636
  17.9 0.5 %collective-permute-start.6 = (f32[3,8,8,128]{3,2,1,0:T(8,128)S(1)}, f32[3,8,8,128]{3,2,1,0:T(8,128)S(1)}, u32[]{:S(2)}, u32[]{:S(2)}) collective-permute-start(f32[3,8,8,128]{3,2,1,0:T(8,128)S(1)} %get-tuple-element.54), channel_id=1, source_target_pairs={{0,4},{1,5},{2,6},{3,7},{4,0},{5,1},{6,2},{7,3},{8,12},{9,13},{10,... | collective-permute-start | bytes 294920 | tf_op jit(solution)/shard_map/ppermute | solution.py:678
  18.5 1.0 %shard_map.92 = (f32[2,8,8,256]{3,2,1,0:T(8,128)}, f32[8,8,256]{2,1,0:T(8,128)}, f32[16,8,16,128]{3,2,1,0:T(8,128)}) custom-call(f32[3,8,8,128]{3,2,1,0:T(8,128)S(1)} %get-tuple-element.55.keep, f32[16,4,8,128]{3,2,1,0:T(8,128)S(1)} %get-tuple-element.56.rim, f32[20,20,8,128]{3,2,1,0:T(8,128)S(1)} %get-tuple-element.53.m2_in.m, ...), custom_call_target="tpu_custom_call", output_to_operand_aliasing={{2}: (3, {})} | custom-call | flops 1000000000 | bytes 4194304 | tf_op jit(solution)/shard_map/pallas_call | solution.py:636
  19.4 0.0 collective-permute-done.6.got
  19.4 0.7 %shard_map.93 = (f32[2,8,8,256]{3,2,1,0:T(8,128)}, f32[8,8,256]{2,1,0:T(8,128)}) custom-call(f32[3,8,8,128]{3,2,1,0:T(8,128)S(1)} %collective-permute-done.6.got, f32[2,8,8,256]{3,2,1,0:T(8,128)} %get-tuple-element.58.flow_in, f32[8,8,256]{2,1,0:T(8,128)} %get-tuple-element.59.temp_in), custom_call_target="tpu_custom_call", output_to_operand_aliasing={{0}: (1, {}), {1}: (2, {})} | custom-call | flops 1000000000 | bytes 4194304 | tf_op jit(solution)/shard_map/pallas_call | solution.py:636
Async XLA Ops:
  2.1 1.7 %collective-permute-start = (f32[30,8,128]{2,1,0:T(8,128)S(1)}, f32[30,8,128]{2,1,0:T(8,128)S(1)}, u32[]{:S(2)}, u32[]{:S(2)}) collective-permute-start(f32[30,8,128]{2,1,0:T(8,128)S(1)} %get-tuple-element.36.to_partner), channel_id=1, source_target_pairs={{0,4},{1,5},{2,6},{3,7},{4,0},{5,1},{6,2},{7,3},{8,12},{9,13},{10,... | collective-permute-start | bytes 368648 | tf_op jit(solution)/shard_map/ppermute | solution.py:678
  3.4 2.5 %collective-permute-start.1 = (f32[16,8,128]{2,1,0:T(8,128)S(1)}, f32[16,8,128]{2,1,0:T(8,128)S(1)}, u32[]{:S(2)}, u32[]{:S(2)}) collective-permute-start(f32[16,8,128]{2,1,0:T(8,128)S(1)} %get-tuple-element.37.g_tracers), channel_id=1, source_target_pairs={{0,4},{1,5},{2,6},{3,7},{4,0},{5,1},{6,2},{7,3},{8,12},{9,13},{10,... | collective-permute-start | bytes 196616 | tf_op jit(solution)/shard_map/ppermute | solution.py:678
  3.8 2.2 %copy-start = (f32[16,16]{1,0:T(8,128)S(1)}, f32[16,16]{1,0:T(8,128)}, u32[]{:S(2)}) copy-start(f32[16,16]{1,0:T(8,128)} %rates.1) | copy-start | bytes 3076
  4.1 3.3 %collective-permute-start.2 = (f32[5,8,128]{2,1,0:T(8,128)S(1)}, f32[5,8,128]{2,1,0:T(8,128)S(1)}, u32[]{:S(2)}, u32[]{:S(2)}) collective-permute-start(f32[5,8,128]{2,1,0:T(8,128)S(1)} %get-tuple-element.47), channel_id=1, source_target_pairs={{0,8},{1,4},{2,5},{3,6},{4,1},{5,2},{6,3},{7,15},{8,0},{9,12},{10,... | collective-permute-start | bytes 61448 | tf_op jit(solution)/shard_map/ppermute | solution.py:678
  5.7 9.5 %collective-permute-start.3 = (f32[40,8,128]{2,1,0:T(8,128)S(1)}, f32[40,8,128]{2,1,0:T(8,128)S(1)}, u32[]{:S(2)}, u32[]{:S(2)}) collective-permute-start(f32[40,8,128]{2,1,0:T(8,128)S(1)} %get-tuple-element.49), channel_id=1, source_target_pairs={{0,8},{1,9},{2,10},{3,11},{4,12},{5,13},{6,14},{7,15},{8,0},{9,1},... | collective-permute-start | bytes 491528 | tf_op jit(solution)/shard_map/ppermute | solution.py:678
  7.5 7.6 %collective-permute-start.5 = (f32[8,128]{1,0:T(8,128)S(1)}, f32[8,128]{1,0:T(8,128)S(1)}, u32[]{:S(2)}, u32[]{:S(2)}) collective-permute-start(f32[8,128]{1,0:T(8,128)S(1)} %get-tuple-element.51), channel_id=1, source_target_pairs={{0,8},{1,9},{2,10},{3,11},{4,12},{5,13},{6,14},{7,15},{8,0},{9,1},... | collective-permute-start | bytes 12296 | tf_op jit(solution)/shard_map/ppermute | solution.py:678
  8.2 8.1 %collective-permute-start.4 = (f32[41,8,128]{2,1,0:T(8,128)S(1)}, f32[41,8,128]{2,1,0:T(8,128)S(1)}, u32[]{:S(2)}, u32[]{:S(2)}) collective-permute-start(f32[41,8,128]{2,1,0:T(8,128)S(1)} %get-tuple-element.50), channel_id=1, source_target_pairs={{0,4},{1,5},{2,6},{3,7},{4,0},{5,1},{6,2},{7,3},{8,16},{9,17},{10,... | collective-permute-start | bytes 503816 | tf_op jit(solution)/shard_map/ppermute | solution.py:678
  17.9 1.5 %collective-permute-start.6 = (f32[3,8,8,128]{3,2,1,0:T(8,128)S(1)}, f32[3,8,8,128]{3,2,1,0:T(8,128)S(1)}, u32[]{:S(2)}, u32[]{:S(2)}) collective-permute-start(f32[3,8,8,128]{3,2,1,0:T(8,128)S(1)} %get-tuple-element.54), channel_id=1, source_target_pairs={{0,4},{1,5},{2,6},{3,7},{4,0},{5,1},{6,2},{7,3},{8,12},{9,13},{10,... | collective-permute-start | bytes 294920 | tf_op jit(solution)/shard_map/ppermute | solution.py:678
